TPU v7x, 256 devices: a whole 4x4x8 slice. The times are simulated.
256 devices in a mesh: tm: 32 (over z_hi, x, core), chan: 4 (over y), bank: 2 (over z_lo).
Axes of the slice: x: 4, y: 4, z: 8 (z_hi: 4, z_lo: 2; z = z_hi * 2 + z_lo), core: 2. Of those that a mesh axis runs over, the one named last changes fastest.
Arguments:
- record: bfloat16 [512, 131072], P('chan', ('tm', 'bank')), as said below
- templates: bfloat16 [2048, 512, 256], P(('tm', 'bank'), 'chan'), as said below
- block_ids: int32 [2], replicated, may hold values from 0 to 63
- sensor_group: int32 [512], P('chan'), may hold values from 0 to 3
Outputs:
- traces: float32 [2, 32, 131072], P(None, 'chan', ('tm', 'bank'))
Inputs may be any that keep to these rules, and one draw needn't show every extreme that they name: `record`: real-valued samples of order one to a few tens, scales differing from sensor to sensor. `templates`: real-valued template samples.
All inputs are finite; a program needn't handle non-finite values.
Results may differ from a plain program's by a relative error of at most 0.0003.
Values may be sent and summed in bfloat16 or wider, within the bound.
No kernel may reach another device: no remote copies, remote signals or barrier semaphores. Data moves between devices by JAX's collectives and lax.ppermute only.
A program may use at most 64 MiB of HBM per device.

v0:
```python
import math

import jax
import jax.numpy as jnp
from jax import lax
from jax.sharding import PartitionSpec as P

SENSORS = 512
K = 32
GROUPS = 4
DSTEP = 64
BLOCKS_DEV = 1
HALO = 512


def shifted(value, axis, steps):
    count = lax.axis_size(axis)
    initial, last = (max(0, -steps), min(count, count - steps))
    return lax.ppermute(value, axis, [(source, source + steps) for source in range(initial, last)])


def broadcast(block, axis, owner):
    block = jnp.where(lax.axis_index(axis) == owner, block, jnp.zeros_like(block))
    return lax.psum(block, axis)


def correlate(template_block, delayed, samples_dev):
    tap_count = template_block.shape[2]
    window = delayed[:, : samples_dev + tap_count - 1]
    result = lax.conv_general_dilated(
        window[None],
        template_block,
        (1,),
        "VALID",
        dimension_numbers=("NCH", "OIH", "NCH"),
        preferred_element_type=jnp.float32,
    )
    return result[0]


def local(record, templates, block_ids, sensor_group):
    sensors, samples_dev = record.shape
    tap_count = templates.shape[2]
    leading = record[:, :HALO]
    following = shifted(leading, ("tm", "bank"), -1)
    extended = jnp.concatenate([record, following], 1)
    ext_width = samples_dev + tap_count
    delayed = jnp.zeros((sensors, ext_width), jnp.bfloat16)
    for group_id in range(GROUPS):
        moved = extended[:, DSTEP * group_id : DSTEP * group_id + ext_width]
        delayed = jnp.where((sensor_group == group_id)[:, None], moved, delayed)
    power_sum = jnp.einsum("st,st->t", delayed, delayed, preferred_element_type=jnp.float32)
    running = jnp.concatenate([jnp.zeros((1,), jnp.float32), jnp.cumsum(power_sum)])
    energy = lax.psum(running[tap_count : tap_count + samples_dev] - running[:samples_dev], "chan")
    rounds = block_ids.shape[0]
    block_list = []
    for round_id in range(rounds):
        chosen = block_ids[round_id]
        owner_id = chosen // BLOCKS_DEV
        template_block = broadcast(templates, ("tm", "bank"), owner_id)
        block_list.append(template_block)
    combined = jnp.concatenate(block_list, 0)
    partial_all = correlate(combined, delayed, samples_dev)
    norm_all = jnp.einsum("kst,kst->k", combined, combined, preferred_element_type=jnp.float32)
    partials = []
    norm_list = []
    for round_id in range(rounds):
        partial_value = partial_all[round_id * K : (round_id + 1) * K]
        norm_part = norm_all[round_id * K : (round_id + 1) * K]
        partial_value, norm_part = (
            lax.psum_scatter(partial_value, "chan", scatter_dimension=0, tiled=True),
            lax.psum_scatter(norm_part, "chan", scatter_dimension=0, tiled=True),
        )
        partials.append(partial_value)
        norm_list.append(norm_part)
    traces = jnp.stack(partials)
    tmpl_norm = jnp.stack(norm_list)
    unit_scale = math.sqrt(SENSORS * tap_count)
    return traces * unit_scale * lax.rsqrt(tmpl_norm[:, :, None] * (energy[None, None, :] + 1e-05))


def solution(mesh):
    return jax.shard_map(
        local,
        mesh=mesh,
        in_specs=(P("chan", ("tm", "bank")), P(("tm", "bank"), "chan", None), P(), P("chan")),
        out_specs=P(None, "chan", ("tm", "bank")),
        check_vma=False,
    )
```

profile of v0, /device:TPU:1, one launch (start us, length us, event | category | flops | bytes accessed | tf_op | source)
XLA Modules:
  0.0 704.1 jit_solution(4225436234559200866)
XLA Ops:
  6.5 1.3 fusion.25
  9.2 3.4 copy.19
  12.7 2.2 broadcast_select_fusion
  15.0 1.0 copy-done.2
  16.0 0.3 copy.16
  16.2 4.9 collective-permute-start
  21.2 0.6 dynamic-slice
  22.5 0.7 collective-permute-done
  23.1 0.4 fusion.2
  23.5 0.3 reduce-window.9
  24.0 0.2 copy.18
  24.3 0.1 slice.86
  24.4 0.1 slice_reduce_fusion
  24.6 0.1 fusion.18
  24.7 188.2 %all-reduce.6.cloned.1.call-done = (bf16[32,128,256]{1,0,2:T(8,128)(2,1)}, bf16[32,128,256]{1,0,2:T(8,128)(2,1)}) async-done(((bf16[32,128,256]{1,0,2:T(8,128)(2,1)}, bf16[32,128,256]{1,0,2:T(8,128)(2,1)}), (bf16[32,128,256]{1,0,2:T(8,128)(2,1)}, bf16[32,128,256]{1,0,2:T(8,128)(2,1)})) %all-reduce.6.cloned.1.call-update) | async-done | bytes 4194320 | tf_op jit(solution)/shard_map/psum | solution.py:24
  212.9 2.5 constant_dynamic-update-slice_fusion.1
  215.4 0.5 constant_dynamic-update-slice_fusion
  215.9 0.2 copy-done.4
  216.1 431.1 %convolution_select_fusion = f32[8,288,64]{2,0,1:T(8,128)S(1)} fusion(bf16[64,128,256]{1,0,2:T(8,128)(2,1)S(1)} %constant_dynamic-update-slice_fusion, bf16[128,1,7,255]{0,2,3,1:T(8,128)(2,1)S(1)} %slice.86, bf16[128,1,8,288]{0,2,3,1:T(8,128)(2,1)S(1)} %copy.18, pred[8,288]{0,1:T(8,128)(4,1)S(1)} %bitcast.39), kind=kOutput, calls=%fused_computation.6 | convolution fusion | flops 9667160064 | bytes 5833216 | tf_op jit(solution)/shard_map/conv_general_dilated | solution.py:30
  647.3 0.4 fusion.23
  647.7 0.5 copy.22
  648.2 0.1 reshape.33
  648.4 0.7 slice_bitcast_fusion.1
  649.2 3.3 fusion
  652.5 0.5 copy.21
  653.0 0.1 reshape.31
  653.2 0.7 slice_bitcast_fusion.2
  654.0 8.7 %all-reduce.2 = (f32[2048]{0:T(1024)S(1)}, f32[32]{0:T(128)S(1)}, f32[32]{0:T(128)S(1)}) all-reduce(f32[2048]{0:T(1024)S(1)} %fusion.18, f32[32]{0:T(128)S(1)} %get-tuple-element.17, f32[32]{0:T(128)S(1)} %get-tuple-element.16), channel_id=1, replica_groups=mesh['tm'=32,'chan'=4,'bank'=2] {'chan'}, use_global_device_ids=true, to_apply=%region_8.9 | all-reduce | flops 2112 | bytes 16896 | tf_op jit(solution)/shard_map/psum | solution.py:54
  662.6 0.1 dynamic-slice_bitcast_fusion
  662.7 7.8 %reduce-scatter.5.cloned.1.call-done = f32[8,2048]{1,0:T(8,128)} async-done(((f32[32,2048]{1,0:T(8,128)}), f32[8,2048]{1,0:T(8,128)}) %reduce-scatter.5.cloned.1.call-update) | async-done | bytes 65552 | tf_op jit(solution)/shard_map/reduce_scatter | solution.py:71
  670.5 25.5 %reduce-scatter.3.cloned.1.call-done = f32[8,2048]{1,0:T(8,128)} async-done(((f32[32,2048]{1,0:T(8,128)}), f32[8,2048]{1,0:T(8,128)}) %reduce-scatter.3.cloned.1.call-update) | async-done | bytes 65552 | tf_op jit(solution)/shard_map/reduce_scatter | solution.py:71
  696.0 1.6 fusion.17
  (26 shorter events, 0.5 us)
Async XLA Ops:
  6.5 206.3 %all-reduce.6.cloned.1.call-start = ((), (), s32[]{:S(2)}) async-start(), calls=%async_computation.4 | async-start | bytes 8388608 | tf_op jit(solution)/shard_map/psum | solution.py:24
  14.9 1.0 copy-start.2
  14.9 6.3 copy-start.5
  14.9 7.5 %copy-start.3 = (s32[128]{0:T(128)S(1)}, s32[128]{0:T(128)}, u32[]{:S(2)}) copy-start(s32[128]{0:T(128)} %param.7) | copy-start | bytes 1540
  14.9 655.6 %reduce-scatter.5.cloned.1.call-start = ((), (), s32[]{:S(2)}) async-start(), calls=%async_computation.3 | async-start | bytes 327680 | tf_op jit(solution)/shard_map/reduce_scatter | solution.py:71
  16.2 6.9 collective-permute-start
  212.9 2.5 copy-start.1
  215.4 0.8 copy-start.4
  215.9 431.4 %copy-start = (bf16[64,128,256]{1,0,2:T(8,128)(2,1)}, bf16[64,128,256]{1,0,2:T(8,128)(2,1)S(1)}, u32[]{:S(2)}) copy-start(bf16[64,128,256]{1,0,2:T(8,128)(2,1)S(1)} %constant_dynamic-update-slice_fusion) | copy-start | bytes 12582916
  649.1 46.9 %reduce-scatter.3.cloned.1.call-start = ((), (), s32[]{:S(2)}) async-start(), calls=%async_computation.2 | async-start | bytes 327680 | tf_op jit(solution)/shard_map/reduce_scatter | solution.py:71
Sparse Core Ops, SparseCore 0:
  15.1 197.7 all-reduce.5
  649.2 21.2 reduce-scatter.4
  673.0 22.9 reduce-scatter.2
where the time goes:
time: 706 us; the launch traced here: 704 us
  matrix products  431 us (61%)
  waiting for transfers between devices  222 us (31%)
  between operations  15.3 us (2%)
  local copies, waits for them, and re-layouts  13.8 us (2%)
  blocking collectives  8.66 us (1%)
  other arithmetic  8.08 us (1%)
    conv_general_dilated x1, matrix products, correlate(): lax.conv_general_dilated(window[None], template_block, (1,), 'VALID', dim...  431 us
    psum x1, waiting for transfers between devices, broadcast(): return lax.psum(block, axis)  188 us
    reduce_scatter x2, waiting for transfers between devices, local(): lax.psum_scatter(partial_value, 'chan', scatter_dimension=0, tiled=True)  33.3 us
  transfers between devices with their start and end apart: 4, of which 4 were waited for; matrix products, arithmetic and copies ran while one was open for 1% of the time, Pallas kernels for 0%

commit v1 on v0

v1 whole, which is shorter than its diff:
```python
import math

import jax
import jax.numpy as jnp
from jax import lax
from jax.experimental import pallas as pl
from jax.experimental.pallas import tpu as pltpu
from jax.sharding import Mesh, PartitionSpec as P

SENSORS = 512
TLEN = 256
GROUPS = 4
DSTEP = 64
HALO = 512
TILE = 2048
EXT = TILE + TLEN
FINE = 8
COARSE = TLEN // FINE
NX, NZ, NY = 4, 8, 4
SUB = 16
DEPTH = FINE * NY * SUB
ROWS = 2 * COARSE
HALF = NX * ROWS
TIME_TILE = 768
VMEM_LIMIT = 40 * 1024 * 1024

PLANE = ("zh", "x", "bank")
ZAXES = ("zh", "bank")
BLOCKS = ("zh", "x", "core", "bank")


def shift(value, axis, steps):
    count = lax.axis_size(axis)
    return lax.ppermute(value, axis, [(i, (i + steps) % count) for i in range(count)])


def plane_index(x, z):
    return ((z // 2) * NX + x) * 2 + z % 2


def turn_kernel(*refs):
    inputs, out_ref, turned_ref = refs[:NY], refs[NY], refs[NY + 1]
    rows = [ref[r].astype(jnp.float32) for r in range(2) for ref in inputs]
    turned_ref[...] = jnp.concatenate(rows, 0).T
    for pair in range(FINE // 2):
        even = turned_ref[pl.ds(2 * pair, COARSE, stride=FINE), :].astype(jnp.bfloat16)
        odd = turned_ref[pl.ds(2 * pair + 1, COARSE, stride=FINE), :].astype(jnp.bfloat16)
        for r in range(2):
            lanes = slice(64 * r, 64 * r + 64)
            out_ref[COARSE * r : COARSE * (r + 1), 128 * pair : 128 * (pair + 1)] = jnp.concatenate(
                [even[:, lanes], odd[:, lanes]], 1
            )


def turn(parts):
    return pl.pallas_call(
        turn_kernel,
        out_shape=jax.ShapeDtypeStruct((ROWS, DEPTH), jnp.bfloat16),
        scratch_shapes=[pltpu.VMEM((TLEN, 128), jnp.float32)],
        name="turn",
    )(*parts)


def join_kernel(x_ref, *refs):
    inputs, out_ref, wide_ref = refs[:NX], refs[NX], refs[NX + 1]
    for d, ref in enumerate(inputs):
        kk = lax.rem(x_ref[0] + NX - d, NX)
        for r in range(2):
            block = ref[COARSE * r : COARSE * (r + 1), :].astype(jnp.float32)
            for i in range(DEPTH // 128):
                rows = pl.ds(NX * r + kk, COARSE, stride=2 * NX)
                wide_ref[i, rows, :] = block[:, 128 * i : 128 * (i + 1)]
    for i in range(DEPTH // 128):
        out_ref[:, 128 * i : 128 * (i + 1)] = wide_ref[i].astype(jnp.bfloat16)


def join(x, parts):
    return pl.pallas_call(
        join_kernel,
        grid_spec=pltpu.PrefetchScalarGridSpec(
            num_scalar_prefetch=1,
            grid=(1,),
            in_specs=[pl.BlockSpec((ROWS, DEPTH), lambda n, i: (0, 0))] * NX,
            out_specs=pl.BlockSpec((HALF, DEPTH), lambda n, i: (0, 0)),
            scratch_shapes=[pltpu.VMEM((DEPTH // 128, HALF, 128), jnp.float32)],
        ),
        out_shape=jax.ShapeDtypeStruct((HALF, DEPTH), jnp.bfloat16),
        name="join",
    )(x[None], *parts)


def spread_kernel(*refs):
    inputs, x2_ref, energy_ref, power_ref = refs[:NY], refs[NY], refs[NY + 1], refs[NY + 2]
    step = pl.program_id(0)

    @pl.when(step == 0)
    def _():
        power_ref[...] = jnp.zeros_like(power_ref)

    rows = jnp.concatenate([ref[...].astype(jnp.float32) for ref in inputs], 0)
    power_ref[...] += jnp.sum((rows * rows).reshape(NY * SUB // 8, 8, EXT), 0)
    for e in range(FINE):
        moved = pltpu.roll(rows, EXT - e, 1) if e else rows
        x2_ref[0, 64 * e : 64 * (e + 1), :] = moved.astype(jnp.bfloat16)

    @pl.when(step == pl.num_programs(0) - 1)
    def _():
        total = power_ref[...]
        width = 1
        while width < TLEN:
            total = total + pltpu.roll(total, EXT - width, 1)
            width *= 2
        energy_ref[...] = jnp.sum(total, 0, keepdims=True)[:, :TILE]


def spread(sensors):
    return pl.pallas_call(
        spread_kernel,
        grid=(NZ,),
        in_specs=[pl.BlockSpec((SUB, EXT), lambda n: (n, 0))] * NY,
        out_specs=[
            pl.BlockSpec((1, DEPTH, EXT), lambda n: (n, 0, 0)),
            pl.BlockSpec((1, TILE), lambda n: (0, 0)),
        ],
        out_shape=[
            jax.ShapeDtypeStruct((NZ, DEPTH, EXT), jnp.bfloat16),
            jax.ShapeDtypeStruct((1, TILE), jnp.float32),
        ],
        scratch_shapes=[pltpu.VMEM((8, EXT), jnp.float32)],
        compiler_params=pltpu.CompilerParams(vmem_limit_bytes=VMEM_LIMIT),
        cost_estimate=pl.CostEstimate(flops=2**24, bytes_accessed=24 * 2**20, transcendentals=0),
        name="spread",
    )(*sensors)


def square_sums(left):
    wide = left.astype(jnp.float32)
    wide = wide * wide
    total = wide[:, :128]
    for i in range(128, wide.shape[1], 128):
        total = total + wide[:, i : i + 128]
    return total


def fold(y_ref, start):
    split = COARSE // 2
    parts = []
    for j in range(split):
        near, far = start + 8 * j, start + 8 * (j + split)
        parts.append(y_ref[near : near + 8, : EXT - 128] + y_ref[far : far + 8, 128:])
    width = FINE
    while len(parts) > 1:
        parts = [
            parts[i] + pltpu.roll(parts[i + 1], EXT - 128 - width, 1)
            for i in range(0, len(parts), 2)
        ]
        width *= 2
    return parts[0][:, :TILE]


def correlate_kernel(blocks, places, seeded, closing, index_ref, *refs):
    refs = list(refs)
    take = lambda n: [refs.pop(0) for _ in range(n)]
    lefts = [take(n) for n in blocks]
    x2_ref = take(1)[0]
    extra_refs = take(2 * seeded + closing)
    outs = take(1 if closing else 2)
    y_ref, left_ref, right_ref = take(3)
    extras = take(len(extra_refs))
    sem_ref = take(1)[0]
    used = 0

    def begin(source, target):
        nonlocal used
        copy = pltpu.make_async_copy(source, target, sem_ref.at[used])
        copy.start()
        used += 1
        return copy

    left_copies = []
    for c, group in enumerate(lefts):
        row = 0
        for ref in group:
            target = left_ref.at[row : row + ref.shape[0], DEPTH * c : DEPTH * (c + 1)]
            left_copies.append(begin(ref, target))
            row += ref.shape[0]
    right_copies = []
    for t in range(EXT // TIME_TILE):
        lanes = slice(TIME_TILE * t, TIME_TILE * (t + 1))
        right_copies.append(
            [
                begin(
                    x2_ref.at[index_ref[place], :, lanes],
                    right_ref.at[t, DEPTH * c : DEPTH * (c + 1)],
                )
                for c, place in enumerate(places)
            ]
        )
    extra_copies = [begin(ref, extra) for ref, extra in zip(extra_refs, extras)]
    for copy in left_copies:
        copy.wait()
    for t in range(EXT // TIME_TILE):
        for copy in right_copies[t]:
            copy.wait()
        y_ref[:, TIME_TILE * t : TIME_TILE * (t + 1)] = jnp.dot(
            left_ref[...], right_ref[t], preferred_element_type=jnp.float32
        )
    for copy in extra_copies:
        copy.wait()

    norm = square_sums(left_ref[...])
    sums = [fold(y_ref, half * HALF) for half in range(2)]
    if seeded:
        norm = norm + extras[1][...]
        sums = [sums[half] + extras[0][8 * half : 8 * half + 8] for half in range(2)]
    if not closing:
        for half in range(2):
            outs[0][8 * half : 8 * half + 8, :] = sums[half]
        outs[1][...] = norm
        return
    scale = math.sqrt(SENSORS * TLEN)
    level = extras[2][...] + 1e-05
    for half in range(2):
        squares = jnp.sum(norm[half * HALF : (half + 1) * HALF].reshape(COARSE, 8, 128), 0)
        squares = jnp.sum(squares, 1, keepdims=True)
        sums[half] = sums[half] * scale * lax.rsqrt(squares * level)
    first = index_ref[NZ] == 0
    low = jnp.where(first, sums[0], sums[1])
    high = jnp.where(first, sums[1], sums[0])
    for r in range(2):
        outs[0][r, :NX, :] = low[NX * r : NX * (r + 1)]
        outs[0][r, NX:, :] = high[NX * r : NX * (r + 1)]


def correlate(index, places, lefts, x2, before=None, energy=None):
    count = len(lefts)
    seeded, closing = before is not None, energy is not None
    extra = (list(before) if seeded else []) + ([energy] if closing else [])
    operands = [ref for group in lefts for ref in group] + [x2] + extra
    if closing:
        out_shape = jax.ShapeDtypeStruct((2, 8, TILE), jnp.float32)
    else:
        out_shape = [
            jax.ShapeDtypeStruct((16, TILE), jnp.float32),
            jax.ShapeDtypeStruct((2 * HALF, 128), jnp.float32),
        ]
    blocks = [len(group) for group in lefts]
    tiles = EXT // TIME_TILE
    return pl.pallas_call(
        lambda *refs: correlate_kernel(blocks, list(places), seeded, closing, *refs),
        in_specs=[pl.BlockSpec(memory_space=pltpu.SMEM)]
        + [pl.BlockSpec(memory_space=pl.ANY)] * len(operands),
        scratch_shapes=[
            pltpu.VMEM((2 * HALF, EXT), jnp.float32),
            pltpu.VMEM((2 * HALF, DEPTH * count), jnp.bfloat16),
            pltpu.VMEM((tiles, DEPTH * count, TIME_TILE), jnp.bfloat16),
            *[pltpu.VMEM(a.shape, a.dtype) for a in extra],
            pltpu.SemaphoreType.DMA((sum(blocks) + tiles * count + len(extra),)),
        ],
        out_shape=out_shape,
        compiler_params=pltpu.CompilerParams(vmem_limit_bytes=VMEM_LIMIT),
        cost_estimate=pl.CostEstimate(
            flops=2 * 2 * HALF * DEPTH * count * EXT,
            bytes_accessed=count * 3 * 2**20,
            transcendentals=0,
        ),
        name="correlate",
    )(index, *operands)


def local(record, templates, block_ids, sensor_group):
    zh, x, core = lax.axis_index("zh"), lax.axis_index("x"), lax.axis_index("core")
    y, bank = lax.axis_index("chan"), lax.axis_index("bank")
    z = zh * 2 + bank

    owner_chip = plane_index((block_ids >> 2) & 3, (block_ids >> 4) * 2 + (block_ids & 1))
    owner_core = (block_ids >> 1) & 1
    my_chip = plane_index(x, z)
    halves = templates.reshape(NY, 2, NX, 4, 2, SUB, TLEN).transpose(1, 3, 2, 4, 0, 5, 6)
    halves = halves.reshape(2, 32, NY * SUB, TLEN)
    given = lax.dynamic_index_in_dim(halves, 1 - core, 0, keepdims=False)
    received = shift(given, "core", 1)
    mine = lax.dynamic_index_in_dim(halves, core, 0, keepdims=False)

    leading = record[:, :HALO]
    following = lax.ppermute(leading, BLOCKS, [(i, i - 1) for i in range(1, 64)])

    extended = jnp.concatenate([record, following], 1)
    delayed = jnp.zeros((128, EXT), jnp.bfloat16)
    for group_id in range(GROUPS):
        moved = extended[:, DSTEP * group_id : DSTEP * group_id + EXT]
        delayed = jnp.where((sensor_group == group_id)[:, None], moved, delayed)
    first_core = jnp.where(owner_chip[0] == my_chip, owner_core[0], owner_core[1])
    block = jnp.where(first_core == core, mine, received)
    delayed, block = lax.optimization_barrier((delayed, block))
    sensors = [delayed] + [shift(delayed, "chan", d) for d in (1, 2, 3)]
    x2, energy = spread(sensors)
    got = lax.all_to_all(block, PLANE, 0, 0, tiled=True)
    clash = (owner_chip[0] == owner_chip[1]) & (owner_core[0] != owner_core[1])

    def second():
        block = jnp.where(owner_core[1] == core, mine, received)
        return lax.all_to_all(block, PLANE, 0, 0, tiled=True)[owner_chip[1]]

    spare = lax.cond(clash, second, lambda: jnp.zeros(mine.shape[1:], mine.dtype))
    piece = jnp.stack([got[owner_chip[0]], jnp.where(clash, spare, got[owner_chip[1]])])

    piece, x2, energy = lax.optimization_barrier((piece, x2, energy))
    piece = piece.reshape(2, NY, SUB, TLEN)
    parts = [lax.dynamic_index_in_dim(piece, y, 1, keepdims=False)]
    for d in (1, 2, 3):
        part = lax.dynamic_index_in_dim(piece, (y + d) % NY, 1, keepdims=False)
        parts.append(shift(part, "chan", d))
    piece = turn(parts)

    column = join(x, [piece] + [shift(piece, "x", d) for d in (1, 2, 3)])
    column, x2, energy = lax.optimization_barrier((column, x2, energy))
    offsets = jnp.array([0, 1, -1, 2, -2, 3, -3, 4], jnp.int32)
    index = jnp.concatenate([(z - offsets) % NZ, core[None]]).astype(jnp.int32)
    arrived, ahead, behind, sums = [column], column, column, None
    for i in range(4):
        if i < 3:
            nearer, farther = shift(ahead, ZAXES, 1), shift(behind, ZAXES, -1)
        else:
            nearer = shift(ahead[: HALF // 2], ZAXES, 1)
            farther = shift(behind[HALF // 2 :], ZAXES, -1)
        lefts = [[block, shift(block, "core", 1)] for block in arrived]
        places = range(max(0, 2 * i - 1), 2 * i + 1)
        sums = correlate(index, places, lefts, x2, sums)
        ahead, behind, sums = lax.optimization_barrier((nearer, farther, sums))
        arrived = [ahead, behind]
    lefts = [[ahead, behind, shift(ahead, "core", 1), shift(behind, "core", 1)]]
    return correlate(index, [7], lefts, x2, sums, energy)


def solution(mesh):
    fine = Mesh(mesh.devices.reshape(4, NX, 2, NY, 2), ("zh", "x", "core", "chan", "bank"))
    return jax.shard_map(
        local,
        mesh=fine,
        in_specs=(P("chan", BLOCKS), P(BLOCKS, "chan", None), P(), P("chan")),
        out_specs=P(None, "chan", BLOCKS),
        check_vma=False,
    )
```

time: 706 us -> 138 us (0.20)
  matrix products: 431 us -> 0 us
  waiting for transfers between devices: 222 us -> 28 us
  starting transfers between devices: 5.02 us -> 48.3 us
  Pallas kernels: 0 us -> 43.1 us
  blocking collectives: 8.66 us -> 0 us
    conv_general_dilated x1 -> x0, matrix products: 431 us -> none  [correlate(): lax.conv_general_dilated(window[None], template_block, (1,), 'VALID', dim...]
    psum x1 -> x0, waiting for transfers between devices: 188 us -> none  [broadcast(): return lax.psum(block, axis)]
    pallas_call x0 -> x8, Pallas kernels: none -> 43.1 us  [the longest x5 30.2 us: correlate(): pl.pallas_call(lambda *refs: correlate_kernel(blocks, list(places), seede...]
    ppermute x1 -> x28, starting transfers between devices: 4.94 us -> 38.3 us  [the longest x27 36.4 us: shift(): lax.ppermute(value, axis, [(i, (i + steps) % count) for i in range(count)])]
    reduce_scatter x2 -> x0, waiting for transfers between devices: 33.3 us -> none  [local(): lax.psum_scatter(partial_value, 'chan', scatter_dimension=0, tiled=True)]
    ppermute x1 -> x28, waiting for transfers between devices: 0.65 us -> 28 us  [the longest x27 27.9 us: shift(): lax.ppermute(value, axis, [(i, (i + steps) % count) for i in range(count)])]
    all_to_all x0 -> x1, starting transfers between devices: none -> 10 us  [local(): got = lax.all_to_all(block, PLANE, 0, 0, tiled=True)]
    psum x1 -> x0, blocking collectives: 8.66 us -> none  [local(): lax.psum(running[tap_count:tap_count + samples_dev] - running[:samples_de...]
  transfers between devices with their start and end apart: 4 -> 29, of which waited for: 4 -> 10; matrix products, arithmetic and copies ran while one was open for 1% -> 1% of each run, Pallas kernels for 0% -> 24%
where the time goes in v1:
time: 138 us; the launch traced here: 139 us
  starting transfers between devices  48.3 us (35%)
  Pallas kernels  43.1 us (31%)
  waiting for transfers between devices  28 us (20%)
  between operations  8.67 us (6%)
  local copies, waits for them, and re-layouts  7.13 us (5%)
  other arithmetic  3.29 us (2%)
    ppermute x27, starting transfers between devices, shift(): lax.ppermute(value, axis, [(i, (i + steps) % count) for i in range(count)])  36.4 us
    pallas_call x5, Pallas kernels, correlate(): pl.pallas_call(lambda *refs: correlate_kernel(blocks, list(places), seede...  30.2 us
    ppermute x27, waiting for transfers between devices, shift(): lax.ppermute(value, axis, [(i, (i + steps) % count) for i in range(count)])  27.9 us
    all_to_all x1, starting transfers between devices, local(): got = lax.all_to_all(block, PLANE, 0, 0, tiled=True)  10 us
    pallas_call x1, Pallas kernels, spread(): pl.pallas_call(spread_kernel, grid=(NZ,), in_specs=[pl.BlockSpec((SUB, EX...  9.48 us
  transfers between devices with their start and end apart: 29, of which 10 were waited for; matrix products, arithmetic and copies ran while one was open for 1% of the time, Pallas kernels for 24%

profile of v1, /device:TPU:1, one launch (start us, length us, event | category | flops | bytes accessed | tf_op | source)
XLA Modules:
  0.0 138.5 jit_solution(9199010060038791468)
XLA Ops:
  0.0 1.9 %copy.6 = bf16[2,4,4,2,4,16,256]{6,5,4,3,2,1,0:T(8,128)(2,1)S(1)} copy(bf16[2,4,4,2,4,16,256]{6,5,3,1,2,0,4:T(8,128)(2,1)} %bitcast.44) | data formatting | bytes 4194304 | tf_op jit(solution)/shard_map/transpose | solution.py:279
  3.0 3.2 %collective-permute-start.1 = (bf16[32,64,256]{2,1,0:T(8,128)(2,1)}, bf16[32,64,256]{2,1,0:T(8,128)(2,1)}, u32[]{:S(2)}, u32[]{:S(2)}) collective-permute-start(bf16[32,64,256]{2,1,0:T(8,128)(2,1)} %dynamic-slice_bitcast_fusion.1), channel_id=1, source_target_pairs={{0,8},{8,0},{1,9},{9,1},{2,10},{10,2},{3,11},{11,3},{4,12},{12,4},... | collective-permute-start | bytes 3145736 | tf_op jit(solution)/shard_map/ppermute | solution.py:34
  6.9 1.9 %collective-permute-start = (bf16[128,512]{1,0:T(8,128)(2,1)}, bf16[128,512]{1,0:T(8,128)(2,1)S(1)}, u32[]{:S(2)}, u32[]{:S(2)}) collective-permute-start(bf16[128,512]{1,0:T(8,128)(2,1)} %slice.44), channel_id=1, source_target_pairs={{1,0},{8,1},{9,8},{16,9},{17,16},{24,17},{25,24},{32,25},{33,32},{... | collective-permute-start | bytes 393224 | tf_op jit(solution)/shard_map/ppermute | solution.py:286
  14.6 2.7 %broadcast_select_fusion.1 = (bf16[32,64,256]{2,1,0:T(8,128)(2,1)}, bf16[32,64,256]{2,1,0:T(8,128)(2,1)}) fusion(bf16[32,64,256]{2,1,0:T(8,128)(2,1)} %collective-permute-done.1, pred[]{:T(512)S(6)} %eq.54, bf16[2,32,64,256]{3,2,1,0:T(8,128)(2,1)S(1)} %bitcast.43, s32[]{:T(128)S(6)} %select_n.118), kind=kLoop, calls=%fused_computation.4 | loop fusion | flops 524288 | bytes 4194309 | tf_op jit(solution)/shard_map/jit(_where)/select_n | solution.py:294
  17.3 10.0 %all-to-all-start.1 = ((bf16[32,64,256]{2,1,0:T(8,128)(2,1)}), bf16[32,64,256]{2,1,0:T(8,128)(2,1)S(1)}, u32[]{:S(2)}, u32[]{:S(2)}) async-start(bf16[32,64,256]{2,1,0:T(8,128)(2,1)} %get-tuple-element.57), calls=%async_computation.1 | async-start | bytes 2097152 | tf_op jit(solution)/shard_map/all_to_all | solution.py:298
  27.3 1.4 collective-permute-start.2
  28.7 2.6 %collective-permute-start.3 = (bf16[128,2304]{1,0:T(8,128)(2,1)S(1)}, bf16[128,2304]{1,0:T(8,128)(2,1)S(1)}, u32[]{:S(2)}, u32[]{:S(2)}) collective-permute-start(bf16[128,2304]{1,0:T(8,128)(2,1)S(1)} %fusion.2.refs_0_), channel_id=1, source_target_pairs={{0,4},{2,6},{4,0},{6,2},{1,5},{3,7},{5,1},{7,3},{8,12},{10,14},{12... | collective-permute-start | bytes 1769480 | tf_op jit(solution)/shard_map/ppermute | solution.py:34
  31.3 1.1 collective-permute-start.4
  36.2 7.6 %collective-permute-done.2.refs_1_ = bf16[128,2304]{1,0:T(8,128)(2,1)S(1)} collective-permute-done((bf16[128,2304]{1,0:T(8,128)(2,1)S(1)}, bf16[128,2304]{1,0:T(8,128)(2,1)S(1)}, u32[]{:S(2)}, u32[]{:S(2)}) %collective-permute-start.2) | collective-permute-done | bytes 589856 | tf_op jit(solution)/shard_map/ppermute | solution.py:34
  43.8 13.7 %collective-permute-done.3.refs_2_ = bf16[128,2304]{1,0:T(8,128)(2,1)S(1)} collective-permute-done((bf16[128,2304]{1,0:T(8,128)(2,1)S(1)}, bf16[128,2304]{1,0:T(8,128)(2,1)S(1)}, u32[]{:S(2)}, u32[]{:S(2)}) %collective-permute-start.3) | collective-permute-done | bytes 589856 | tf_op jit(solution)/shard_map/ppermute | solution.py:34
  57.5 9.5 %spread.1 = (bf16[8,512,2304]{2,1,0:T(8,128)(2,1)}, f32[1,2048]{1,0:T(1,128)S(1)}) custom-call(bf16[128,2304]{1,0:T(8,128)(2,1)S(1)} %fusion.2.refs_0_, bf16[128,2304]{1,0:T(8,128)(2,1)S(1)} %collective-permute-done.2.refs_1_, bf16[128,2304]{1,0:T(8,128)(2,1)S(1)} %collective-permute-done.3.refs_2_, bf16[128,2304]{1,0:T(8,128)(2,1)S(1)} %collective-permute-done.4.refs_3_), custom_call_target="tpu_custom_call" | custom-call | flops 16777216 | bytes 25165824 | tf_op jit(solution)/shard_map/spread/pallas_call | solution.py:117
  68.6 2.3 %collective-permute-start.6 = (bf16[2,16,256]{2,1,0:T(8,128)(2,1)S(1)}, bf16[2,16,256]{2,1,0:T(8,128)(2,1)S(1)}, u32[]{:S(2)}, u32[]{:S(2)}) collective-permute-start(bf16[2,16,256]{2,1,0:T(8,128)(2,1)S(1)} %get-tuple-element.94), channel_id=1, source_target_pairs={{0,4},{2,6},{4,0},{6,2},{1,5},{3,7},{5,1},{7,3},{8,12},{10,14},{12... | collective-permute-start | bytes 49160 | tf_op jit(solution)/shard_map/ppermute | solution.py:34
  70.9 1.2 collective-permute-start.7
  72.7 1.1 collective-permute-done.7.refs_3_
  74.4 1.6 %turn.1.refs_0_ = bf16[64,512]{1,0:T(8,128)(2,1)} custom-call(bf16[2,16,256]{2,1,0:T(8,128)(2,1)} %get-tuple-element.96.refs_0_, bf16[2,16,256]{2,1,0:T(8,128)(2,1)} %copy-done.5, bf16[2,16,256]{2,1,0:T(8,128)(2,1)} %copy-done.6, bf16[2,16,256]{2,1,0:T(8,128)(2,1)} %copy-done.7), custom_call_target="tpu_custom_call" | custom-call | tf_op jit(solution)/shard_map/turn/pallas_call | solution.py:56
  76.0 1.3 collective-permute-start.8
  77.4 2.4 %collective-permute-start.9 = (bf16[64,512]{1,0:T(8,128)(2,1)}, bf16[64,512]{1,0:T(8,128)(2,1)S(1)}, u32[]{:S(2)}, u32[]{:S(2)}) collective-permute-start(bf16[64,512]{1,0:T(8,128)(2,1)} %turn.1.refs_0_), channel_id=1, source_target_pairs={{0,32},{16,48},{32,0},{48,16},{1,33},{17,49},{33,1},{49,17},{2,34}... | collective-permute-start | bytes 196616 | tf_op jit(solution)/shard_map/ppermute | solution.py:34
  79.8 1.2 collective-permute-start.10
  81.0 1.4 %collective-permute-done.9.refs_2_ = bf16[64,512]{1,0:T(8,128)(2,1)S(1)} collective-permute-done((bf16[64,512]{1,0:T(8,128)(2,1)}, bf16[64,512]{1,0:T(8,128)(2,1)S(1)}, u32[]{:S(2)}, u32[]{:S(2)}) %collective-permute-start.9) | collective-permute-done | bytes 65568 | tf_op jit(solution)/shard_map/ppermute | solution.py:34
  84.0 1.8 %join.1.refs_1_ = bf16[256,512]{1,0:T(8,128)(2,1)} custom-call(s32[1]{0:T(128)} %bitcast.4.x_ref, bf16[64,512]{1,0:T(8,128)(2,1)} %turn.1.refs_0_, bf16[64,512]{1,0:T(8,128)(2,1)} %copy-done.2, bf16[64,512]{1,0:T(8,128)(2,1)} %copy-done.3, bf16[64,512]{1,0:T(8,128)(2,1)} %copy-done.4), custom_call_target="tpu_custom_call" | custom-call | tf_op jit(solution)/shard_map/join/pallas_call | solution.py:78
  85.8 1.2 collective-permute-start.11
  87.0 1.5 %collective-permute-start.12 = (bf16[256,512]{1,0:T(8,128)(2,1)}, bf16[256,512]{1,0:T(8,128)(2,1)S(1)}, u32[]{:S(2)}, u32[]{:S(2)}) collective-permute-start(bf16[256,512]{1,0:T(8,128)(2,1)} %join.1.refs_1_), channel_id=1, source_target_pairs={{0,193},{1,0},{64,1},{65,64},{128,65},{129,128},{192,129},{193,192... | collective-permute-start | bytes 786440 | tf_op jit(solution)/shard_map/ppermute | solution.py:34
  88.5 3.8 %collective-permute-start.13 = (bf16[256,512]{1,0:T(8,128)(2,1)}, bf16[256,512]{1,0:T(8,128)(2,1)S(1)}, u32[]{:S(2)}, u32[]{:S(2)}) collective-permute-start(bf16[256,512]{1,0:T(8,128)(2,1)} %join.1.refs_1_), channel_id=1, source_target_pairs={{0,8},{8,0},{1,9},{9,1},{2,10},{10,2},{3,11},{11,3},{4,12},{12,4},... | collective-permute-start | bytes 786440 | tf_op jit(solution)/shard_map/ppermute | solution.py:34
  92.4 1.3 collective-permute-done.13.refs_2_
  94.6 4.2 %correlate.5 = (f32[16,2048]{1,0:T(8,128)S(1)}, f32[512,128]{1,0:T(8,128)S(1)}) custom-call(s32[9]{0:T(128)S(1)} %pad_add_fusion.refs_0_, bf16[256,512]{1,0:T(8,128)(2,1)S(1)} %copy-done, bf16[256,512]{1,0:T(8,128)(2,1)S(1)} %collective-permute-done.13.refs_2_, bf16[8,512,2304]{2,1,0:T(8,128)(2,1)} %get-tuple-element.65.refs_3_.refs_5_), custom_call_target="tpu_custom_call" | custom-call | flops 1207959552 | bytes 3145728 | tf_op jit(solution)/shard_map/correlate/pallas_call | solution.py:249
  99.5 2.7 %collective-permute-start.15 = (bf16[256,512]{1,0:T(8,128)(2,1)S(1)}, bf16[256,512]{1,0:T(8,128)(2,1)S(1)}, u32[]{:S(2)}, u32[]{:S(2)}) collective-permute-start(bf16[256,512]{1,0:T(8,128)(2,1)S(1)} %collective-permute-done.12.refs_3_), channel_id=1, source_target_pairs={{0,193},{1,0},{64,1},{65,64},{128,65},{129,128},{192,129},{193,192... | collective-permute-start | bytes 786440 | tf_op jit(solution)/shard_map/ppermute | solution.py:34
  102.1 6.7 %correlate.6 = (f32[16,2048]{1,0:T(8,128)S(1)}, f32[512,128]{1,0:T(8,128)S(1)}) custom-call(s32[9]{0:T(128)S(1)} %pad_add_fusion.refs_0_, bf16[256,512]{1,0:T(8,128)(2,1)S(1)} %collective-permute-done.11.refs_1_, bf16[256,512]{1,0:T(8,128)(2,1)S(1)} %collective-permute-done.16.refs_2_, bf16[256,512]{1,0:T(8,128)(2,1)S(1)} %collective-permute-done.12.refs_3_, ...), custom_call_target="tpu_custom_call" | custom-call | flops 2415919104 | bytes 6291456 | tf_op jit(solution)/shard_map/correlate/pallas_call | solution.py:249
  110.3 2.3 %collective-permute-start.19 = (bf16[256,512]{1,0:T(8,128)(2,1)S(1)}, bf16[256,512]{1,0:T(8,128)(2,1)S(1)}, u32[]{:S(2)}, u32[]{:S(2)}) collective-permute-start(bf16[256,512]{1,0:T(8,128)(2,1)S(1)} %collective-permute-done.15.refs_3_), channel_id=1, source_target_pairs={{0,193},{1,0},{64,1},{65,64},{128,65},{129,128},{192,129},{193,192... | collective-permute-start | bytes 786440 | tf_op jit(solution)/shard_map/ppermute | solution.py:34
  112.7 6.7 %correlate.7 = (f32[16,2048]{1,0:T(8,128)S(1)}, f32[512,128]{1,0:T(8,128)S(1)}) custom-call(s32[9]{0:T(128)S(1)} %pad_add_fusion.refs_0_, bf16[256,512]{1,0:T(8,128)(2,1)S(1)} %collective-permute-done.14.refs_1_, bf16[256,512]{1,0:T(8,128)(2,1)S(1)} %collective-permute-done.20.refs_2_, bf16[256,512]{1,0:T(8,128)(2,1)S(1)} %collective-permute-done.15.refs_3_, ...), custom_call_target="tpu_custom_call" | custom-call | flops 2415919104 | bytes 6291456 | tf_op jit(solution)/shard_map/correlate/pallas_call | solution.py:249
  120.5 2.2 %collective-permute-start.22 = (bf16[128,512]{1,0:T(8,128)(2,1)S(1)}, bf16[128,512]{1,0:T(8,128)(2,1)S(1)}, u32[]{:S(2)}, u32[]{:S(2)}) collective-permute-start(bf16[128,512]{1,0:T(8,128)(2,1)S(1)} %slice.53), channel_id=1, source_target_pairs={{0,1},{1,64},{64,65},{65,128},{128,129},{129,192},{192,193},{193,0... | collective-permute-start | bytes 393224 | tf_op jit(solution)/shard_map/ppermute | solution.py:34
  123.3 6.7 %correlate.8 = (f32[16,2048]{1,0:T(8,128)S(1)}, f32[512,128]{1,0:T(8,128)S(1)}) custom-call(s32[9]{0:T(128)S(1)} %pad_add_fusion.refs_0_, bf16[256,512]{1,0:T(8,128)(2,1)S(1)} %collective-permute-done.18.refs_1_, bf16[256,512]{1,0:T(8,128)(2,1)S(1)} %collective-permute-done.24.refs_2_, bf16[256,512]{1,0:T(8,128)(2,1)S(1)} %collective-permute-done.19.refs_3_, ...), custom_call_target="tpu_custom_call" | custom-call | flops 2415919104 | bytes 6291456 | tf_op jit(solution)/shard_map/correlate/pallas_call | solution.py:249
  132.4 5.9 %correlate.9 = f32[2,8,2048]{2,1,0:T(8,128)} custom-call(s32[9]{0:T(128)S(1)} %pad_add_fusion.refs_0_, bf16[128,512]{1,0:T(8,128)(2,1)S(1)} %collective-permute-done.22.refs_1_, bf16[128,512]{1,0:T(8,128)(2,1)S(1)} %collective-permute-done.23.refs_2_, bf16[128,512]{1,0:T(8,128)(2,1)S(1)} %collective-permute-done.26.refs_3_, ...), custom_call_target="tpu_custom_call" | custom-call | flops 1207959552 | bytes 3145728 | tf_op jit(solution)/shard_map/correlate/pallas_call | solution.py:249
  (76 shorter events, 14.8 us)
Async XLA Ops:
  1.9 7.0 %copy-start.9 = (s32[2]{0:T(128)S(1)}, s32[2]{0:T(128)}, u32[]{:S(2)}) copy-start(s32[2]{0:T(128)} %param.9) | copy-start | bytes 28
  1.9 12.0 %copy-start.8 = (s32[128]{0:T(128)S(1)}, s32[128]{0:T(128)}, u32[]{:S(2)}) copy-start(s32[128]{0:T(128)} %param.10) | copy-start | bytes 1540
  3.0 11.6 %collective-permute-start.1 = (bf16[32,64,256]{2,1,0:T(8,128)(2,1)}, bf16[32,64,256]{2,1,0:T(8,128)(2,1)}, u32[]{:S(2)}, u32[]{:S(2)}) collective-permute-start(bf16[32,64,256]{2,1,0:T(8,128)(2,1)} %dynamic-slice_bitcast_fusion.1), channel_id=1, source_target_pairs={{0,8},{8,0},{1,9},{9,1},{2,10},{10,2},{3,11},{11,3},{4,12},{12,4},... | collective-permute-start | bytes 3145736 | tf_op jit(solution)/shard_map/ppermute | solution.py:34
  6.9 7.2 %collective-permute-start = (bf16[128,512]{1,0:T(8,128)(2,1)}, bf16[128,512]{1,0:T(8,128)(2,1)S(1)}, u32[]{:S(2)}, u32[]{:S(2)}) collective-permute-start(bf16[128,512]{1,0:T(8,128)(2,1)} %slice.44), channel_id=1, source_target_pairs={{1,0},{8,1},{9,8},{16,9},{17,16},{24,17},{25,24},{32,25},{33,32},{... | collective-permute-start | bytes 393224 | tf_op jit(solution)/shard_map/ppermute | solution.py:286
  17.3 49.7 %all-to-all-start.1 = ((bf16[32,64,256]{2,1,0:T(8,128)(2,1)}), bf16[32,64,256]{2,1,0:T(8,128)(2,1)S(1)}, u32[]{:S(2)}, u32[]{:S(2)}) async-start(bf16[32,64,256]{2,1,0:T(8,128)(2,1)} %get-tuple-element.57), calls=%async_computation.1 | async-start | bytes 2097152 | tf_op jit(solution)/shard_map/all_to_all | solution.py:298
  27.3 65.0 %copy-start.10 = (s32[8]{0:T(128)S(1)}, s32[8]{0:T(128)}, u32[]{:S(2)}) copy-start(s32[8]{0:T(128)} %constant.134) | copy-start | bytes 100
  27.3 16.5 %collective-permute-start.2 = (bf16[128,2304]{1,0:T(8,128)(2,1)S(1)}, bf16[128,2304]{1,0:T(8,128)(2,1)S(1)}, u32[]{:S(2)}, u32[]{:S(2)}) collective-permute-start(bf16[128,2304]{1,0:T(8,128)(2,1)S(1)} %fusion.2.refs_0_), channel_id=1, source_target_pairs={{0,2},{2,4},{4,6},{6,0},{1,3},{3,5},{5,7},{7,1},{8,10},{10,12},{12... | collective-permute-start | bytes 1769480 | tf_op jit(solution)/shard_map/ppermute | solution.py:34
  28.7 28.8 %collective-permute-start.3 = (bf16[128,2304]{1,0:T(8,128)(2,1)S(1)}, bf16[128,2304]{1,0:T(8,128)(2,1)S(1)}, u32[]{:S(2)}, u32[]{:S(2)}) collective-permute-start(bf16[128,2304]{1,0:T(8,128)(2,1)S(1)} %fusion.2.refs_0_), channel_id=1, source_target_pairs={{0,4},{2,6},{4,0},{6,2},{1,5},{3,7},{5,1},{7,3},{8,12},{10,14},{12... | collective-permute-start | bytes 1769480 | tf_op jit(solution)/shard_map/ppermute | solution.py:34
  31.3 26.2 %collective-permute-start.4 = (bf16[128,2304]{1,0:T(8,128)(2,1)S(1)}, bf16[128,2304]{1,0:T(8,128)(2,1)S(1)}, u32[]{:S(2)}, u32[]{:S(2)}) collective-permute-start(bf16[128,2304]{1,0:T(8,128)(2,1)S(1)} %fusion.2.refs_0_), channel_id=1, source_target_pairs={{0,6},{2,0},{4,2},{6,4},{1,7},{3,1},{5,3},{7,5},{8,14},{10,8},{12,... | collective-permute-start | bytes 1769480 | tf_op jit(solution)/shard_map/ppermute | solution.py:34
  67.6 4.5 %collective-permute-start.5 = (bf16[2,16,256]{2,1,0:T(8,128)(2,1)S(1)}, bf16[2,16,256]{2,1,0:T(8,128)(2,1)S(1)}, u32[]{:S(2)}, u32[]{:S(2)}) collective-permute-start(bf16[2,16,256]{2,1,0:T(8,128)(2,1)S(1)} %get-tuple-element.95), channel_id=1, source_target_pairs={{0,2},{2,4},{4,6},{6,0},{1,3},{3,5},{5,7},{7,1},{8,10},{10,12},{12... | collective-permute-start | bytes 49160 | tf_op jit(solution)/shard_map/ppermute | solution.py:34
  68.6 4.1 %collective-permute-start.6 = (bf16[2,16,256]{2,1,0:T(8,128)(2,1)S(1)}, bf16[2,16,256]{2,1,0:T(8,128)(2,1)S(1)}, u32[]{:S(2)}, u32[]{:S(2)}) collective-permute-start(bf16[2,16,256]{2,1,0:T(8,128)(2,1)S(1)} %get-tuple-element.94), channel_id=1, source_target_pairs={{0,4},{2,6},{4,0},{6,2},{1,5},{3,7},{5,1},{7,3},{8,12},{10,14},{12... | collective-permute-start | bytes 49160 | tf_op jit(solution)/shard_map/ppermute | solution.py:34
  70.9 2.9 %collective-permute-start.7 = (bf16[2,16,256]{2,1,0:T(8,128)(2,1)S(1)}, bf16[2,16,256]{2,1,0:T(8,128)(2,1)S(1)}, u32[]{:S(2)}, u32[]{:S(2)}) collective-permute-start(bf16[2,16,256]{2,1,0:T(8,128)(2,1)S(1)} %get-tuple-element.93), channel_id=1, source_target_pairs={{0,6},{2,0},{4,2},{6,4},{1,7},{3,1},{5,3},{7,5},{8,14},{10,8},{12,... | collective-permute-start | bytes 49160 | tf_op jit(solution)/shard_map/ppermute | solution.py:34
  76.0 4.9 %collective-permute-start.8 = (bf16[64,512]{1,0:T(8,128)(2,1)}, bf16[64,512]{1,0:T(8,128)(2,1)S(1)}, u32[]{:S(2)}, u32[]{:S(2)}) collective-permute-start(bf16[64,512]{1,0:T(8,128)(2,1)} %turn.1.refs_0_), channel_id=1, source_target_pairs={{0,16},{16,32},{32,48},{48,0},{1,17},{17,33},{33,49},{49,1},{2,18}... | collective-permute-start | bytes 196616 | tf_op jit(solution)/shard_map/ppermute | solution.py:34
  77.4 5.0 %collective-permute-start.9 = (bf16[64,512]{1,0:T(8,128)(2,1)}, bf16[64,512]{1,0:T(8,128)(2,1)S(1)}, u32[]{:S(2)}, u32[]{:S(2)}) collective-permute-start(bf16[64,512]{1,0:T(8,128)(2,1)} %turn.1.refs_0_), channel_id=1, source_target_pairs={{0,32},{16,48},{32,0},{48,16},{1,33},{17,49},{33,1},{49,17},{2,34}... | collective-permute-start | bytes 196616 | tf_op jit(solution)/shard_map/ppermute | solution.py:34
  79.8 3.6 %collective-permute-start.10 = (bf16[64,512]{1,0:T(8,128)(2,1)}, bf16[64,512]{1,0:T(8,128)(2,1)S(1)}, u32[]{:S(2)}, u32[]{:S(2)}) collective-permute-start(bf16[64,512]{1,0:T(8,128)(2,1)} %turn.1.refs_0_), channel_id=1, source_target_pairs={{0,48},{16,0},{32,16},{48,32},{1,49},{17,1},{33,17},{49,33},{2,50}... | collective-permute-start | bytes 196616 | tf_op jit(solution)/shard_map/ppermute | solution.py:34
  85.8 13.1 %collective-permute-start.11 = (bf16[256,512]{1,0:T(8,128)(2,1)}, bf16[256,512]{1,0:T(8,128)(2,1)S(1)}, u32[]{:S(2)}, u32[]{:S(2)}) collective-permute-start(bf16[256,512]{1,0:T(8,128)(2,1)} %join.1.refs_1_), channel_id=1, source_target_pairs={{0,1},{1,64},{64,65},{65,128},{128,129},{129,192},{192,193},{193,0... | collective-permute-start | bytes 786440 | tf_op jit(solution)/shard_map/ppermute | solution.py:34
  87.0 11.9 %collective-permute-start.12 = (bf16[256,512]{1,0:T(8,128)(2,1)}, bf16[256,512]{1,0:T(8,128)(2,1)S(1)}, u32[]{:S(2)}, u32[]{:S(2)}) collective-permute-start(bf16[256,512]{1,0:T(8,128)(2,1)} %join.1.refs_1_), channel_id=1, source_target_pairs={{0,193},{1,0},{64,1},{65,64},{128,65},{129,128},{192,129},{193,192... | collective-permute-start | bytes 786440 | tf_op jit(solution)/shard_map/ppermute | solution.py:34
  88.5 5.2 %collective-permute-start.13 = (bf16[256,512]{1,0:T(8,128)(2,1)}, bf16[256,512]{1,0:T(8,128)(2,1)S(1)}, u32[]{:S(2)}, u32[]{:S(2)}) collective-permute-start(bf16[256,512]{1,0:T(8,128)(2,1)} %join.1.refs_1_), channel_id=1, source_target_pairs={{0,8},{8,0},{1,9},{9,1},{2,10},{10,2},{3,11},{11,3},{4,12},{12,4},... | collective-permute-start | bytes 786440 | tf_op jit(solution)/shard_map/ppermute | solution.py:34
  98.9 3.3 %collective-permute-start.16 = (bf16[256,512]{1,0:T(8,128)(2,1)S(1)}, bf16[256,512]{1,0:T(8,128)(2,1)S(1)}, u32[]{:S(2)}, u32[]{:S(2)}) collective-permute-start(bf16[256,512]{1,0:T(8,128)(2,1)S(1)} %collective-permute-done.11.refs_1_), channel_id=1, source_target_pairs={{0,8},{8,0},{1,9},{9,1},{2,10},{10,2},{3,11},{11,3},{4,12},{12,4},... | collective-permute-start | bytes 786440 | tf_op jit(solution)/shard_map/ppermute | solution.py:34
  99.3 2.8 %collective-permute-start.17 = (bf16[256,512]{1,0:T(8,128)(2,1)S(1)}, bf16[256,512]{1,0:T(8,128)(2,1)S(1)}, u32[]{:S(2)}, u32[]{:S(2)}) collective-permute-start(bf16[256,512]{1,0:T(8,128)(2,1)S(1)} %collective-permute-done.12.refs_3_), channel_id=1, source_target_pairs={{0,8},{8,0},{1,9},{9,1},{2,10},{10,2},{3,11},{11,3},{4,12},{12,4},... | collective-permute-start | bytes 786440 | tf_op jit(solution)/shard_map/ppermute | solution.py:34
  99.5 9.4 %collective-permute-start.14 = (bf16[256,512]{1,0:T(8,128)(2,1)S(1)}, bf16[256,512]{1,0:T(8,128)(2,1)S(1)}, u32[]{:S(2)}, u32[]{:S(2)}) collective-permute-start(bf16[256,512]{1,0:T(8,128)(2,1)S(1)} %collective-permute-done.11.refs_1_), channel_id=1, source_target_pairs={{0,1},{1,64},{64,65},{65,128},{128,129},{129,192},{192,193},{193,0... | collective-permute-start | bytes 786440 | tf_op jit(solution)/shard_map/ppermute | solution.py:34
  99.5 9.4 %collective-permute-start.15 = (bf16[256,512]{1,0:T(8,128)(2,1)S(1)}, bf16[256,512]{1,0:T(8,128)(2,1)S(1)}, u32[]{:S(2)}, u32[]{:S(2)}) collective-permute-start(bf16[256,512]{1,0:T(8,128)(2,1)S(1)} %collective-permute-done.12.refs_3_), channel_id=1, source_target_pairs={{0,193},{1,0},{64,1},{65,64},{128,65},{129,128},{192,129},{193,192... | collective-permute-start | bytes 786440 | tf_op jit(solution)/shard_map/ppermute | solution.py:34
  108.8 3.8 %collective-permute-start.20 = (bf16[256,512]{1,0:T(8,128)(2,1)S(1)}, bf16[256,512]{1,0:T(8,128)(2,1)S(1)}, u32[]{:S(2)}, u32[]{:S(2)}) collective-permute-start(bf16[256,512]{1,0:T(8,128)(2,1)S(1)} %collective-permute-done.14.refs_1_), channel_id=1, source_target_pairs={{0,8},{8,0},{1,9},{9,1},{2,10},{10,2},{3,11},{11,3},{4,12},{12,4},... | collective-permute-start | bytes 786440 | tf_op jit(solution)/shard_map/ppermute | solution.py:34
  109.9 2.8 %collective-permute-start.21 = (bf16[256,512]{1,0:T(8,128)(2,1)S(1)}, bf16[256,512]{1,0:T(8,128)(2,1)S(1)}, u32[]{:S(2)}, u32[]{:S(2)}) collective-permute-start(bf16[256,512]{1,0:T(8,128)(2,1)S(1)} %collective-permute-done.15.refs_3_), channel_id=1, source_target_pairs={{0,8},{8,0},{1,9},{9,1},{2,10},{10,2},{3,11},{11,3},{4,12},{12,4},... | collective-permute-start | bytes 786440 | tf_op jit(solution)/shard_map/ppermute | solution.py:34
  110.0 9.4 %collective-permute-start.18 = (bf16[256,512]{1,0:T(8,128)(2,1)S(1)}, bf16[256,512]{1,0:T(8,128)(2,1)S(1)}, u32[]{:S(2)}, u32[]{:S(2)}) collective-permute-start(bf16[256,512]{1,0:T(8,128)(2,1)S(1)} %collective-permute-done.14.refs_1_), channel_id=1, source_target_pairs={{0,1},{1,64},{64,65},{65,128},{128,129},{129,192},{192,193},{193,0... | collective-permute-start | bytes 786440 | tf_op jit(solution)/shard_map/ppermute | solution.py:34
  110.3 9.0 %collective-permute-start.19 = (bf16[256,512]{1,0:T(8,128)(2,1)S(1)}, bf16[256,512]{1,0:T(8,128)(2,1)S(1)}, u32[]{:S(2)}, u32[]{:S(2)}) collective-permute-start(bf16[256,512]{1,0:T(8,128)(2,1)S(1)} %collective-permute-done.15.refs_3_), channel_id=1, source_target_pairs={{0,193},{1,0},{64,1},{65,64},{128,65},{129,128},{192,129},{193,192... | collective-permute-start | bytes 786440 | tf_op jit(solution)/shard_map/ppermute | solution.py:34
  119.3 3.9 %collective-permute-start.24 = (bf16[256,512]{1,0:T(8,128)(2,1)S(1)}, bf16[256,512]{1,0:T(8,128)(2,1)S(1)}, u32[]{:S(2)}, u32[]{:S(2)}) collective-permute-start(bf16[256,512]{1,0:T(8,128)(2,1)S(1)} %collective-permute-done.18.refs_1_), channel_id=1, source_target_pairs={{0,8},{8,0},{1,9},{9,1},{2,10},{10,2},{3,11},{11,3},{4,12},{12,4},... | collective-permute-start | bytes 786440 | tf_op jit(solution)/shard_map/ppermute | solution.py:34
  120.4 2.9 %collective-permute-start.25 = (bf16[256,512]{1,0:T(8,128)(2,1)S(1)}, bf16[256,512]{1,0:T(8,128)(2,1)S(1)}, u32[]{:S(2)}, u32[]{:S(2)}) collective-permute-start(bf16[256,512]{1,0:T(8,128)(2,1)S(1)} %collective-permute-done.19.refs_3_), channel_id=1, source_target_pairs={{0,8},{8,0},{1,9},{9,1},{2,10},{10,2},{3,11},{11,3},{4,12},{12,4},... | collective-permute-start | bytes 786440 | tf_op jit(solution)/shard_map/ppermute | solution.py:34
  120.5 9.4 %collective-permute-start.22 = (bf16[128,512]{1,0:T(8,128)(2,1)S(1)}, bf16[128,512]{1,0:T(8,128)(2,1)S(1)}, u32[]{:S(2)}, u32[]{:S(2)}) collective-permute-start(bf16[128,512]{1,0:T(8,128)(2,1)S(1)} %slice.53), channel_id=1, source_target_pairs={{0,1},{1,64},{64,65},{65,128},{128,129},{129,192},{192,193},{193,0... | collective-permute-start | bytes 393224 | tf_op jit(solution)/shard_map/ppermute | solution.py:34
  122.7 7.2 %collective-permute-start.23 = (bf16[128,512]{1,0:T(8,128)(2,1)S(1)}, bf16[128,512]{1,0:T(8,128)(2,1)S(1)}, u32[]{:S(2)}, u32[]{:S(2)}) collective-permute-start(bf16[128,512]{1,0:T(8,128)(2,1)S(1)} %slice.54), channel_id=1, source_target_pairs={{0,193},{1,0},{64,1},{65,64},{128,65},{129,128},{192,129},{193,192... | collective-permute-start | bytes 393224 | tf_op jit(solution)/shard_map/ppermute | solution.py:34
  130.0 2.0 %collective-permute-start.26 = (bf16[128,512]{1,0:T(8,128)(2,1)S(1)}, bf16[128,512]{1,0:T(8,128)(2,1)S(1)}, u32[]{:S(2)}, u32[]{:S(2)}) collective-permute-start(bf16[128,512]{1,0:T(8,128)(2,1)S(1)} %collective-permute-done.22.refs_1_), channel_id=1, source_target_pairs={{0,8},{8,0},{1,9},{9,1},{2,10},{10,2},{3,11},{11,3},{4,12},{12,4},... | collective-permute-start | bytes 393224 | tf_op jit(solution)/shard_map/ppermute | solution.py:34
  131.0 1.3 collective-permute-start.27
  (8 other events, 12.6 us)

commit v2 on v1

v2 whole, which is shorter than its diff:
```python
import math

import jax
import jax.numpy as jnp
from jax import lax
from jax.experimental import pallas as pl
from jax.experimental.pallas import tpu as pltpu
from jax.sharding import Mesh, PartitionSpec as P

SENSORS = 512
TLEN = 256
GROUPS = 4
DSTEP = 64
HALO = 512
TILE = 2048
EXT = TILE + TLEN
FINE = 8
COARSE = TLEN // FINE
NX, NZ, NY = 4, 8, 4
SUB = 16
DEPTH = FINE * NY * SUB
ROWS = 2 * COARSE
HALF = NX * ROWS
TIME_TILE = 768
VMEM_LIMIT = 12 * 1024 * 1024

PLANE = ("zh", "x", "bank")
ZAXES = ("zh", "bank")
BLOCKS = ("zh", "x", "core", "bank")


def shift(value, axis, steps):
    count = lax.axis_size(axis)
    return lax.ppermute(value, axis, [(i, (i + steps) % count) for i in range(count)])


def plane_index(x, z):
    return ((z // 2) * NX + x) * 2 + z % 2


def turn_kernel(*refs):
    inputs, out_ref, turned_ref = refs[:NY], refs[NY], refs[NY + 1]
    rows = [ref[r].astype(jnp.float32) for r in range(2) for ref in inputs]
    turned_ref[...] = jnp.concatenate(rows, 0).T
    for pair in range(FINE // 2):
        even = turned_ref[pl.ds(2 * pair, COARSE, stride=FINE), :].astype(jnp.bfloat16)
        odd = turned_ref[pl.ds(2 * pair + 1, COARSE, stride=FINE), :].astype(jnp.bfloat16)
        for r in range(2):
            lanes = slice(64 * r, 64 * r + 64)
            out_ref[COARSE * r : COARSE * (r + 1), 128 * pair : 128 * (pair + 1)] = jnp.concatenate(
                [even[:, lanes], odd[:, lanes]], 1
            )


def turn(parts):
    return pl.pallas_call(
        turn_kernel,
        out_shape=jax.ShapeDtypeStruct((ROWS, DEPTH), jnp.bfloat16),
        scratch_shapes=[pltpu.VMEM((TLEN, 128), jnp.float32)],
        compiler_params=pltpu.CompilerParams(vmem_limit_bytes=VMEM_LIMIT),
        name="turn",
    )(*parts)


def join_kernel(x_ref, *refs):
    inputs, out_ref, wide_ref = refs[:NX], refs[NX], refs[NX + 1]
    for d, ref in enumerate(inputs):
        kk = lax.rem(x_ref[0] + NX - d, NX)
        for r in range(2):
            block = ref[COARSE * r : COARSE * (r + 1), :].astype(jnp.float32)
            for i in range(DEPTH // 128):
                rows = pl.ds(NX * r + kk, COARSE, stride=2 * NX)
                wide_ref[i, rows, :] = block[:, 128 * i : 128 * (i + 1)]
    for i in range(DEPTH // 128):
        out_ref[:, 128 * i : 128 * (i + 1)] = wide_ref[i].astype(jnp.bfloat16)


def join(x, parts):
    return pl.pallas_call(
        join_kernel,
        grid_spec=pltpu.PrefetchScalarGridSpec(
            num_scalar_prefetch=1,
            grid=(1,),
            in_specs=[pl.BlockSpec((ROWS, DEPTH), lambda n, i: (0, 0))] * NX,
            out_specs=pl.BlockSpec((HALF, DEPTH), lambda n, i: (0, 0)),
            scratch_shapes=[pltpu.VMEM((DEPTH // 128, HALF, 128), jnp.float32)],
        ),
        out_shape=jax.ShapeDtypeStruct((HALF, DEPTH), jnp.bfloat16),
        compiler_params=pltpu.CompilerParams(vmem_limit_bytes=VMEM_LIMIT),
        name="join",
    )(x[None], *parts)


def spread_kernel(*refs):
    near, low, high, x2_ref, energy_ref = refs[:3], refs[3], refs[4], refs[5], refs[6]

    def section(sub, power, far, base):
        rows = pl.ds(pl.multiple_of(sub * SUB, SUB), SUB)
        far_rows = pl.ds(pl.multiple_of((sub - base) * SUB, SUB), SUB)
        blocks = [near[0][rows, :], near[1][rows, :], far[far_rows, :], near[2][rows, :]]
        block = jnp.concatenate([part.astype(jnp.float32) for part in blocks], 0)
        for e in range(FINE):
            moved = pltpu.roll(block, EXT - e, 1) if e else block
            x2_ref[sub, 64 * e : 64 * (e + 1), :] = moved.astype(jnp.bfloat16)
        return power + jnp.sum((block * block).reshape(NY * SUB // 8, 8, EXT), 0)

    total = jnp.zeros((8, EXT), jnp.float32)
    total = lax.fori_loop(0, NZ // 2, lambda i, c: section(i, c, low, 0), total)
    total = lax.fori_loop(NZ // 2, NZ, lambda i, c: section(i, c, high, NZ // 2), total)
    width = 1
    while width < TLEN:
        total = total + pltpu.roll(total, EXT - width, 1)
        width *= 2
    energy_ref[...] = jnp.sum(total, 0, keepdims=True)[:, :TILE]


def spread(sensors):
    return pl.pallas_call(
        spread_kernel,
        out_shape=[
            pltpu.VMEM((NZ, DEPTH, EXT), jnp.bfloat16),
            jax.ShapeDtypeStruct((1, TILE), jnp.float32),
        ],
        compiler_params=pltpu.CompilerParams(vmem_limit_bytes=VMEM_LIMIT),
        cost_estimate=pl.CostEstimate(flops=2**24, bytes_accessed=24 * 2**20, transcendentals=0),
        name="spread",
    )(*sensors)


def square_sums(refs):
    total = None
    for ref in refs:
        wide = ref[...].astype(jnp.float32)
        wide = wide * wide
        for i in range(0, DEPTH, 128):
            part = wide[:, i : i + 128]
            total = part if total is None else total + part
    return jnp.sum(total.reshape(COARSE, 8, 128), 0)


def fold(y_ref, half):
    split = COARSE // 2
    parts = []
    for j in range(split):
        near, far = 8 * j, 8 * (j + split)
        parts.append(y_ref[half, near : near + 8, : EXT - 128] + y_ref[half, far : far + 8, 128:])
    width = FINE
    while len(parts) > 1:
        parts = [
            parts[i] + pltpu.roll(parts[i + 1], EXT - 128 - width, 1)
            for i in range(0, len(parts), 2)
        ]
        width *= 2
    return parts[0][:, :TILE]


def correlate_kernel(count, places, seeded, closing, index_ref, *refs):
    refs = list(refs)
    take = lambda n: [refs.pop(0) for _ in range(n)]
    lefts = [take(count), take(count)]
    x2_ref = take(1)[0]
    before = take(2) if seeded else None
    energy_ref = take(1)[0] if closing else None
    outs = take(1 if closing else 2)
    y_ref = take(1)[0]
    sums, norms = [], []
    for half in range(2):
        for t in range(0, EXT, TIME_TILE):
            total = None
            for ref, place in zip(lefts[half], places):
                right = x2_ref[index_ref[place], :, t : t + TIME_TILE]
                term = jnp.dot(ref[...], right, preferred_element_type=jnp.float32)
                total = term if total is None else total + term
            y_ref[half, :, t : t + TIME_TILE] = total
        rows = slice(8 * half, 8 * half + 8)
        sums.append(fold(y_ref, half))
        norms.append(square_sums(lefts[half]))
        if seeded:
            sums[half] = sums[half] + before[0][rows, :]
            norms[half] = norms[half] + before[1][rows, :]
        if not closing:
            outs[0][rows, :] = sums[half]
            outs[1][rows, :] = norms[half]
    if not closing:
        return
    scale = math.sqrt(SENSORS * TLEN)
    level = energy_ref[...] + 1e-05
    for half in range(2):
        squares = jnp.sum(norms[half], 1, keepdims=True)
        sums[half] = sums[half] * scale * lax.rsqrt(squares * level)
    first = index_ref[NZ] == 0
    low = jnp.where(first, sums[0], sums[1])
    high = jnp.where(first, sums[1], sums[0])
    for r in range(2):
        outs[0][r, :NX, :] = low[NX * r : NX * (r + 1)]
        outs[0][r, NX:, :] = high[NX * r : NX * (r + 1)]


def correlate(index, places, own, other, x2, before=None, energy=None):
    count = len(own)
    seeded, closing = before is not None, energy is not None
    extra = (list(before) if seeded else []) + ([energy] if closing else [])
    operands = [*own, *other, x2, *extra]
    if closing:
        out_shape = jax.ShapeDtypeStruct((2, 8, TILE), jnp.float32)
    else:
        out_shape = [
            jax.ShapeDtypeStruct((16, TILE), jnp.float32),
            jax.ShapeDtypeStruct((16, 128), jnp.float32),
        ]
    return pl.pallas_call(
        lambda *refs: correlate_kernel(count, list(places), seeded, closing, *refs),
        in_specs=[pl.BlockSpec(memory_space=pltpu.SMEM)]
        + [pl.BlockSpec(memory_space=pltpu.VMEM)] * len(operands),
        scratch_shapes=[pltpu.VMEM((2, HALF, EXT), jnp.float32)],
        out_shape=out_shape,
        compiler_params=pltpu.CompilerParams(vmem_limit_bytes=VMEM_LIMIT),
        cost_estimate=pl.CostEstimate(
            flops=2 * 2 * HALF * DEPTH * count * EXT,
            bytes_accessed=count * 3 * 2**20,
            transcendentals=0,
        ),
        name="correlate",
    )(index, *operands)


def local(record, templates, block_ids, sensor_group):
    zh, x, core = lax.axis_index("zh"), lax.axis_index("x"), lax.axis_index("core")
    y, bank = lax.axis_index("chan"), lax.axis_index("bank")
    z = zh * 2 + bank

    owner_chip = plane_index((block_ids >> 2) & 3, (block_ids >> 4) * 2 + (block_ids & 1))
    owner_core = (block_ids >> 1) & 1
    my_chip = plane_index(x, z)
    halves = templates.reshape(NY, 2, NX, 4, 2, SUB, TLEN).transpose(1, 3, 2, 4, 0, 5, 6)
    halves = halves.reshape(2, 32, NY * SUB, TLEN)
    given = lax.dynamic_index_in_dim(halves, 1 - core, 0, keepdims=False)
    received = shift(given, "core", 1)
    mine = lax.dynamic_index_in_dim(halves, core, 0, keepdims=False)

    leading = record[:, :HALO]
    following = lax.ppermute(leading, BLOCKS, [(i, i - 1) for i in range(1, 64)])

    extended = jnp.concatenate([record, following], 1)
    delayed = jnp.zeros((128, EXT), jnp.bfloat16)
    for group_id in range(GROUPS):
        moved = extended[:, DSTEP * group_id : DSTEP * group_id + EXT]
        delayed = jnp.where((sensor_group == group_id)[:, None], moved, delayed)
    first_core = jnp.where(owner_chip[0] == my_chip, owner_core[0], owner_core[1])
    block = jnp.where(first_core == core, mine, received)
    delayed, block = lax.optimization_barrier((delayed, block))
    above, below = shift(delayed, "chan", 1), shift(delayed, "chan", -1)
    above, below = lax.optimization_barrier((above, below))
    low, high = shift(above[:64], "chan", 1), shift(below[64:], "chan", -1)
    got = lax.all_to_all(block, PLANE, 0, 0, tiled=True)
    clash = (owner_chip[0] == owner_chip[1]) & (owner_core[0] != owner_core[1])

    def second():
        block = jnp.where(owner_core[1] == core, mine, received)
        return lax.all_to_all(block, PLANE, 0, 0, tiled=True)[owner_chip[1]]

    spare = lax.cond(clash, second, lambda: jnp.zeros(mine.shape[1:], mine.dtype))
    piece = jnp.stack([got[owner_chip[0]], jnp.where(clash, spare, got[owner_chip[1]])])

    piece, low, high = lax.optimization_barrier((piece, low, high))
    x2, energy = spread([delayed, above, below, low, high])
    piece = piece.reshape(2, NY, SUB, TLEN)
    parts = [lax.dynamic_index_in_dim(piece, y, 1, keepdims=False)]
    for d in (1, 2, 3):
        part = lax.dynamic_index_in_dim(piece, (y + d) % NY, 1, keepdims=False)
        parts.append(shift(part, "chan", d))
    parts, x2, energy = lax.optimization_barrier((parts, x2, energy))
    piece = turn(parts)

    column = join(x, [piece] + [shift(piece, "x", d) for d in (1, 2, 3)])
    offsets = jnp.array([0, 1, -1, 2, -2, 3, -3, 4], jnp.int32)
    index = jnp.concatenate([(z - offsets) % NZ, core[None]]).astype(jnp.int32)
    arrived, ahead, behind, sums = [column], column, column, None
    for i in range(4):
        if i < 3:
            nearer, farther = shift(ahead, ZAXES, 1), shift(behind, ZAXES, -1)
        else:
            nearer = shift(ahead[: HALF // 2], ZAXES, 1)
            farther = shift(behind[HALF // 2 :], ZAXES, -1)
        other = [shift(block, "core", 1) for block in arrived]
        places = range(max(0, 2 * i - 1), 2 * i + 1)
        sums = correlate(index, places, arrived, other, x2, sums)
        ahead, behind, sums = lax.optimization_barrier((nearer, farther, sums))
        arrived = [ahead, behind]
    last = jnp.concatenate([ahead, behind], 0)
    return correlate(index, [7], [last], [shift(last, "core", 1)], x2, sums, energy)


def solution(mesh):
    fine = Mesh(mesh.devices.reshape(4, NX, 2, NY, 2), ("zh", "x", "core", "chan", "bank"))
    return jax.shard_map(
        local,
        mesh=fine,
        in_specs=(P("chan", BLOCKS), P(BLOCKS, "chan", None), P(), P("chan")),
        out_specs=P(None, "chan", BLOCKS),
        check_vma=False,
    )
```

time: 138 us -> 123 us (0.89); the launches traced: 139 us -> 121 us
  Pallas kernels: 43.1 us -> 22 us
  waiting for transfers between devices: 28 us -> 33.9 us
    pallas_call x6, Pallas kernels: 39.7 us -> 21.6 us  [the longest x5 16.1 us: correlate(): pl.pallas_call(lambda *refs: correlate_kernel(count, list(places), seeded...]
    all_to_all x1, waiting for transfers between devices: 0.01 us -> 6.28 us  [local(): got = lax.all_to_all(block, PLANE, 0, 0, tiled=True)]
    ppermute x27, starting transfers between devices: 36.4 us -> 33.1 us  [shift(): lax.ppermute(value, axis, [(i, (i + steps) % count) for i in range(count)])]
    ppermute x1, starting transfers between devices: 1.91 us -> 4.92 us  [local(): lax.ppermute(leading, BLOCKS, [(i, i - 1) for i in range(1, 64)])]
    unnamed x23 -> x10, local copies, waits for them, and re-layouts: 2.24 us -> 0.1 us
    pallas_call x1, Pallas kernels: 1.82 us -> 0.16 us  [join(): pl.pallas_call(join_kernel, grid_spec=pltpu.PrefetchScalarGridSpec(num_sc...]
    slice x0 -> x2, local copies, waits for them, and re-layouts: none -> 1.47 us  [local(): low, high = (shift(above[:64], 'chan', 1), shift(below[64:], 'chan', -1))]
    pallas_call x1, Pallas kernels: 1.62 us -> 0.21 us  [turn(): pl.pallas_call(turn_kernel, out_shape=jax.ShapeDtypeStruct((ROWS, DEPTH),...]
  transfers between devices with their start and end apart: 29 -> 29, of which waited for: 10 -> 11; matrix products, arithmetic and copies ran while one was open for 1% -> 5% of each run, Pallas kernels for 24% -> 15%
where the time goes in v2:
time: 123 us; the launch traced here: 121 us
  starting transfers between devices  48.2 us (39%)
  waiting for transfers between devices  33.9 us (28%)
  Pallas kernels  22 us (18%)
  between operations  7.86 us (6%)
  local copies, waits for them, and re-layouts  6.81 us (6%)
  other arithmetic  2.07 us (2%)
    ppermute x27, starting transfers between devices, shift(): lax.ppermute(value, axis, [(i, (i + steps) % count) for i in range(count)])  33.1 us
    ppermute x27, waiting for transfers between devices, shift(): lax.ppermute(value, axis, [(i, (i + steps) % count) for i in range(count)])  27.7 us
    pallas_call x5, Pallas kernels, correlate(): pl.pallas_call(lambda *refs: correlate_kernel(count, list(places), seeded...  16.1 us
    all_to_all x1, starting transfers between devices, local(): got = lax.all_to_all(block, PLANE, 0, 0, tiled=True)  10.1 us
    all_to_all x1, waiting for transfers between devices, local(): got = lax.all_to_all(block, PLANE, 0, 0, tiled=True)  6.28 us
    pallas_call x1, Pallas kernels, spread(): pl.pallas_call(spread_kernel, out_shape=[pltpu.VMEM((NZ, DEPTH, EXT), jnp...  5.5 us
    ppermute x1, starting transfers between devices, local(): lax.ppermute(leading, BLOCKS, [(i, i - 1) for i in range(1, 64)])  4.92 us
  transfers between devices with their start and end apart: 29, of which 11 were waited for; matrix products, arithmetic and copies ran while one was open for 5% of the time, Pallas kernels for 15%

profile of v2, /device:TPU:1, one launch (start us, length us, event | category | flops | bytes accessed | tf_op | source)
XLA Modules:
  0.0 120.8 jit_solution(449032828374181928)
XLA Ops:
  0.0 1.6 %slice.50 = bf16[128,512]{1,0:T(8,128)(2,1)} slice(bf16[128,2048]{1,0:T(8,128)(2,1)} %param.7), slice={[0:128], [0:512]} | slice | bytes 262144 | tf_op jit(solution)/shard_map/slice | solution.py:241
  1.6 4.9 %collective-permute-start = (bf16[128,512]{1,0:T(8,128)(2,1)}, bf16[128,512]{1,0:T(8,128)(2,1)S(1)}, u32[]{:S(2)}, u32[]{:S(2)}) collective-permute-start(bf16[128,512]{1,0:T(8,128)(2,1)} %slice.50), channel_id=1, source_target_pairs={{1,0},{8,1},{9,8},{16,9},{17,16},{24,17},{25,24},{32,25},{33,32},{... | collective-permute-start | bytes 393224 | tf_op jit(solution)/shard_map/ppermute | solution.py:242
  6.5 1.9 %copy.6 = bf16[2,4,4,2,4,16,256]{6,5,4,3,2,1,0:T(8,128)(2,1)S(1)} copy(bf16[2,4,4,2,4,16,256]{6,5,3,1,2,0,4:T(8,128)(2,1)} %bitcast.44) | data formatting | bytes 4194304 | tf_op jit(solution)/shard_map/transpose | solution.py:235
  15.0 1.5 %broadcast_select_fusion.1 = (bf16[32,64,256]{2,1,0:T(8,128)(2,1)}, bf16[32,64,256]{2,1,0:T(8,128)(2,1)}) fusion(bf16[32,64,256]{2,1,0:T(8,128)(2,1)} %collective-permute-done.1, pred[]{:T(512)S(6)} %eq.54, bf16[2,32,64,256]{3,2,1,0:T(8,128)(2,1)S(1)} %bitcast.43, s32[]{:T(128)S(6)} %select_n.118), kind=kLoop, calls=%fused_computation.4 | loop fusion | flops 524288 | bytes 4194309 | tf_op jit(solution)/shard_map/jit(_where)/select_n | solution.py:250
  16.5 10.1 %all-to-all-start.1 = ((bf16[32,64,256]{2,1,0:T(8,128)(2,1)}), bf16[32,64,256]{2,1,0:T(8,128)(2,1)S(1)}, u32[]{:S(2)}, u32[]{:S(2)}) async-start(bf16[32,64,256]{2,1,0:T(8,128)(2,1)} %get-tuple-element.62), calls=%async_computation.1 | async-start | bytes 2097152 | tf_op jit(solution)/shard_map/all_to_all | solution.py:255
  26.6 2.8 %collective-permute-start.3 = (bf16[128,2304]{1,0:T(8,128)(2,1)S(1)}, bf16[128,2304]{1,0:T(8,128)(2,1)S(1)}, u32[]{:S(2)}, u32[]{:S(2)}) collective-permute-start(bf16[128,2304]{1,0:T(8,128)(2,1)S(1)} %fusion.2.refs_0_), channel_id=1, source_target_pairs={{0,6},{2,0},{4,2},{6,4},{1,7},{3,1},{5,3},{7,5},{8,14},{10,8},{12,... | collective-permute-start | bytes 1769480 | tf_op jit(solution)/shard_map/ppermute | solution.py:34
  32.8 7.3 %collective-permute-done.3.refs_2_ = bf16[128,2304]{1,0:T(8,128)(2,1)S(1)} collective-permute-done((bf16[128,2304]{1,0:T(8,128)(2,1)S(1)}, bf16[128,2304]{1,0:T(8,128)(2,1)S(1)}, u32[]{:S(2)}, u32[]{:S(2)}) %collective-permute-start.3) | collective-permute-done | bytes 589856 | tf_op jit(solution)/shard_map/ppermute | solution.py:34
  40.1 3.1 %collective-permute-done.2.refs_1_ = bf16[128,2304]{1,0:T(8,128)(2,1)S(1)} collective-permute-done((bf16[128,2304]{1,0:T(8,128)(2,1)S(1)}, bf16[128,2304]{1,0:T(8,128)(2,1)S(1)}, u32[]{:S(2)}, u32[]{:S(2)}) %collective-permute-start.2) | collective-permute-done | bytes 589856 | tf_op jit(solution)/shard_map/ppermute | solution.py:34
  46.2 6.3 %all-to-all-done.1 = bf16[32,64,256]{2,1,0:T(8,128)(2,1)S(1)} async-done(((bf16[32,64,256]{2,1,0:T(8,128)(2,1)}), bf16[32,64,256]{2,1,0:T(8,128)(2,1)S(1)}, u32[]{:S(2)}, u32[]{:S(2)}) %all-to-all-start.1) | async-done | bytes 1048608 | tf_op jit(solution)/shard_map/all_to_all | solution.py:255
  52.5 2.8 %collective-permute-start.8 = (bf16[2,16,256]{2,1,0:T(8,128)(2,1)S(1)}, bf16[2,16,256]{2,1,0:T(8,128)(2,1)S(1)}, u32[]{:S(2)}, u32[]{:S(2)}) collective-permute-start(bf16[2,16,256]{2,1,0:T(8,128)(2,1)S(1)} %get-tuple-element.103), channel_id=1, source_target_pairs={{0,6},{2,0},{4,2},{6,4},{1,7},{3,1},{5,3},{7,5},{8,14},{10,8},{12,... | collective-permute-start | bytes 49160 | tf_op jit(solution)/shard_map/ppermute | solution.py:34
  56.4 5.5 %spread.1 = (bf16[8,512,2304]{2,1,0:T(8,128)(2,1)S(1)}, f32[1,2048]{1,0:T(1,128)S(1)}) custom-call(bf16[128,2304]{1,0:T(8,128)(2,1)S(1)} %fusion.2.refs_0_, bf16[128,2304]{1,0:T(8,128)(2,1)S(1)} %collective-permute-done.2.refs_1_, bf16[128,2304]{1,0:T(8,128)(2,1)S(1)} %collective-permute-done.3.refs_2_, bf16[64,2304]{1,0:T(8,128)(2,1)S(1)} %collective-permute-done.4.refs_3_, ...), custom_call_target="tpu_custom_call" | custom-call | flops 16777216 | bytes 25165824 | tf_op jit(solution)/shard_map/spread/pallas_call | solution.py:118
  63.3 1.9 %collective-permute-start.10 = (bf16[64,512]{1,0:T(8,128)(2,1)S(1)}, bf16[64,512]{1,0:T(8,128)(2,1)S(1)}, u32[]{:S(2)}, u32[]{:S(2)}) collective-permute-start(bf16[64,512]{1,0:T(8,128)(2,1)S(1)} %turn.1.refs_0_), channel_id=1, source_target_pairs={{0,32},{16,48},{32,0},{48,16},{1,33},{17,49},{33,1},{49,17},{2,34}... | collective-permute-start | bytes 196616 | tf_op jit(solution)/shard_map/ppermute | solution.py:34
  66.0 1.9 %collective-permute-done.10.refs_2_ = bf16[64,512]{1,0:T(8,128)(2,1)S(1)} collective-permute-done((bf16[64,512]{1,0:T(8,128)(2,1)S(1)}, bf16[64,512]{1,0:T(8,128)(2,1)S(1)}, u32[]{:S(2)}, u32[]{:S(2)}) %collective-permute-start.10) | collective-permute-done | bytes 65568 | tf_op jit(solution)/shard_map/ppermute | solution.py:34
  67.9 1.6 %collective-permute-done.9.refs_1_ = bf16[64,512]{1,0:T(8,128)(2,1)S(1)} collective-permute-done((bf16[64,512]{1,0:T(8,128)(2,1)S(1)}, bf16[64,512]{1,0:T(8,128)(2,1)S(1)}, u32[]{:S(2)}, u32[]{:S(2)}) %collective-permute-start.9) | collective-permute-done | bytes 65568 | tf_op jit(solution)/shard_map/ppermute | solution.py:34
  69.7 5.8 %collective-permute-start.14 = (bf16[256,512]{1,0:T(8,128)(2,1)S(1)}, bf16[256,512]{1,0:T(8,128)(2,1)S(1)}, u32[]{:S(2)}, u32[]{:S(2)}) collective-permute-start(bf16[256,512]{1,0:T(8,128)(2,1)S(1)} %join.1.refs_1_), channel_id=1, source_target_pairs={{0,8},{8,0},{1,9},{9,1},{2,10},{10,2},{3,11},{11,3},{4,12},{12,4},... | collective-permute-start | bytes 786440 | tf_op jit(solution)/shard_map/ppermute | solution.py:34
  75.6 1.3 %collective-permute-start.13 = (bf16[256,512]{1,0:T(8,128)(2,1)S(1)}, bf16[256,512]{1,0:T(8,128)(2,1)S(1)}, u32[]{:S(2)}, u32[]{:S(2)}) collective-permute-start(bf16[256,512]{1,0:T(8,128)(2,1)S(1)} %join.1.refs_1_), channel_id=1, source_target_pairs={{0,193},{1,0},{64,1},{65,64},{128,65},{129,128},{192,129},{193,192... | collective-permute-start | bytes 786440 | tf_op jit(solution)/shard_map/ppermute | solution.py:34
  77.1 2.3 %correlate.5 = (f32[16,2048]{1,0:T(8,128)S(1)}, f32[16,128]{1,0:T(8,128)S(1)}) custom-call(s32[9]{0:T(128)S(1)} %pad_add_fusion.refs_0_, bf16[256,512]{1,0:T(8,128)(2,1)S(1)} %join.1.refs_1_, bf16[256,512]{1,0:T(8,128)(2,1)S(1)} %collective-permute-done.14.refs_2_, bf16[8,512,2304]{2,1,0:T(8,128)(2,1)S(1)} %get-tuple-element.75.refs_3_.refs_5_), custom_call_target="tpu_custom_call" | custom-call | flops 1207959552 | bytes 3145728 | tf_op jit(solution)/shard_map/correlate/pallas_call | solution.py:211
  79.4 4.0 %collective-permute-done.13.refs_2_ = bf16[256,512]{1,0:T(8,128)(2,1)S(1)} collective-permute-done((bf16[256,512]{1,0:T(8,128)(2,1)S(1)}, bf16[256,512]{1,0:T(8,128)(2,1)S(1)}, u32[]{:S(2)}, u32[]{:S(2)}) %collective-permute-start.13) | collective-permute-done | bytes 262176 | tf_op jit(solution)/shard_map/ppermute | solution.py:34
  83.4 2.2 %collective-permute-done.12.refs_1_ = bf16[256,512]{1,0:T(8,128)(2,1)S(1)} collective-permute-done((bf16[256,512]{1,0:T(8,128)(2,1)S(1)}, bf16[256,512]{1,0:T(8,128)(2,1)S(1)}, u32[]{:S(2)}, u32[]{:S(2)}) %collective-permute-start.12) | collective-permute-done | bytes 262176 | tf_op jit(solution)/shard_map/ppermute | solution.py:34
  86.8 2.7 %collective-permute-start.16 = (bf16[256,512]{1,0:T(8,128)(2,1)S(1)}, bf16[256,512]{1,0:T(8,128)(2,1)S(1)}, u32[]{:S(2)}, u32[]{:S(2)}) collective-permute-start(bf16[256,512]{1,0:T(8,128)(2,1)S(1)} %collective-permute-done.13.refs_2_), channel_id=1, source_target_pairs={{0,193},{1,0},{64,1},{65,64},{128,65},{129,128},{192,129},{193,192... | collective-permute-start | bytes 786440 | tf_op jit(solution)/shard_map/ppermute | solution.py:34
  89.5 3.6 %correlate.6 = (f32[16,2048]{1,0:T(8,128)S(1)}, f32[16,128]{1,0:T(8,128)S(1)}) custom-call(s32[9]{0:T(128)S(1)} %pad_add_fusion.refs_0_, bf16[256,512]{1,0:T(8,128)(2,1)S(1)} %collective-permute-done.12.refs_1_, bf16[256,512]{1,0:T(8,128)(2,1)S(1)} %collective-permute-done.13.refs_2_, bf16[256,512]{1,0:T(8,128)(2,1)S(1)} %collective-permute-done.17.refs_3_, ...), custom_call_target="tpu_custom_call" | custom-call | flops 2415919104 | bytes 6291456 | tf_op jit(solution)/shard_map/correlate/pallas_call | solution.py:211
  93.1 2.3 %collective-permute-done.15.refs_1_ = bf16[256,512]{1,0:T(8,128)(2,1)S(1)} collective-permute-done((bf16[256,512]{1,0:T(8,128)(2,1)S(1)}, bf16[256,512]{1,0:T(8,128)(2,1)S(1)}, u32[]{:S(2)}, u32[]{:S(2)}) %collective-permute-start.15) | collective-permute-done | bytes 262176 | tf_op jit(solution)/shard_map/ppermute | solution.py:34
  95.4 1.4 %collective-permute-start.21 = (bf16[256,512]{1,0:T(8,128)(2,1)S(1)}, bf16[256,512]{1,0:T(8,128)(2,1)S(1)}, u32[]{:S(2)}, u32[]{:S(2)}) collective-permute-start(bf16[256,512]{1,0:T(8,128)(2,1)S(1)} %collective-permute-done.15.refs_1_), channel_id=1, source_target_pairs={{0,8},{8,0},{1,9},{9,1},{2,10},{10,2},{3,11},{11,3},{4,12},{12,4},... | collective-permute-start | bytes 786440 | tf_op jit(solution)/shard_map/ppermute | solution.py:34
  96.7 2.7 %collective-permute-start.20 = (bf16[256,512]{1,0:T(8,128)(2,1)S(1)}, bf16[256,512]{1,0:T(8,128)(2,1)S(1)}, u32[]{:S(2)}, u32[]{:S(2)}) collective-permute-start(bf16[256,512]{1,0:T(8,128)(2,1)S(1)} %collective-permute-done.16.refs_2_), channel_id=1, source_target_pairs={{0,193},{1,0},{64,1},{65,64},{128,65},{129,128},{192,129},{193,192... | collective-permute-start | bytes 786440 | tf_op jit(solution)/shard_map/ppermute | solution.py:34
  99.4 3.6 %correlate.7 = (f32[16,2048]{1,0:T(8,128)S(1)}, f32[16,128]{1,0:T(8,128)S(1)}) custom-call(s32[9]{0:T(128)S(1)} %pad_add_fusion.refs_0_, bf16[256,512]{1,0:T(8,128)(2,1)S(1)} %collective-permute-done.15.refs_1_, bf16[256,512]{1,0:T(8,128)(2,1)S(1)} %collective-permute-done.16.refs_2_, bf16[256,512]{1,0:T(8,128)(2,1)S(1)} %collective-permute-done.21.refs_3_, ...), custom_call_target="tpu_custom_call" | custom-call | flops 2415919104 | bytes 6291456 | tf_op jit(solution)/shard_map/correlate/pallas_call | solution.py:211
  103.1 2.3 %collective-permute-done.19.refs_1_ = bf16[256,512]{1,0:T(8,128)(2,1)S(1)} collective-permute-done((bf16[256,512]{1,0:T(8,128)(2,1)S(1)}, bf16[256,512]{1,0:T(8,128)(2,1)S(1)}, u32[]{:S(2)}, u32[]{:S(2)}) %collective-permute-start.19) | collective-permute-done | bytes 262176 | tf_op jit(solution)/shard_map/ppermute | solution.py:34
  105.3 1.4 %collective-permute-start.25 = (bf16[256,512]{1,0:T(8,128)(2,1)S(1)}, bf16[256,512]{1,0:T(8,128)(2,1)S(1)}, u32[]{:S(2)}, u32[]{:S(2)}) collective-permute-start(bf16[256,512]{1,0:T(8,128)(2,1)S(1)} %collective-permute-done.19.refs_1_), channel_id=1, source_target_pairs={{0,8},{8,0},{1,9},{9,1},{2,10},{10,2},{3,11},{11,3},{4,12},{12,4},... | collective-permute-start | bytes 786440 | tf_op jit(solution)/shard_map/ppermute | solution.py:34
  106.7 2.7 %collective-permute-start.24 = (bf16[128,512]{1,0:T(8,128)(2,1)S(1)}, bf16[128,512]{1,0:T(8,128)(2,1)S(1)}, u32[]{:S(2)}, u32[]{:S(2)}) collective-permute-start(bf16[128,512]{1,0:T(8,128)(2,1)S(1)} %slice.62), channel_id=1, source_target_pairs={{0,193},{1,0},{64,1},{65,64},{128,65},{129,128},{192,129},{193,192... | collective-permute-start | bytes 393224 | tf_op jit(solution)/shard_map/ppermute | solution.py:34
  109.5 3.6 %correlate.8 = (f32[16,2048]{1,0:T(8,128)S(1)}, f32[16,128]{1,0:T(8,128)S(1)}) custom-call(s32[9]{0:T(128)S(1)} %pad_add_fusion.refs_0_, bf16[256,512]{1,0:T(8,128)(2,1)S(1)} %collective-permute-done.19.refs_1_, bf16[256,512]{1,0:T(8,128)(2,1)S(1)} %collective-permute-done.20.refs_2_, bf16[256,512]{1,0:T(8,128)(2,1)S(1)} %collective-permute-done.25.refs_3_, ...), custom_call_target="tpu_custom_call" | custom-call | flops 2415919104 | bytes 6291456 | tf_op jit(solution)/shard_map/correlate/pallas_call | solution.py:211
  113.1 1.8 %collective-permute-done.23 = bf16[128,512]{1,0:T(8,128)(2,1)S(1)} collective-permute-done((bf16[128,512]{1,0:T(8,128)(2,1)S(1)}, bf16[128,512]{1,0:T(8,128)(2,1)S(1)}, u32[]{:S(2)}, u32[]{:S(2)}) %collective-permute-start.23) | collective-permute-done | bytes 131104 | tf_op jit(solution)/shard_map/ppermute | solution.py:34
  114.9 1.8 %collective-permute-start.27 = (bf16[256,512]{1,0:T(8,128)(2,1)S(1)}, bf16[256,512]{1,0:T(8,128)(2,1)S(1)}, u32[]{:S(2)}, u32[]{:S(2)}) collective-permute-start(bf16[256,512]{1,0:T(8,128)(2,1)S(1)} %constant_dynamic-update-slice_fusion.2.refs_1_), channel_id=1, source_target_pairs={{0,8},{8,0},{1,9},{9,1},{2,10},{10,2},{3,11},{11,3},{4,12},{12,4},... | collective-permute-start | bytes 786440 | tf_op jit(solution)/shard_map/ppermute | solution.py:34
  117.9 2.9 %correlate.9 = f32[2,8,2048]{2,1,0:T(8,128)} custom-call(s32[9]{0:T(128)S(1)} %pad_add_fusion.refs_0_, bf16[256,512]{1,0:T(8,128)(2,1)S(1)} %constant_dynamic-update-slice_fusion.2.refs_1_, bf16[256,512]{1,0:T(8,128)(2,1)S(1)} %collective-permute-done.27.refs_2_, bf16[8,512,2304]{2,1,0:T(8,128)(2,1)S(1)} %get-tuple-element.75.refs_3_.refs_5_, ...), custom_call_target="tpu_custom_call" | custom-call | flops 1207959552 | bytes 3145728 | tf_op jit(solution)/shard_map/correlate/pallas_call | solution.py:211
  (66 shorter events, 11.4 us)
Async XLA Ops:
  1.6 12.9 %collective-permute-start = (bf16[128,512]{1,0:T(8,128)(2,1)}, bf16[128,512]{1,0:T(8,128)(2,1)S(1)}, u32[]{:S(2)}, u32[]{:S(2)}) collective-permute-start(bf16[128,512]{1,0:T(8,128)(2,1)} %slice.50), channel_id=1, source_target_pairs={{1,0},{8,1},{9,8},{16,9},{17,16},{24,17},{25,24},{32,25},{33,32},{... | collective-permute-start | bytes 393224 | tf_op jit(solution)/shard_map/ppermute | solution.py:242
  8.4 1.2 copy-start.2
  8.4 6.0 %copy-start.1 = (s32[128]{0:T(128)S(1)}, s32[128]{0:T(128)}, u32[]{:S(2)}) copy-start(s32[128]{0:T(128)} %param.10) | copy-start | bytes 1540
  9.5 5.5 %collective-permute-start.1 = (bf16[32,64,256]{2,1,0:T(8,128)(2,1)}, bf16[32,64,256]{2,1,0:T(8,128)(2,1)}, u32[]{:S(2)}, u32[]{:S(2)}) collective-permute-start(bf16[32,64,256]{2,1,0:T(8,128)(2,1)} %dynamic-slice_bitcast_fusion.1), channel_id=1, source_target_pairs={{0,8},{8,0},{1,9},{9,1},{2,10},{10,2},{3,11},{11,3},{4,12},{12,4},... | collective-permute-start | bytes 3145736 | tf_op jit(solution)/shard_map/ppermute | solution.py:34
  16.5 36.0 %all-to-all-start.1 = ((bf16[32,64,256]{2,1,0:T(8,128)(2,1)}), bf16[32,64,256]{2,1,0:T(8,128)(2,1)S(1)}, u32[]{:S(2)}, u32[]{:S(2)}) async-start(bf16[32,64,256]{2,1,0:T(8,128)(2,1)} %get-tuple-element.62), calls=%async_computation.1 | async-start | bytes 2097152 | tf_op jit(solution)/shard_map/all_to_all | solution.py:255
  26.6 13.5 %collective-permute-start.3 = (bf16[128,2304]{1,0:T(8,128)(2,1)S(1)}, bf16[128,2304]{1,0:T(8,128)(2,1)S(1)}, u32[]{:S(2)}, u32[]{:S(2)}) collective-permute-start(bf16[128,2304]{1,0:T(8,128)(2,1)S(1)} %fusion.2.refs_0_), channel_id=1, source_target_pairs={{0,6},{2,0},{4,2},{6,4},{1,7},{3,1},{5,3},{7,5},{8,14},{10,8},{12,... | collective-permute-start | bytes 1769480 | tf_op jit(solution)/shard_map/ppermute | solution.py:34
  29.4 13.8 %collective-permute-start.2 = (bf16[128,2304]{1,0:T(8,128)(2,1)S(1)}, bf16[128,2304]{1,0:T(8,128)(2,1)S(1)}, u32[]{:S(2)}, u32[]{:S(2)}) collective-permute-start(bf16[128,2304]{1,0:T(8,128)(2,1)S(1)} %fusion.2.refs_0_), channel_id=1, source_target_pairs={{0,2},{2,4},{4,6},{6,0},{1,3},{3,5},{5,7},{7,1},{8,10},{10,12},{12... | collective-permute-start | bytes 1769480 | tf_op jit(solution)/shard_map/ppermute | solution.py:34
  43.9 33.1 %copy-start.3 = (s32[8]{0:T(128)S(1)}, s32[8]{0:T(128)}, u32[]{:S(2)}) copy-start(s32[8]{0:T(128)} %constant.134) | copy-start | bytes 100
  44.7 7.8 %collective-permute-start.5 = (bf16[64,2304]{1,0:T(8,128)(2,1)}, bf16[64,2304]{1,0:T(8,128)(2,1)S(1)}, u32[]{:S(2)}, u32[]{:S(2)}) collective-permute-start(bf16[64,2304]{1,0:T(8,128)(2,1)} %slice.60), channel_id=1, source_target_pairs={{0,6},{2,0},{4,2},{6,4},{1,7},{3,1},{5,3},{7,5},{8,14},{10,8},{12,... | collective-permute-start | bytes 884744 | tf_op jit(solution)/shard_map/ppermute | solution.py:34
  45.0 7.5 %collective-permute-start.4 = (bf16[64,2304]{1,0:T(8,128)(2,1)}, bf16[64,2304]{1,0:T(8,128)(2,1)S(1)}, u32[]{:S(2)}, u32[]{:S(2)}) collective-permute-start(bf16[64,2304]{1,0:T(8,128)(2,1)} %slice.59), channel_id=1, source_target_pairs={{0,2},{2,4},{4,6},{6,0},{1,3},{3,5},{5,7},{7,1},{8,10},{10,12},{12... | collective-permute-start | bytes 884744 | tf_op jit(solution)/shard_map/ppermute | solution.py:34
  52.5 9.4 %collective-permute-start.8 = (bf16[2,16,256]{2,1,0:T(8,128)(2,1)S(1)}, bf16[2,16,256]{2,1,0:T(8,128)(2,1)S(1)}, u32[]{:S(2)}, u32[]{:S(2)}) collective-permute-start(bf16[2,16,256]{2,1,0:T(8,128)(2,1)S(1)} %get-tuple-element.103), channel_id=1, source_target_pairs={{0,6},{2,0},{4,2},{6,4},{1,7},{3,1},{5,3},{7,5},{8,14},{10,8},{12,... | collective-permute-start | bytes 49160 | tf_op jit(solution)/shard_map/ppermute | solution.py:34
  55.3 6.6 %collective-permute-start.7 = (bf16[2,16,256]{2,1,0:T(8,128)(2,1)S(1)}, bf16[2,16,256]{2,1,0:T(8,128)(2,1)S(1)}, u32[]{:S(2)}, u32[]{:S(2)}) collective-permute-start(bf16[2,16,256]{2,1,0:T(8,128)(2,1)S(1)} %get-tuple-element.104), channel_id=1, source_target_pairs={{0,4},{2,6},{4,0},{6,2},{1,5},{3,7},{5,1},{7,3},{8,12},{10,14},{12... | collective-permute-start | bytes 49160 | tf_op jit(solution)/shard_map/ppermute | solution.py:34
  55.7 6.2 %collective-permute-start.6 = (bf16[2,16,256]{2,1,0:T(8,128)(2,1)S(1)}, bf16[2,16,256]{2,1,0:T(8,128)(2,1)S(1)}, u32[]{:S(2)}, u32[]{:S(2)}) collective-permute-start(bf16[2,16,256]{2,1,0:T(8,128)(2,1)S(1)} %get-tuple-element.105), channel_id=1, source_target_pairs={{0,2},{2,4},{4,6},{6,0},{1,3},{3,5},{5,7},{7,1},{8,10},{10,12},{12... | collective-permute-start | bytes 49160 | tf_op jit(solution)/shard_map/ppermute | solution.py:34
  62.1 3.9 %collective-permute-start.11 = (bf16[64,512]{1,0:T(8,128)(2,1)S(1)}, bf16[64,512]{1,0:T(8,128)(2,1)S(1)}, u32[]{:S(2)}, u32[]{:S(2)}) collective-permute-start(bf16[64,512]{1,0:T(8,128)(2,1)S(1)} %turn.1.refs_0_), channel_id=1, source_target_pairs={{0,48},{16,0},{32,16},{48,32},{1,49},{17,1},{33,17},{49,33},{2,50}... | collective-permute-start | bytes 196616 | tf_op jit(solution)/shard_map/ppermute | solution.py:34
  63.3 4.6 %collective-permute-start.10 = (bf16[64,512]{1,0:T(8,128)(2,1)S(1)}, bf16[64,512]{1,0:T(8,128)(2,1)S(1)}, u32[]{:S(2)}, u32[]{:S(2)}) collective-permute-start(bf16[64,512]{1,0:T(8,128)(2,1)S(1)} %turn.1.refs_0_), channel_id=1, source_target_pairs={{0,32},{16,48},{32,0},{48,16},{1,33},{17,49},{33,1},{49,17},{2,34}... | collective-permute-start | bytes 196616 | tf_op jit(solution)/shard_map/ppermute | solution.py:34
  65.2 4.3 %collective-permute-start.9 = (bf16[64,512]{1,0:T(8,128)(2,1)S(1)}, bf16[64,512]{1,0:T(8,128)(2,1)S(1)}, u32[]{:S(2)}, u32[]{:S(2)}) collective-permute-start(bf16[64,512]{1,0:T(8,128)(2,1)S(1)} %turn.1.refs_0_), channel_id=1, source_target_pairs={{0,16},{16,32},{32,48},{48,0},{1,17},{17,33},{33,49},{49,1},{2,18}... | collective-permute-start | bytes 196616 | tf_op jit(solution)/shard_map/ppermute | solution.py:34
  69.7 7.4 %collective-permute-start.14 = (bf16[256,512]{1,0:T(8,128)(2,1)S(1)}, bf16[256,512]{1,0:T(8,128)(2,1)S(1)}, u32[]{:S(2)}, u32[]{:S(2)}) collective-permute-start(bf16[256,512]{1,0:T(8,128)(2,1)S(1)} %join.1.refs_1_), channel_id=1, source_target_pairs={{0,8},{8,0},{1,9},{9,1},{2,10},{10,2},{3,11},{11,3},{4,12},{12,4},... | collective-permute-start | bytes 786440 | tf_op jit(solution)/shard_map/ppermute | solution.py:34
  75.6 7.9 %collective-permute-start.13 = (bf16[256,512]{1,0:T(8,128)(2,1)S(1)}, bf16[256,512]{1,0:T(8,128)(2,1)S(1)}, u32[]{:S(2)}, u32[]{:S(2)}) collective-permute-start(bf16[256,512]{1,0:T(8,128)(2,1)S(1)} %join.1.refs_1_), channel_id=1, source_target_pairs={{0,193},{1,0},{64,1},{65,64},{128,65},{129,128},{192,129},{193,192... | collective-permute-start | bytes 786440 | tf_op jit(solution)/shard_map/ppermute | solution.py:34
  76.9 8.7 %collective-permute-start.12 = (bf16[256,512]{1,0:T(8,128)(2,1)S(1)}, bf16[256,512]{1,0:T(8,128)(2,1)S(1)}, u32[]{:S(2)}, u32[]{:S(2)}) collective-permute-start(bf16[256,512]{1,0:T(8,128)(2,1)S(1)} %join.1.refs_1_), channel_id=1, source_target_pairs={{0,1},{1,64},{64,65},{65,128},{128,129},{129,192},{192,193},{193,0... | collective-permute-start | bytes 786440 | tf_op jit(solution)/shard_map/ppermute | solution.py:34
  85.6 3.9 %collective-permute-start.17 = (bf16[256,512]{1,0:T(8,128)(2,1)S(1)}, bf16[256,512]{1,0:T(8,128)(2,1)S(1)}, u32[]{:S(2)}, u32[]{:S(2)}) collective-permute-start(bf16[256,512]{1,0:T(8,128)(2,1)S(1)} %collective-permute-done.12.refs_1_), channel_id=1, source_target_pairs={{0,8},{8,0},{1,9},{9,1},{2,10},{10,2},{3,11},{11,3},{4,12},{12,4},... | collective-permute-start | bytes 786440 | tf_op jit(solution)/shard_map/ppermute | solution.py:34
  86.8 2.7 %collective-permute-start.18 = (bf16[256,512]{1,0:T(8,128)(2,1)S(1)}, bf16[256,512]{1,0:T(8,128)(2,1)S(1)}, u32[]{:S(2)}, u32[]{:S(2)}) collective-permute-start(bf16[256,512]{1,0:T(8,128)(2,1)S(1)} %collective-permute-done.13.refs_2_), channel_id=1, source_target_pairs={{0,8},{8,0},{1,9},{9,1},{2,10},{10,2},{3,11},{11,3},{4,12},{12,4},... | collective-permute-start | bytes 786440 | tf_op jit(solution)/shard_map/ppermute | solution.py:34
  86.8 8.6 %collective-permute-start.15 = (bf16[256,512]{1,0:T(8,128)(2,1)S(1)}, bf16[256,512]{1,0:T(8,128)(2,1)S(1)}, u32[]{:S(2)}, u32[]{:S(2)}) collective-permute-start(bf16[256,512]{1,0:T(8,128)(2,1)S(1)} %collective-permute-done.12.refs_1_), channel_id=1, source_target_pairs={{0,1},{1,64},{64,65},{65,128},{128,129},{129,192},{192,193},{193,0... | collective-permute-start | bytes 786440 | tf_op jit(solution)/shard_map/ppermute | solution.py:34
  86.8 8.6 %collective-permute-start.16 = (bf16[256,512]{1,0:T(8,128)(2,1)S(1)}, bf16[256,512]{1,0:T(8,128)(2,1)S(1)}, u32[]{:S(2)}, u32[]{:S(2)}) collective-permute-start(bf16[256,512]{1,0:T(8,128)(2,1)S(1)} %collective-permute-done.13.refs_2_), channel_id=1, source_target_pairs={{0,193},{1,0},{64,1},{65,64},{128,65},{129,128},{192,129},{193,192... | collective-permute-start | bytes 786440 | tf_op jit(solution)/shard_map/ppermute | solution.py:34
  95.4 4.0 %collective-permute-start.21 = (bf16[256,512]{1,0:T(8,128)(2,1)S(1)}, bf16[256,512]{1,0:T(8,128)(2,1)S(1)}, u32[]{:S(2)}, u32[]{:S(2)}) collective-permute-start(bf16[256,512]{1,0:T(8,128)(2,1)S(1)} %collective-permute-done.15.refs_1_), channel_id=1, source_target_pairs={{0,8},{8,0},{1,9},{9,1},{2,10},{10,2},{3,11},{11,3},{4,12},{12,4},... | collective-permute-start | bytes 786440 | tf_op jit(solution)/shard_map/ppermute | solution.py:34
  96.7 2.7 %collective-permute-start.22 = (bf16[256,512]{1,0:T(8,128)(2,1)S(1)}, bf16[256,512]{1,0:T(8,128)(2,1)S(1)}, u32[]{:S(2)}, u32[]{:S(2)}) collective-permute-start(bf16[256,512]{1,0:T(8,128)(2,1)S(1)} %collective-permute-done.16.refs_2_), channel_id=1, source_target_pairs={{0,8},{8,0},{1,9},{9,1},{2,10},{10,2},{3,11},{11,3},{4,12},{12,4},... | collective-permute-start | bytes 786440 | tf_op jit(solution)/shard_map/ppermute | solution.py:34
  96.7 8.6 %collective-permute-start.19 = (bf16[256,512]{1,0:T(8,128)(2,1)S(1)}, bf16[256,512]{1,0:T(8,128)(2,1)S(1)}, u32[]{:S(2)}, u32[]{:S(2)}) collective-permute-start(bf16[256,512]{1,0:T(8,128)(2,1)S(1)} %collective-permute-done.15.refs_1_), channel_id=1, source_target_pairs={{0,1},{1,64},{64,65},{65,128},{128,129},{129,192},{192,193},{193,0... | collective-permute-start | bytes 786440 | tf_op jit(solution)/shard_map/ppermute | solution.py:34
  96.7 8.6 %collective-permute-start.20 = (bf16[256,512]{1,0:T(8,128)(2,1)S(1)}, bf16[256,512]{1,0:T(8,128)(2,1)S(1)}, u32[]{:S(2)}, u32[]{:S(2)}) collective-permute-start(bf16[256,512]{1,0:T(8,128)(2,1)S(1)} %collective-permute-done.16.refs_2_), channel_id=1, source_target_pairs={{0,193},{1,0},{64,1},{65,64},{128,65},{129,128},{192,129},{193,192... | collective-permute-start | bytes 786440 | tf_op jit(solution)/shard_map/ppermute | solution.py:34
  105.3 4.2 %collective-permute-start.25 = (bf16[256,512]{1,0:T(8,128)(2,1)S(1)}, bf16[256,512]{1,0:T(8,128)(2,1)S(1)}, u32[]{:S(2)}, u32[]{:S(2)}) collective-permute-start(bf16[256,512]{1,0:T(8,128)(2,1)S(1)} %collective-permute-done.19.refs_1_), channel_id=1, source_target_pairs={{0,8},{8,0},{1,9},{9,1},{2,10},{10,2},{3,11},{11,3},{4,12},{12,4},... | collective-permute-start | bytes 786440 | tf_op jit(solution)/shard_map/ppermute | solution.py:34
  106.7 2.8 %collective-permute-start.26 = (bf16[256,512]{1,0:T(8,128)(2,1)S(1)}, bf16[256,512]{1,0:T(8,128)(2,1)S(1)}, u32[]{:S(2)}, u32[]{:S(2)}) collective-permute-start(bf16[256,512]{1,0:T(8,128)(2,1)S(1)} %collective-permute-done.20.refs_2_), channel_id=1, source_target_pairs={{0,8},{8,0},{1,9},{9,1},{2,10},{10,2},{3,11},{11,3},{4,12},{12,4},... | collective-permute-start | bytes 786440 | tf_op jit(solution)/shard_map/ppermute | solution.py:34
  106.7 6.4 %collective-permute-start.24 = (bf16[128,512]{1,0:T(8,128)(2,1)S(1)}, bf16[128,512]{1,0:T(8,128)(2,1)S(1)}, u32[]{:S(2)}, u32[]{:S(2)}) collective-permute-start(bf16[128,512]{1,0:T(8,128)(2,1)S(1)} %slice.62), channel_id=1, source_target_pairs={{0,193},{1,0},{64,1},{65,64},{128,65},{129,128},{192,129},{193,192... | collective-permute-start | bytes 393224 | tf_op jit(solution)/shard_map/ppermute | solution.py:34
  109.5 5.4 %collective-permute-start.23 = (bf16[128,512]{1,0:T(8,128)(2,1)S(1)}, bf16[128,512]{1,0:T(8,128)(2,1)S(1)}, u32[]{:S(2)}, u32[]{:S(2)}) collective-permute-start(bf16[128,512]{1,0:T(8,128)(2,1)S(1)} %slice.61), channel_id=1, source_target_pairs={{0,1},{1,64},{64,65},{65,128},{128,129},{129,192},{192,193},{193,0... | collective-permute-start | bytes 393224 | tf_op jit(solution)/shard_map/ppermute | solution.py:34
  114.9 2.9 %collective-permute-start.27 = (bf16[256,512]{1,0:T(8,128)(2,1)S(1)}, bf16[256,512]{1,0:T(8,128)(2,1)S(1)}, u32[]{:S(2)}, u32[]{:S(2)}) collective-permute-start(bf16[256,512]{1,0:T(8,128)(2,1)S(1)} %constant_dynamic-update-slice_fusion.2.refs_1_), channel_id=1, source_target_pairs={{0,8},{8,0},{1,9},{9,1},{2,10},{10,2},{3,11},{11,3},{4,12},{12,4},... | collective-permute-start | bytes 786440 | tf_op jit(solution)/shard_map/ppermute | solution.py:34
  (1 other events, 1.1 us)

commit v3 on v2

--- a/solution.py
+++ b/solution.py
@@ -24,7 +24,7 @@
 TIME_TILE = 768
 VMEM_LIMIT = 12 * 1024 * 1024
 
-PLANE = ("zh", "x", "bank")
+PLANE = ("x", "zh", "bank")
 ZAXES = ("zh", "bank")
 BLOCKS = ("zh", "x", "core", "bank")
 
@@ -35,7 +35,34 @@
 
 
 def plane_index(x, z):
-    return ((z // 2) * NX + x) * 2 + z % 2
+    return x * NZ + z
+
+
+def owner_place(ids_ref, r):
+    block = ids_ref[r]
+    chip = plane_index((block >> 2) & 3, (block >> 4) * 2 + (block & 1))
+    return chip, (block >> 1) & 1
+
+
+def plan_kernel(ids_ref, out_ref):
+    places = [owner_place(ids_ref, r) for r in range(2)]
+    clash = jnp.logical_and(places[0][0] == places[1][0], places[0][1] != places[1][1])
+    out_ref[0] = clash.astype(jnp.int32)
+    out_ref[1] = places[0][0]
+    out_ref[2] = places[1][0]
+    out_ref[3] = places[0][1]
+    out_ref[4] = places[1][1]
+
+
+def plan(block_ids):
+    return pl.pallas_call(
+        plan_kernel,
+        in_specs=[pl.BlockSpec(memory_space=pltpu.SMEM)],
+        out_specs=pl.BlockSpec(memory_space=pltpu.SMEM),
+        out_shape=jax.ShapeDtypeStruct((5,), jnp.int32),
+        compiler_params=pltpu.CompilerParams(vmem_limit_bytes=VMEM_LIMIT),
+        name="plan",
+    )(block_ids)
 
 
 def turn_kernel(*refs):
@@ -91,22 +118,26 @@
     )(x[None], *parts)
 
 
-def spread_kernel(*refs):
-    near, low, high, x2_ref, energy_ref = refs[:3], refs[3], refs[4], refs[5], refs[6]
-
-    def section(sub, power, far, base):
-        rows = pl.ds(pl.multiple_of(sub * SUB, SUB), SUB)
-        far_rows = pl.ds(pl.multiple_of((sub - base) * SUB, SUB), SUB)
-        blocks = [near[0][rows, :], near[1][rows, :], far[far_rows, :], near[2][rows, :]]
-        block = jnp.concatenate([part.astype(jnp.float32) for part in blocks], 0)
+def spread_kernel(base, sources, power, x2_ref):
+    def section(sub, power):
+        rows = pl.ds(pl.multiple_of((sub - base) * SUB, SUB), SUB)
+        block = jnp.concatenate([ref[rows, :].astype(jnp.float32) for ref in sources], 0)
         for e in range(FINE):
             moved = pltpu.roll(block, EXT - e, 1) if e else block
             x2_ref[sub, 64 * e : 64 * (e + 1), :] = moved.astype(jnp.bfloat16)
         return power + jnp.sum((block * block).reshape(NY * SUB // 8, 8, EXT), 0)
 
-    total = jnp.zeros((8, EXT), jnp.float32)
-    total = lax.fori_loop(0, NZ // 2, lambda i, c: section(i, c, low, 0), total)
-    total = lax.fori_loop(NZ // 2, NZ, lambda i, c: section(i, c, high, NZ // 2), total)
+    return lax.fori_loop(base, base + NZ // 2, section, power)
+
+
+def spread_low_kernel(*refs):
+    sources, x2_ref, power_ref = refs[:NY], refs[NY], refs[NY + 1]
+    power_ref[...] = spread_kernel(0, sources, jnp.zeros((8, EXT), jnp.float32), x2_ref)
+
+
+def spread_high_kernel(*refs):
+    sources, before_ref, x2_ref, energy_ref = refs[:NY], refs[NY], refs[NY + 2], refs[NY + 3]
+    total = spread_kernel(NZ // 2, sources, before_ref[...], x2_ref)
     width = 1
     while width < TLEN:
         total = total + pltpu.roll(total, EXT - width, 1)
@@ -114,17 +145,18 @@
     energy_ref[...] = jnp.sum(total, 0, keepdims=True)[:, :TILE]
 
 
-def spread(sensors):
-    return pl.pallas_call(
-        spread_kernel,
-        out_shape=[
-            pltpu.VMEM((NZ, DEPTH, EXT), jnp.bfloat16),
-            jax.ShapeDtypeStruct((1, TILE), jnp.float32),
-        ],
-        compiler_params=pltpu.CompilerParams(vmem_limit_bytes=VMEM_LIMIT),
-        cost_estimate=pl.CostEstimate(flops=2**24, bytes_accessed=24 * 2**20, transcendentals=0),
+def spread(sources, before=None):
+    x2 = pltpu.VMEM((NZ, DEPTH, EXT), jnp.bfloat16)
+    power, energy = (8, EXT), (1, TILE)
+    return pl.pallas_call(
+        spread_high_kernel if before else spread_low_kernel,
+        in_specs=[pl.BlockSpec(memory_space=pltpu.VMEM)] * (NY + 2 if before else NY),
+        out_shape=[x2, jax.ShapeDtypeStruct(energy if before else power, jnp.float32)],
+        input_output_aliases={NY + 1: 0} if before else {},
+        compiler_params=pltpu.CompilerParams(vmem_limit_bytes=VMEM_LIMIT),
+        cost_estimate=pl.CostEstimate(flops=2**23, bytes_accessed=12 * 2**20, transcendentals=0),
         name="spread",
-    )(*sensors)
+    )(*sources, *(before or ()))
 
 
 def square_sums(refs):
@@ -229,10 +261,11 @@
     y, bank = lax.axis_index("chan"), lax.axis_index("bank")
     z = zh * 2 + bank
 
-    owner_chip = plane_index((block_ids >> 2) & 3, (block_ids >> 4) * 2 + (block_ids & 1))
-    owner_core = (block_ids >> 1) & 1
+    places = plan(block_ids)
+    clash, chip0, chip1, core0, core1 = [places[i] for i in range(5)]
+    owner_chip, owner_core, clash = (chip0, chip1), (core0, core1), clash != 0
     my_chip = plane_index(x, z)
-    halves = templates.reshape(NY, 2, NX, 4, 2, SUB, TLEN).transpose(1, 3, 2, 4, 0, 5, 6)
+    halves = templates.reshape(NY, 2, NX, NZ, SUB, TLEN).transpose(1, 2, 3, 0, 4, 5)
     halves = halves.reshape(2, 32, NY * SUB, TLEN)
     given = lax.dynamic_index_in_dim(halves, 1 - core, 0, keepdims=False)
     received = shift(given, "core", 1)
@@ -241,19 +274,24 @@
     leading = record[:, :HALO]
     following = lax.ppermute(leading, BLOCKS, [(i, i - 1) for i in range(1, 64)])
 
-    extended = jnp.concatenate([record, following], 1)
-    delayed = jnp.zeros((128, EXT), jnp.bfloat16)
-    for group_id in range(GROUPS):
-        moved = extended[:, DSTEP * group_id : DSTEP * group_id + EXT]
-        delayed = jnp.where((sensor_group == group_id)[:, None], moved, delayed)
+    def moveout(rows):
+        extended = jnp.concatenate([record[rows], following[rows]], 1)
+        group, delayed = sensor_group[rows, None], jnp.zeros((64, EXT), jnp.bfloat16)
+        for group_id in range(GROUPS):
+            moved = extended[:, DSTEP * group_id : DSTEP * group_id + EXT]
+            delayed = jnp.where(group == group_id, moved, delayed)
+        return delayed
+
+    low, high = moveout(slice(0, 64)), moveout(slice(64, 128))
+
     first_core = jnp.where(owner_chip[0] == my_chip, owner_core[0], owner_core[1])
     block = jnp.where(first_core == core, mine, received)
-    delayed, block = lax.optimization_barrier((delayed, block))
-    above, below = shift(delayed, "chan", 1), shift(delayed, "chan", -1)
-    above, below = lax.optimization_barrier((above, below))
-    low, high = shift(above[:64], "chan", 1), shift(below[64:], "chan", -1)
+    low, high, block = lax.optimization_barrier((low, high, block))
+    low_above, high_below = shift(low, "chan", 1), shift(high, "chan", -1)
+    low_below, high_above = shift(low, "chan", -1), shift(high, "chan", 1)
+    low_far, high_far = shift(low_above, "chan", 1), shift(high_below, "chan", -1)
+    lows, highs = [low, low_above, low_far, low_below], [high, high_above, high_far, high_below]
     got = lax.all_to_all(block, PLANE, 0, 0, tiled=True)
-    clash = (owner_chip[0] == owner_chip[1]) & (owner_core[0] != owner_core[1])
 
     def second():
         block = jnp.where(owner_core[1] == core, mine, received)
@@ -262,33 +300,32 @@
     spare = lax.cond(clash, second, lambda: jnp.zeros(mine.shape[1:], mine.dtype))
     piece = jnp.stack([got[owner_chip[0]], jnp.where(clash, spare, got[owner_chip[1]])])
 
-    piece, low, high = lax.optimization_barrier((piece, low, high))
-    x2, energy = spread([delayed, above, below, low, high])
+    piece, lows, highs = lax.optimization_barrier((piece, lows, highs))
+    x2, power = spread(lows)
     piece = piece.reshape(2, NY, SUB, TLEN)
     parts = [lax.dynamic_index_in_dim(piece, y, 1, keepdims=False)]
     for d in (1, 2, 3):
         part = lax.dynamic_index_in_dim(piece, (y + d) % NY, 1, keepdims=False)
         parts.append(shift(part, "chan", d))
-    parts, x2, energy = lax.optimization_barrier((parts, x2, energy))
+    parts, x2, power = lax.optimization_barrier((parts, x2, power))
     piece = turn(parts)
 
-    column = join(x, [piece] + [shift(piece, "x", d) for d in (1, 2, 3)])
+    x2, energy = spread(highs, (power, x2))
+    pieces = [piece] + [shift(piece, "x", d) for d in (1, 2, 3)]
+    pieces, x2, energy = lax.optimization_barrier((pieces, x2, energy))
+    column = join(x, pieces)
     offsets = jnp.array([0, 1, -1, 2, -2, 3, -3, 4], jnp.int32)
     index = jnp.concatenate([(z - offsets) % NZ, core[None]]).astype(jnp.int32)
     arrived, ahead, behind, sums = [column], column, column, None
     for i in range(4):
-        if i < 3:
-            nearer, farther = shift(ahead, ZAXES, 1), shift(behind, ZAXES, -1)
-        else:
-            nearer = shift(ahead[: HALF // 2], ZAXES, 1)
-            farther = shift(behind[HALF // 2 :], ZAXES, -1)
+        nearer = shift(ahead, ZAXES, 1)
+        farther = shift(behind, ZAXES, -1) if i < 3 else behind
         other = [shift(block, "core", 1) for block in arrived]
         places = range(max(0, 2 * i - 1), 2 * i + 1)
         sums = correlate(index, places, arrived, other, x2, sums)
         ahead, behind, sums = lax.optimization_barrier((nearer, farther, sums))
         arrived = [ahead, behind]
-    last = jnp.concatenate([ahead, behind], 0)
-    return correlate(index, [7], [last], [shift(last, "core", 1)], x2, sums, energy)
+    return correlate(index, [7], [ahead], [shift(ahead, "core", 1)], x2, sums, energy)
 
 
 def solution(mesh):

time: 123 us -> 117 us (0.951); the launches traced: 121 us -> 117 us
  local copies, waits for them, and re-layouts: 6.81 us -> 3.7 us
  starting transfers between devices: 48.2 us -> 45.2 us
  other arithmetic: 2.07 us -> 4.1 us
  between operations: 7.86 us -> 6.31 us
    ppermute x27 -> x28, waiting for transfers between devices: 27.7 us -> 18.8 us  [shift(): lax.ppermute(value, axis, [(i, (i + steps) % count) for i in range(count)])]
    all_to_all x1, waiting for transfers between devices: 6.28 us -> 15.1 us  [local(): got = lax.all_to_all(block, PLANE, 0, 0, tiled=True)]
    ppermute x1, starting transfers between devices: 4.92 us -> 1.92 us  [local(): lax.ppermute(leading, BLOCKS, [(i, i - 1) for i in range(1, 64)])]
    slice x1, local copies, waits for them, and re-layouts: 1.57 us -> 0.01 us  [local(): leading = record[:, :HALO]]
    slice x5 -> x3, local copies, waits for them, and re-layouts: 2.14 us -> 0.69 us  [the longest x1 0.65 us: local(): clash, chip0, chip1, core0, core1 = [places[i] for i in range(5)]]
    pallas_call x1 -> x3, Pallas kernels: 5.5 us -> 6.61 us  [the longest x2 5.46 us: spread(): pl.pallas_call(spread_high_kernel if before else spread_low_kernel, in_sp...]
    ppermute x27 -> x28, starting transfers between devices: 33.1 us -> 33.3 us  [shift(): lax.ppermute(value, axis, [(i, (i + steps) % count) for i in range(count)])]
  transfers between devices with their start and end apart: 29 -> 30, of which waited for: 11 -> 14; matrix products, arithmetic and copies ran while one was open for 5% -> 2% of each run, Pallas kernels for 15% -> 17%
where the time goes in v3:
time: 117 us
  starting transfers between devices  45.2 us (39%)
  waiting for transfers between devices  34.5 us (29%)
  Pallas kernels  23 us (20%)
  between operations  6.31 us (5%)
  other arithmetic  4.1 us (4%)
  local copies, waits for them, and re-layouts  3.7 us (3%)
    ppermute x28, starting transfers between devices, shift(): lax.ppermute(value, axis, [(i, (i + steps) % count) for i in range(count)])  33.3 us
    ppermute x28, waiting for transfers between devices, shift(): lax.ppermute(value, axis, [(i, (i + steps) % count) for i in range(count)])  18.8 us
    pallas_call x5, Pallas kernels, correlate(): pl.pallas_call(lambda *refs: correlate_kernel(count, list(places), seeded...  16.1 us
    all_to_all x1, waiting for transfers between devices, local(): got = lax.all_to_all(block, PLANE, 0, 0, tiled=True)  15.1 us
    all_to_all x1, starting transfers between devices, local(): got = lax.all_to_all(block, PLANE, 0, 0, tiled=True)  10 us
    pallas_call x2, Pallas kernels, spread(): pl.pallas_call(spread_high_kernel if before else spread_low_kernel, in_sp...  5.46 us
    select_n x1, other arithmetic, local(): block = jnp.where(first_core == core, mine, received)  2.68 us
  transfers between devices with their start and end apart: 30, of which 14 were waited for; matrix products, arithmetic and copies ran while one was open for 2% of the time, Pallas kernels for 17%

profile of v3, /device:TPU:1, one launch (start us, length us, event | category | flops | bytes accessed | tf_op | source)
XLA Modules:
  0.0 116.9 jit_solution(16027410084730340859)
XLA Ops:
  0.0 1.9 %copy.7 = bf16[2,4,8,4,16,256]{5,4,3,2,1,0:T(8,128)(2,1)S(1)} copy(bf16[2,4,8,4,16,256]{5,4,2,1,0,3:T(8,128)(2,1)} %bitcast.43) | data formatting | bytes 4194304 | tf_op jit(solution)/shard_map/transpose | solution.py:268
  3.0 3.2 %collective-permute-start.1 = (bf16[32,64,256]{2,1,0:T(8,128)(2,1)}, bf16[32,64,256]{2,1,0:T(8,128)(2,1)}, u32[]{:S(2)}, u32[]{:S(2)}) collective-permute-start(bf16[32,64,256]{2,1,0:T(8,128)(2,1)} %dynamic-slice_bitcast_fusion.1), channel_id=1, source_target_pairs={{0,8},{8,0},{1,9},{9,1},{2,10},{10,2},{3,11},{11,3},{4,12},{12,4},... | collective-permute-start | bytes 3145736 | tf_op jit(solution)/shard_map/ppermute | solution.py:34
  6.3 1.9 %collective-permute-start = (bf16[128,512]{1,0:T(8,128)(2,1)S(1)}, bf16[128,512]{1,0:T(8,128)(2,1)S(1)}, u32[]{:S(2)}, u32[]{:S(2)}) collective-permute-start(bf16[128,512]{1,0:T(8,128)(2,1)S(1)} %slice.62), channel_id=1, source_target_pairs={{1,0},{8,1},{9,8},{16,9},{17,16},{24,17},{25,24},{32,25},{33,32},{... | collective-permute-start | bytes 393224 | tf_op jit(solution)/shard_map/ppermute | solution.py:275
  14.5 2.7 %broadcast_select_fusion.1 = (bf16[32,64,256]{2,1,0:T(8,128)(2,1)}, bf16[32,64,256]{2,1,0:T(8,128)(2,1)}) fusion(bf16[32,64,256]{2,1,0:T(8,128)(2,1)} %collective-permute-done.1, pred[]{:T(512)S(6)} %eq.56, bf16[2,32,64,256]{3,2,1,0:T(8,128)(2,1)S(1)} %bitcast.42, s32[]{:T(128)S(6)} %select_n.111), kind=kLoop, calls=%fused_computation.4 | loop fusion | flops 524288 | bytes 4194309 | tf_op jit(solution)/shard_map/jit(_where)/select_n | solution.py:288
  17.2 10.0 %all-to-all-start.1 = ((bf16[32,64,256]{2,1,0:T(8,128)(2,1)}), bf16[32,64,256]{2,1,0:T(8,128)(2,1)S(1)}, u32[]{:S(2)}, u32[]{:S(2)}) async-start(bf16[32,64,256]{2,1,0:T(8,128)(2,1)} %get-tuple-element.74), calls=%async_computation.1 | async-start | bytes 2097152 | tf_op jit(solution)/shard_map/all_to_all | solution.py:294
  27.2 1.4 %collective-permute-start.2 = (bf16[64,2304]{1,0:T(8,128)(2,1)S(1)}, bf16[64,2304]{1,0:T(8,128)(2,1)S(1)}, u32[]{:S(2)}, u32[]{:S(2)}) collective-permute-start(bf16[64,2304]{1,0:T(8,128)(2,1)S(1)} %get-tuple-element.78.refs_0_), channel_id=1, source_target_pairs={{0,2},{2,4},{4,6},{6,0},{1,3},{3,5},{5,7},{7,1},{8,10},{10,12},{12... | collective-permute-start | bytes 884744 | tf_op jit(solution)/shard_map/ppermute | solution.py:34
  28.6 1.5 %collective-permute-start.6 = (bf16[64,2304]{1,0:T(8,128)(2,1)S(1)}, bf16[64,2304]{1,0:T(8,128)(2,1)S(1)}, u32[]{:S(2)}, u32[]{:S(2)}) collective-permute-start(bf16[64,2304]{1,0:T(8,128)(2,1)S(1)} %get-tuple-element.88.refs_0_), channel_id=1, source_target_pairs={{0,6},{2,0},{4,2},{6,4},{1,7},{3,1},{5,3},{7,5},{8,14},{10,8},{12,... | collective-permute-start | bytes 884744 | tf_op jit(solution)/shard_map/ppermute | solution.py:34
  33.7 1.5 %collective-permute-start.4 = (bf16[64,2304]{1,0:T(8,128)(2,1)S(1)}, bf16[64,2304]{1,0:T(8,128)(2,1)S(1)}, u32[]{:S(2)}, u32[]{:S(2)}) collective-permute-start(bf16[64,2304]{1,0:T(8,128)(2,1)S(1)} %get-tuple-element.78.refs_0_), channel_id=1, source_target_pairs={{0,6},{2,0},{4,2},{6,4},{1,7},{3,1},{5,3},{7,5},{8,14},{10,8},{12,... | collective-permute-start | bytes 884744 | tf_op jit(solution)/shard_map/ppermute | solution.py:34
  35.2 1.9 %collective-permute-done.2.refs_1_ = bf16[64,2304]{1,0:T(8,128)(2,1)S(1)} collective-permute-done((bf16[64,2304]{1,0:T(8,128)(2,1)S(1)}, bf16[64,2304]{1,0:T(8,128)(2,1)S(1)}, u32[]{:S(2)}, u32[]{:S(2)}) %collective-permute-start.2) | collective-permute-done | bytes 294944 | tf_op jit(solution)/shard_map/ppermute | solution.py:34
  37.6 2.7 %collective-permute-start.7 = (bf16[64,2304]{1,0:T(8,128)(2,1)S(1)}, bf16[64,2304]{1,0:T(8,128)(2,1)S(1)}, u32[]{:S(2)}, u32[]{:S(2)}) collective-permute-start(bf16[64,2304]{1,0:T(8,128)(2,1)S(1)} %collective-permute-done.6.refs_3_), channel_id=1, source_target_pairs={{0,6},{2,0},{4,2},{6,4},{1,7},{3,1},{5,3},{7,5},{8,14},{10,8},{12,... | collective-permute-start | bytes 884744 | tf_op jit(solution)/shard_map/ppermute | solution.py:34
  40.3 15.1 %all-to-all-done.1 = bf16[32,64,256]{2,1,0:T(8,128)(2,1)S(1)} async-done(((bf16[32,64,256]{2,1,0:T(8,128)(2,1)}), bf16[32,64,256]{2,1,0:T(8,128)(2,1)S(1)}, u32[]{:S(2)}, u32[]{:S(2)}) %all-to-all-start.1) | async-done | bytes 1048608 | tf_op jit(solution)/shard_map/all_to_all | solution.py:294
  55.5 2.8 %collective-permute-start.10 = (bf16[2,16,256]{2,1,0:T(8,128)(2,1)S(1)}, bf16[2,16,256]{2,1,0:T(8,128)(2,1)S(1)}, u32[]{:S(2)}, u32[]{:S(2)}) collective-permute-start(bf16[2,16,256]{2,1,0:T(8,128)(2,1)S(1)} %get-tuple-element.131), channel_id=1, source_target_pairs={{0,6},{2,0},{4,2},{6,4},{1,7},{3,1},{5,3},{7,5},{8,14},{10,8},{12,... | collective-permute-start | bytes 49160 | tf_op jit(solution)/shard_map/ppermute | solution.py:34
  58.4 1.6 %collective-permute-start.9 = (bf16[2,16,256]{2,1,0:T(8,128)(2,1)S(1)}, bf16[2,16,256]{2,1,0:T(8,128)(2,1)S(1)}, u32[]{:S(2)}, u32[]{:S(2)}) collective-permute-start(bf16[2,16,256]{2,1,0:T(8,128)(2,1)S(1)} %get-tuple-element.132), channel_id=1, source_target_pairs={{0,4},{2,6},{4,0},{6,2},{1,5},{3,7},{5,1},{7,3},{8,12},{10,14},{12... | collective-permute-start | bytes 49160 | tf_op jit(solution)/shard_map/ppermute | solution.py:34
  60.0 2.5 %spread.2 = (bf16[8,512,2304]{2,1,0:T(8,128)(2,1)S(1)}, f32[8,2304]{1,0:T(8,128)S(1)}) custom-call(bf16[64,2304]{1,0:T(8,128)(2,1)S(1)} %get-tuple-element.78.refs_0_, bf16[64,2304]{1,0:T(8,128)(2,1)S(1)} %collective-permute-done.2.refs_1_, bf16[64,2304]{1,0:T(8,128)(2,1)S(1)} %collective-permute-done.3.refs_2_, ...), custom_call_target="tpu_custom_call" | custom-call | flops 8388608 | bytes 12582912 | tf_op jit(solution)/shard_map/spread/pallas_call | solution.py:151
  63.2 1.7 %collective-permute-start.12 = (bf16[64,512]{1,0:T(8,128)(2,1)S(1)}, bf16[64,512]{1,0:T(8,128)(2,1)S(1)}, u32[]{:S(2)}, u32[]{:S(2)}) collective-permute-start(bf16[64,512]{1,0:T(8,128)(2,1)S(1)} %turn.1.refs_0_), channel_id=1, source_target_pairs={{0,32},{16,48},{32,0},{48,16},{1,33},{17,49},{33,1},{49,17},{2,34}... | collective-permute-start | bytes 196616 | tf_op jit(solution)/shard_map/ppermute | solution.py:34
  65.8 3.0 %spread.3 = (bf16[8,512,2304]{2,1,0:T(8,128)(2,1)S(1)}, f32[1,2048]{1,0:T(1,128)S(1)}) custom-call(bf16[64,2304]{1,0:T(8,128)(2,1)S(1)} %get-tuple-element.88.refs_0_, bf16[64,2304]{1,0:T(8,128)(2,1)S(1)} %collective-permute-done.5.refs_1_, bf16[64,2304]{1,0:T(8,128)(2,1)S(1)} %collective-permute-done.7.refs_2_, ...), custom_call_target="tpu_custom_call", output_to_operand_aliasing={{0}: (5, {})} | custom-call | flops 8388608 | bytes 12582912 | tf_op jit(solution)/shard_map/spread/pallas_call | solution.py:151
  69.3 1.8 %collective-permute-start.16 = (bf16[256,512]{1,0:T(8,128)(2,1)S(1)}, bf16[256,512]{1,0:T(8,128)(2,1)S(1)}, u32[]{:S(2)}, u32[]{:S(2)}) collective-permute-start(bf16[256,512]{1,0:T(8,128)(2,1)S(1)} %join.1.refs_1_), channel_id=1, source_target_pairs={{0,8},{8,0},{1,9},{9,1},{2,10},{10,2},{3,11},{11,3},{4,12},{12,4},... | collective-permute-start | bytes 786440 | tf_op jit(solution)/shard_map/ppermute | solution.py:34
  71.1 3.1 %collective-permute-start.14 = (bf16[256,512]{1,0:T(8,128)(2,1)S(1)}, bf16[256,512]{1,0:T(8,128)(2,1)S(1)}, u32[]{:S(2)}, u32[]{:S(2)}) collective-permute-start(bf16[256,512]{1,0:T(8,128)(2,1)S(1)} %join.1.refs_1_), channel_id=1, source_target_pairs={{0,1},{1,64},{64,65},{65,128},{128,129},{129,192},{192,193},{193,0... | collective-permute-start | bytes 786440 | tf_op jit(solution)/shard_map/ppermute | solution.py:34
  74.3 2.3 %correlate.5 = (f32[16,2048]{1,0:T(8,128)S(1)}, f32[16,128]{1,0:T(8,128)S(1)}) custom-call(s32[9]{0:T(128)S(1)} %pad_add_fusion.refs_0_, bf16[256,512]{1,0:T(8,128)(2,1)S(1)} %join.1.refs_1_, bf16[256,512]{1,0:T(8,128)(2,1)S(1)} %collective-permute-done.16.refs_2_, bf16[8,512,2304]{2,1,0:T(8,128)(2,1)S(1)} %get-tuple-element.100.refs_3_.refs_5_), custom_call_target="tpu_custom_call" | custom-call | flops 1207959552 | bytes 3145728 | tf_op jit(solution)/shard_map/correlate/pallas_call | solution.py:243
  76.6 4.0 %collective-permute-done.14.refs_1_ = bf16[256,512]{1,0:T(8,128)(2,1)S(1)} collective-permute-done((bf16[256,512]{1,0:T(8,128)(2,1)S(1)}, bf16[256,512]{1,0:T(8,128)(2,1)S(1)}, u32[]{:S(2)}, u32[]{:S(2)}) %collective-permute-start.14) | collective-permute-done | bytes 262176 | tf_op jit(solution)/shard_map/ppermute | solution.py:34
  83.0 2.7 %collective-permute-start.18 = (bf16[256,512]{1,0:T(8,128)(2,1)S(1)}, bf16[256,512]{1,0:T(8,128)(2,1)S(1)}, u32[]{:S(2)}, u32[]{:S(2)}) collective-permute-start(bf16[256,512]{1,0:T(8,128)(2,1)S(1)} %collective-permute-done.15.refs_2_), channel_id=1, source_target_pairs={{0,193},{1,0},{64,1},{65,64},{128,65},{129,128},{192,129},{193,192... | collective-permute-start | bytes 786440 | tf_op jit(solution)/shard_map/ppermute | solution.py:34
  85.7 3.6 %correlate.6 = (f32[16,2048]{1,0:T(8,128)S(1)}, f32[16,128]{1,0:T(8,128)S(1)}) custom-call(s32[9]{0:T(128)S(1)} %pad_add_fusion.refs_0_, bf16[256,512]{1,0:T(8,128)(2,1)S(1)} %collective-permute-done.14.refs_1_, bf16[256,512]{1,0:T(8,128)(2,1)S(1)} %collective-permute-done.15.refs_2_, bf16[256,512]{1,0:T(8,128)(2,1)S(1)} %collective-permute-done.19.refs_3_, ...), custom_call_target="tpu_custom_call" | custom-call | flops 2415919104 | bytes 6291456 | tf_op jit(solution)/shard_map/correlate/pallas_call | solution.py:243
  89.3 2.3 %collective-permute-done.17.refs_1_ = bf16[256,512]{1,0:T(8,128)(2,1)S(1)} collective-permute-done((bf16[256,512]{1,0:T(8,128)(2,1)S(1)}, bf16[256,512]{1,0:T(8,128)(2,1)S(1)}, u32[]{:S(2)}, u32[]{:S(2)}) %collective-permute-start.17) | collective-permute-done | bytes 262176 | tf_op jit(solution)/shard_map/ppermute | solution.py:34
  91.5 1.4 %collective-permute-start.23 = (bf16[256,512]{1,0:T(8,128)(2,1)S(1)}, bf16[256,512]{1,0:T(8,128)(2,1)S(1)}, u32[]{:S(2)}, u32[]{:S(2)}) collective-permute-start(bf16[256,512]{1,0:T(8,128)(2,1)S(1)} %collective-permute-done.17.refs_1_), channel_id=1, source_target_pairs={{0,8},{8,0},{1,9},{9,1},{2,10},{10,2},{3,11},{11,3},{4,12},{12,4},... | collective-permute-start | bytes 786440 | tf_op jit(solution)/shard_map/ppermute | solution.py:34
  92.9 2.7 %collective-permute-start.22 = (bf16[256,512]{1,0:T(8,128)(2,1)S(1)}, bf16[256,512]{1,0:T(8,128)(2,1)S(1)}, u32[]{:S(2)}, u32[]{:S(2)}) collective-permute-start(bf16[256,512]{1,0:T(8,128)(2,1)S(1)} %collective-permute-done.18.refs_2_), channel_id=1, source_target_pairs={{0,193},{1,0},{64,1},{65,64},{128,65},{129,128},{192,129},{193,192... | collective-permute-start | bytes 786440 | tf_op jit(solution)/shard_map/ppermute | solution.py:34
  95.6 3.6 %correlate.7 = (f32[16,2048]{1,0:T(8,128)S(1)}, f32[16,128]{1,0:T(8,128)S(1)}) custom-call(s32[9]{0:T(128)S(1)} %pad_add_fusion.refs_0_, bf16[256,512]{1,0:T(8,128)(2,1)S(1)} %collective-permute-done.17.refs_1_, bf16[256,512]{1,0:T(8,128)(2,1)S(1)} %collective-permute-done.18.refs_2_, bf16[256,512]{1,0:T(8,128)(2,1)S(1)} %collective-permute-done.23.refs_3_, ...), custom_call_target="tpu_custom_call" | custom-call | flops 2415919104 | bytes 6291456 | tf_op jit(solution)/shard_map/correlate/pallas_call | solution.py:243
  99.2 2.3 %collective-permute-done.21.refs_1_ = bf16[256,512]{1,0:T(8,128)(2,1)S(1)} collective-permute-done((bf16[256,512]{1,0:T(8,128)(2,1)S(1)}, bf16[256,512]{1,0:T(8,128)(2,1)S(1)}, u32[]{:S(2)}, u32[]{:S(2)}) %collective-permute-start.21) | collective-permute-done | bytes 262176 | tf_op jit(solution)/shard_map/ppermute | solution.py:34
  101.5 1.4 %collective-permute-start.26 = (bf16[256,512]{1,0:T(8,128)(2,1)S(1)}, bf16[256,512]{1,0:T(8,128)(2,1)S(1)}, u32[]{:S(2)}, u32[]{:S(2)}) collective-permute-start(bf16[256,512]{1,0:T(8,128)(2,1)S(1)} %collective-permute-done.21.refs_1_), channel_id=1, source_target_pairs={{0,8},{8,0},{1,9},{9,1},{2,10},{10,2},{3,11},{11,3},{4,12},{12,4},... | collective-permute-start | bytes 786440 | tf_op jit(solution)/shard_map/ppermute | solution.py:34
  104.4 3.6 %correlate.8 = (f32[16,2048]{1,0:T(8,128)S(1)}, f32[16,128]{1,0:T(8,128)S(1)}) custom-call(s32[9]{0:T(128)S(1)} %pad_add_fusion.refs_0_, bf16[256,512]{1,0:T(8,128)(2,1)S(1)} %collective-permute-done.21.refs_1_, bf16[256,512]{1,0:T(8,128)(2,1)S(1)} %collective-permute-done.22.refs_2_, bf16[256,512]{1,0:T(8,128)(2,1)S(1)} %collective-permute-done.26.refs_3_, ...), custom_call_target="tpu_custom_call" | custom-call | flops 2415919104 | bytes 6291456 | tf_op jit(solution)/shard_map/correlate/pallas_call | solution.py:243
  108.0 3.4 %collective-permute-done.25.refs_1_ = bf16[256,512]{1,0:T(8,128)(2,1)S(1)} collective-permute-done((bf16[256,512]{1,0:T(8,128)(2,1)S(1)}, bf16[256,512]{1,0:T(8,128)(2,1)S(1)}, u32[]{:S(2)}, u32[]{:S(2)}) %collective-permute-start.25) | collective-permute-done | bytes 262176 | tf_op jit(solution)/shard_map/ppermute | solution.py:34
  111.4 1.4 %collective-permute-start.28 = (bf16[256,512]{1,0:T(8,128)(2,1)S(1)}, bf16[256,512]{1,0:T(8,128)(2,1)S(1)}, u32[]{:S(2)}, u32[]{:S(2)}) collective-permute-start(bf16[256,512]{1,0:T(8,128)(2,1)S(1)} %collective-permute-done.25.refs_1_), channel_id=1, source_target_pairs={{0,8},{8,0},{1,9},{9,1},{2,10},{10,2},{3,11},{11,3},{4,12},{12,4},... | collective-permute-start | bytes 786440 | tf_op jit(solution)/shard_map/ppermute | solution.py:34
  113.9 2.9 %correlate.9 = f32[2,8,2048]{2,1,0:T(8,128)} custom-call(s32[9]{0:T(128)S(1)} %pad_add_fusion.refs_0_, bf16[256,512]{1,0:T(8,128)(2,1)S(1)} %collective-permute-done.25.refs_1_, bf16[256,512]{1,0:T(8,128)(2,1)S(1)} %collective-permute-done.28.refs_2_, bf16[8,512,2304]{2,1,0:T(8,128)(2,1)S(1)} %get-tuple-element.100.refs_3_.refs_5_, ...), custom_call_target="tpu_custom_call" | custom-call | flops 1207959552 | bytes 3145728 | tf_op jit(solution)/shard_map/correlate/pallas_call | solution.py:243
  (63 shorter events, 12.6 us)
Async XLA Ops:
  1.9 10.6 %copy-start.2 = (s32[128]{0:T(128)S(1)}, s32[128]{0:T(128)}, u32[]{:S(2)}) copy-start(s32[128]{0:T(128)} %param.10) | copy-start | bytes 1540
  3.0 11.5 %collective-permute-start.1 = (bf16[32,64,256]{2,1,0:T(8,128)(2,1)}, bf16[32,64,256]{2,1,0:T(8,128)(2,1)}, u32[]{:S(2)}, u32[]{:S(2)}) collective-permute-start(bf16[32,64,256]{2,1,0:T(8,128)(2,1)} %dynamic-slice_bitcast_fusion.1), channel_id=1, source_target_pairs={{0,8},{8,0},{1,9},{9,1},{2,10},{10,2},{3,11},{11,3},{4,12},{12,4},... | collective-permute-start | bytes 3145736 | tf_op jit(solution)/shard_map/ppermute | solution.py:34
  6.3 7.0 %collective-permute-start = (bf16[128,512]{1,0:T(8,128)(2,1)S(1)}, bf16[128,512]{1,0:T(8,128)(2,1)S(1)}, u32[]{:S(2)}, u32[]{:S(2)}) collective-permute-start(bf16[128,512]{1,0:T(8,128)(2,1)S(1)} %slice.62), channel_id=1, source_target_pairs={{1,0},{8,1},{9,8},{16,9},{17,16},{24,17},{25,24},{32,25},{33,32},{... | collective-permute-start | bytes 393224 | tf_op jit(solution)/shard_map/ppermute | solution.py:275
  17.2 38.3 %all-to-all-start.1 = ((bf16[32,64,256]{2,1,0:T(8,128)(2,1)}), bf16[32,64,256]{2,1,0:T(8,128)(2,1)S(1)}, u32[]{:S(2)}, u32[]{:S(2)}) async-start(bf16[32,64,256]{2,1,0:T(8,128)(2,1)} %get-tuple-element.74), calls=%async_computation.1 | async-start | bytes 2097152 | tf_op jit(solution)/shard_map/all_to_all | solution.py:294
  27.2 10.0 %collective-permute-start.2 = (bf16[64,2304]{1,0:T(8,128)(2,1)S(1)}, bf16[64,2304]{1,0:T(8,128)(2,1)S(1)}, u32[]{:S(2)}, u32[]{:S(2)}) collective-permute-start(bf16[64,2304]{1,0:T(8,128)(2,1)S(1)} %get-tuple-element.78.refs_0_), channel_id=1, source_target_pairs={{0,2},{2,4},{4,6},{6,0},{1,3},{3,5},{5,7},{7,1},{8,10},{10,12},{12... | collective-permute-start | bytes 884744 | tf_op jit(solution)/shard_map/ppermute | solution.py:34
  28.6 9.0 %collective-permute-start.6 = (bf16[64,2304]{1,0:T(8,128)(2,1)S(1)}, bf16[64,2304]{1,0:T(8,128)(2,1)S(1)}, u32[]{:S(2)}, u32[]{:S(2)}) collective-permute-start(bf16[64,2304]{1,0:T(8,128)(2,1)S(1)} %get-tuple-element.88.refs_0_), channel_id=1, source_target_pairs={{0,6},{2,0},{4,2},{6,4},{1,7},{3,1},{5,3},{7,5},{8,14},{10,8},{12,... | collective-permute-start | bytes 884744 | tf_op jit(solution)/shard_map/ppermute | solution.py:34
  33.7 21.8 %collective-permute-start.4 = (bf16[64,2304]{1,0:T(8,128)(2,1)S(1)}, bf16[64,2304]{1,0:T(8,128)(2,1)S(1)}, u32[]{:S(2)}, u32[]{:S(2)}) collective-permute-start(bf16[64,2304]{1,0:T(8,128)(2,1)S(1)} %get-tuple-element.78.refs_0_), channel_id=1, source_target_pairs={{0,6},{2,0},{4,2},{6,4},{1,7},{3,1},{5,3},{7,5},{8,14},{10,8},{12,... | collective-permute-start | bytes 884744 | tf_op jit(solution)/shard_map/ppermute | solution.py:34
  35.1 20.4 %collective-permute-start.5 = (bf16[64,2304]{1,0:T(8,128)(2,1)S(1)}, bf16[64,2304]{1,0:T(8,128)(2,1)S(1)}, u32[]{:S(2)}, u32[]{:S(2)}) collective-permute-start(bf16[64,2304]{1,0:T(8,128)(2,1)S(1)} %get-tuple-element.88.refs_0_), channel_id=1, source_target_pairs={{0,2},{2,4},{4,6},{6,0},{1,3},{3,5},{5,7},{7,1},{8,10},{10,12},{12... | collective-permute-start | bytes 884744 | tf_op jit(solution)/shard_map/ppermute | solution.py:34
  37.2 18.3 %collective-permute-start.3 = (bf16[64,2304]{1,0:T(8,128)(2,1)S(1)}, bf16[64,2304]{1,0:T(8,128)(2,1)S(1)}, u32[]{:S(2)}, u32[]{:S(2)}) collective-permute-start(bf16[64,2304]{1,0:T(8,128)(2,1)S(1)} %collective-permute-done.2.refs_1_), channel_id=1, source_target_pairs={{0,2},{2,4},{4,6},{6,0},{1,3},{3,5},{5,7},{7,1},{8,10},{10,12},{12... | collective-permute-start | bytes 884744 | tf_op jit(solution)/shard_map/ppermute | solution.py:34
  37.6 17.9 %collective-permute-start.7 = (bf16[64,2304]{1,0:T(8,128)(2,1)S(1)}, bf16[64,2304]{1,0:T(8,128)(2,1)S(1)}, u32[]{:S(2)}, u32[]{:S(2)}) collective-permute-start(bf16[64,2304]{1,0:T(8,128)(2,1)S(1)} %collective-permute-done.6.refs_3_), channel_id=1, source_target_pairs={{0,6},{2,0},{4,2},{6,4},{1,7},{3,1},{5,3},{7,5},{8,14},{10,8},{12,... | collective-permute-start | bytes 884744 | tf_op jit(solution)/shard_map/ppermute | solution.py:34
  55.5 7.0 %collective-permute-start.10 = (bf16[2,16,256]{2,1,0:T(8,128)(2,1)S(1)}, bf16[2,16,256]{2,1,0:T(8,128)(2,1)S(1)}, u32[]{:S(2)}, u32[]{:S(2)}) collective-permute-start(bf16[2,16,256]{2,1,0:T(8,128)(2,1)S(1)} %get-tuple-element.131), channel_id=1, source_target_pairs={{0,6},{2,0},{4,2},{6,4},{1,7},{3,1},{5,3},{7,5},{8,14},{10,8},{12,... | collective-permute-start | bytes 49160 | tf_op jit(solution)/shard_map/ppermute | solution.py:34
  58.4 4.2 %collective-permute-start.8 = (bf16[2,16,256]{2,1,0:T(8,128)(2,1)S(1)}, bf16[2,16,256]{2,1,0:T(8,128)(2,1)S(1)}, u32[]{:S(2)}, u32[]{:S(2)}) collective-permute-start(bf16[2,16,256]{2,1,0:T(8,128)(2,1)S(1)} %get-tuple-element.133), channel_id=1, source_target_pairs={{0,2},{2,4},{4,6},{6,0},{1,3},{3,5},{5,7},{7,1},{8,10},{10,12},{12... | collective-permute-start | bytes 49160 | tf_op jit(solution)/shard_map/ppermute | solution.py:34
  58.4 4.5 %collective-permute-start.9 = (bf16[2,16,256]{2,1,0:T(8,128)(2,1)S(1)}, bf16[2,16,256]{2,1,0:T(8,128)(2,1)S(1)}, u32[]{:S(2)}, u32[]{:S(2)}) collective-permute-start(bf16[2,16,256]{2,1,0:T(8,128)(2,1)S(1)} %get-tuple-element.132), channel_id=1, source_target_pairs={{0,4},{2,6},{4,0},{6,2},{1,5},{3,7},{5,1},{7,3},{8,12},{10,14},{12... | collective-permute-start | bytes 49160 | tf_op jit(solution)/shard_map/ppermute | solution.py:34
  63.0 11.2 %copy-start.3 = (s32[8]{0:T(128)S(1)}, s32[8]{0:T(128)}, u32[]{:S(2)}) copy-start(s32[8]{0:T(128)} %constant.97) | copy-start | bytes 100
  63.1 5.7 %collective-permute-start.11 = (bf16[64,512]{1,0:T(8,128)(2,1)S(1)}, bf16[64,512]{1,0:T(8,128)(2,1)S(1)}, u32[]{:S(2)}, u32[]{:S(2)}) collective-permute-start(bf16[64,512]{1,0:T(8,128)(2,1)S(1)} %turn.1.refs_0_), channel_id=1, source_target_pairs={{0,16},{16,32},{32,48},{48,0},{1,17},{17,33},{33,49},{49,1},{2,18}... | collective-permute-start | bytes 196616 | tf_op jit(solution)/shard_map/ppermute | solution.py:34
  63.2 5.7 %collective-permute-start.12 = (bf16[64,512]{1,0:T(8,128)(2,1)S(1)}, bf16[64,512]{1,0:T(8,128)(2,1)S(1)}, u32[]{:S(2)}, u32[]{:S(2)}) collective-permute-start(bf16[64,512]{1,0:T(8,128)(2,1)S(1)} %turn.1.refs_0_), channel_id=1, source_target_pairs={{0,32},{16,48},{32,0},{48,16},{1,33},{17,49},{33,1},{49,17},{2,34}... | collective-permute-start | bytes 196616 | tf_op jit(solution)/shard_map/ppermute | solution.py:34
  64.9 4.2 %collective-permute-start.13 = (bf16[64,512]{1,0:T(8,128)(2,1)S(1)}, bf16[64,512]{1,0:T(8,128)(2,1)S(1)}, u32[]{:S(2)}, u32[]{:S(2)}) collective-permute-start(bf16[64,512]{1,0:T(8,128)(2,1)S(1)} %turn.1.refs_0_), channel_id=1, source_target_pairs={{0,48},{16,0},{32,16},{48,32},{1,49},{17,1},{33,17},{49,33},{2,50}... | collective-permute-start | bytes 196616 | tf_op jit(solution)/shard_map/ppermute | solution.py:34
  69.3 5.0 %collective-permute-start.16 = (bf16[256,512]{1,0:T(8,128)(2,1)S(1)}, bf16[256,512]{1,0:T(8,128)(2,1)S(1)}, u32[]{:S(2)}, u32[]{:S(2)}) collective-permute-start(bf16[256,512]{1,0:T(8,128)(2,1)S(1)} %join.1.refs_1_), channel_id=1, source_target_pairs={{0,8},{8,0},{1,9},{9,1},{2,10},{10,2},{3,11},{11,3},{4,12},{12,4},... | collective-permute-start | bytes 786440 | tf_op jit(solution)/shard_map/ppermute | solution.py:34
  71.1 9.6 %collective-permute-start.14 = (bf16[256,512]{1,0:T(8,128)(2,1)S(1)}, bf16[256,512]{1,0:T(8,128)(2,1)S(1)}, u32[]{:S(2)}, u32[]{:S(2)}) collective-permute-start(bf16[256,512]{1,0:T(8,128)(2,1)S(1)} %join.1.refs_1_), channel_id=1, source_target_pairs={{0,1},{1,64},{64,65},{65,128},{128,129},{129,192},{192,193},{193,0... | collective-permute-start | bytes 786440 | tf_op jit(solution)/shard_map/ppermute | solution.py:34
  74.2 7.5 %collective-permute-start.15 = (bf16[256,512]{1,0:T(8,128)(2,1)S(1)}, bf16[256,512]{1,0:T(8,128)(2,1)S(1)}, u32[]{:S(2)}, u32[]{:S(2)}) collective-permute-start(bf16[256,512]{1,0:T(8,128)(2,1)S(1)} %join.1.refs_1_), channel_id=1, source_target_pairs={{0,193},{1,0},{64,1},{65,64},{128,65},{129,128},{192,129},{193,192... | collective-permute-start | bytes 786440 | tf_op jit(solution)/shard_map/ppermute | solution.py:34
  81.8 3.9 %collective-permute-start.19 = (bf16[256,512]{1,0:T(8,128)(2,1)S(1)}, bf16[256,512]{1,0:T(8,128)(2,1)S(1)}, u32[]{:S(2)}, u32[]{:S(2)}) collective-permute-start(bf16[256,512]{1,0:T(8,128)(2,1)S(1)} %collective-permute-done.14.refs_1_), channel_id=1, source_target_pairs={{0,8},{8,0},{1,9},{9,1},{2,10},{10,2},{3,11},{11,3},{4,12},{12,4},... | collective-permute-start | bytes 786440 | tf_op jit(solution)/shard_map/ppermute | solution.py:34
  83.0 2.7 %collective-permute-start.20 = (bf16[256,512]{1,0:T(8,128)(2,1)S(1)}, bf16[256,512]{1,0:T(8,128)(2,1)S(1)}, u32[]{:S(2)}, u32[]{:S(2)}) collective-permute-start(bf16[256,512]{1,0:T(8,128)(2,1)S(1)} %collective-permute-done.15.refs_2_), channel_id=1, source_target_pairs={{0,8},{8,0},{1,9},{9,1},{2,10},{10,2},{3,11},{11,3},{4,12},{12,4},... | collective-permute-start | bytes 786440 | tf_op jit(solution)/shard_map/ppermute | solution.py:34
  83.0 8.6 %collective-permute-start.17 = (bf16[256,512]{1,0:T(8,128)(2,1)S(1)}, bf16[256,512]{1,0:T(8,128)(2,1)S(1)}, u32[]{:S(2)}, u32[]{:S(2)}) collective-permute-start(bf16[256,512]{1,0:T(8,128)(2,1)S(1)} %collective-permute-done.14.refs_1_), channel_id=1, source_target_pairs={{0,1},{1,64},{64,65},{65,128},{128,129},{129,192},{192,193},{193,0... | collective-permute-start | bytes 786440 | tf_op jit(solution)/shard_map/ppermute | solution.py:34
  83.0 8.6 %collective-permute-start.18 = (bf16[256,512]{1,0:T(8,128)(2,1)S(1)}, bf16[256,512]{1,0:T(8,128)(2,1)S(1)}, u32[]{:S(2)}, u32[]{:S(2)}) collective-permute-start(bf16[256,512]{1,0:T(8,128)(2,1)S(1)} %collective-permute-done.15.refs_2_), channel_id=1, source_target_pairs={{0,193},{1,0},{64,1},{65,64},{128,65},{129,128},{192,129},{193,192... | collective-permute-start | bytes 786440 | tf_op jit(solution)/shard_map/ppermute | solution.py:34
  91.5 4.0 %collective-permute-start.23 = (bf16[256,512]{1,0:T(8,128)(2,1)S(1)}, bf16[256,512]{1,0:T(8,128)(2,1)S(1)}, u32[]{:S(2)}, u32[]{:S(2)}) collective-permute-start(bf16[256,512]{1,0:T(8,128)(2,1)S(1)} %collective-permute-done.17.refs_1_), channel_id=1, source_target_pairs={{0,8},{8,0},{1,9},{9,1},{2,10},{10,2},{3,11},{11,3},{4,12},{12,4},... | collective-permute-start | bytes 786440 | tf_op jit(solution)/shard_map/ppermute | solution.py:34
  92.9 2.7 %collective-permute-start.24 = (bf16[256,512]{1,0:T(8,128)(2,1)S(1)}, bf16[256,512]{1,0:T(8,128)(2,1)S(1)}, u32[]{:S(2)}, u32[]{:S(2)}) collective-permute-start(bf16[256,512]{1,0:T(8,128)(2,1)S(1)} %collective-permute-done.18.refs_2_), channel_id=1, source_target_pairs={{0,8},{8,0},{1,9},{9,1},{2,10},{10,2},{3,11},{11,3},{4,12},{12,4},... | collective-permute-start | bytes 786440 | tf_op jit(solution)/shard_map/ppermute | solution.py:34
  92.9 8.6 %collective-permute-start.21 = (bf16[256,512]{1,0:T(8,128)(2,1)S(1)}, bf16[256,512]{1,0:T(8,128)(2,1)S(1)}, u32[]{:S(2)}, u32[]{:S(2)}) collective-permute-start(bf16[256,512]{1,0:T(8,128)(2,1)S(1)} %collective-permute-done.17.refs_1_), channel_id=1, source_target_pairs={{0,1},{1,64},{64,65},{65,128},{128,129},{129,192},{192,193},{193,0... | collective-permute-start | bytes 786440 | tf_op jit(solution)/shard_map/ppermute | solution.py:34
  92.9 8.6 %collective-permute-start.22 = (bf16[256,512]{1,0:T(8,128)(2,1)S(1)}, bf16[256,512]{1,0:T(8,128)(2,1)S(1)}, u32[]{:S(2)}, u32[]{:S(2)}) collective-permute-start(bf16[256,512]{1,0:T(8,128)(2,1)S(1)} %collective-permute-done.18.refs_2_), channel_id=1, source_target_pairs={{0,193},{1,0},{64,1},{65,64},{128,65},{129,128},{192,129},{193,192... | collective-permute-start | bytes 786440 | tf_op jit(solution)/shard_map/ppermute | solution.py:34
  101.5 2.5 %collective-permute-start.26 = (bf16[256,512]{1,0:T(8,128)(2,1)S(1)}, bf16[256,512]{1,0:T(8,128)(2,1)S(1)}, u32[]{:S(2)}, u32[]{:S(2)}) collective-permute-start(bf16[256,512]{1,0:T(8,128)(2,1)S(1)} %collective-permute-done.21.refs_1_), channel_id=1, source_target_pairs={{0,8},{8,0},{1,9},{9,1},{2,10},{10,2},{3,11},{11,3},{4,12},{12,4},... | collective-permute-start | bytes 786440 | tf_op jit(solution)/shard_map/ppermute | solution.py:34
  102.8 1.5 %collective-permute-start.27 = (bf16[256,512]{1,0:T(8,128)(2,1)S(1)}, bf16[256,512]{1,0:T(8,128)(2,1)S(1)}, u32[]{:S(2)}, u32[]{:S(2)}) collective-permute-start(bf16[256,512]{1,0:T(8,128)(2,1)S(1)} %collective-permute-done.22.refs_2_), channel_id=1, source_target_pairs={{0,8},{8,0},{1,9},{9,1},{2,10},{10,2},{3,11},{11,3},{4,12},{12,4},... | collective-permute-start | bytes 786440 | tf_op jit(solution)/shard_map/ppermute | solution.py:34
  102.9 8.6 %collective-permute-start.25 = (bf16[256,512]{1,0:T(8,128)(2,1)S(1)}, bf16[256,512]{1,0:T(8,128)(2,1)S(1)}, u32[]{:S(2)}, u32[]{:S(2)}) collective-permute-start(bf16[256,512]{1,0:T(8,128)(2,1)S(1)} %collective-permute-done.21.refs_1_), channel_id=1, source_target_pairs={{0,1},{1,64},{64,65},{65,128},{128,129},{129,192},{192,193},{193,0... | collective-permute-start | bytes 786440 | tf_op jit(solution)/shard_map/ppermute | solution.py:34
  111.4 2.5 %collective-permute-start.28 = (bf16[256,512]{1,0:T(8,128)(2,1)S(1)}, bf16[256,512]{1,0:T(8,128)(2,1)S(1)}, u32[]{:S(2)}, u32[]{:S(2)}) collective-permute-start(bf16[256,512]{1,0:T(8,128)(2,1)S(1)} %collective-permute-done.25.refs_1_), channel_id=1, source_target_pairs={{0,8},{8,0},{1,9},{9,1},{2,10},{10,2},{3,11},{11,3},{4,12},{12,4},... | collective-permute-start | bytes 786440 | tf_op jit(solution)/shard_map/ppermute | solution.py:34
  (2 other events, 10.7 us)

commit v4 on v3

--- a/solution.py
+++ b/solution.py
@@ -34,6 +34,14 @@
     return lax.ppermute(value, axis, [(i, (i + steps) % count) for i in range(count)])
 
 
+def round_z(value, way):
+    place = lambda z, core: z % NZ // 2 * 4 + core * 2 + z % 2
+    pairs = []
+    for z in range(NZ):
+        pairs += [(place(z, 0), place(z + way, 0)), (place(z, 1), place(z - way, 1))]
+    return lax.ppermute(value, ("zh", "core", "bank"), pairs)
+
+
 def plane_index(x, z):
     return x * NZ + z
 
@@ -186,6 +194,11 @@
     return parts[0][:, :TILE]
 
 
+def chip_row(index_ref, place):
+    mirrored = place if place in (0, NZ - 1) else place + (1 if place % 2 else -1)
+    return jnp.where(index_ref[NZ] == 0, index_ref[place], index_ref[mirrored])
+
+
 def correlate_kernel(count, places, seeded, closing, index_ref, *refs):
     refs = list(refs)
     take = lambda n: [refs.pop(0) for _ in range(n)]
@@ -200,7 +213,7 @@
         for t in range(0, EXT, TIME_TILE):
             total = None
             for ref, place in zip(lefts[half], places):
-                right = x2_ref[index_ref[place], :, t : t + TIME_TILE]
+                right = x2_ref[chip_row(index_ref, place), :, t : t + TIME_TILE]
                 term = jnp.dot(ref[...], right, preferred_element_type=jnp.float32)
                 total = term if total is None else total + term
             y_ref[half, :, t : t + TIME_TILE] = total
@@ -318,9 +331,9 @@
     index = jnp.concatenate([(z - offsets) % NZ, core[None]]).astype(jnp.int32)
     arrived, ahead, behind, sums = [column], column, column, None
     for i in range(4):
-        nearer = shift(ahead, ZAXES, 1)
-        farther = shift(behind, ZAXES, -1) if i < 3 else behind
-        other = [shift(block, "core", 1) for block in arrived]
+        nearer = round_z(ahead, 1)
+        farther = round_z(behind, -1) if i < 3 else behind
+        other = [shift(block, "core", 1) for block in arrived[::-1]]
         places = range(max(0, 2 * i - 1), 2 * i + 1)
         sums = correlate(index, places, arrived, other, x2, sums)
         ahead, behind, sums = lax.optimization_barrier((nearer, farther, sums))

time: 117 us -> 115 us (0.983)
  waiting for transfers between devices: 34.5 us -> 33.1 us
  other arithmetic: 4.1 us -> 2.88 us
    ppermute x0 -> x7, waiting for transfers between devices: none -> 16 us  [round_z(): return lax.ppermute(value, ('zh', 'core', 'bank'), pairs)]
    ppermute x28 -> x21, waiting for transfers between devices: 18.8 us -> 2.8 us  [shift(): lax.ppermute(value, axis, [(i, (i + steps) % count) for i in range(count)])]
    ppermute x0 -> x7, starting transfers between devices: none -> 4.6 us  [round_z(): return lax.ppermute(value, ('zh', 'core', 'bank'), pairs)]
    ppermute x28 -> x21, starting transfers between devices: 33.3 us -> 29.5 us  [shift(): lax.ppermute(value, axis, [(i, (i + steps) % count) for i in range(count)])]
    all_to_all x1, waiting for transfers between devices: 15.1 us -> 13.7 us  [local(): got = lax.all_to_all(block, PLANE, 0, 0, tiled=True)]
    select_n x1, other arithmetic: 2.68 us -> 1.46 us  [local(): block = jnp.where(first_core == core, mine, received)]
  transfers between devices with their start and end apart: 30 -> 30, of which waited for: 14 -> 13; matrix products, arithmetic and copies ran while one was open for 2% -> 2% of each run, Pallas kernels for 17% -> 17%
where the time goes in v4:
time: 115 us
  starting transfers between devices  46.1 us (40%)
  waiting for transfers between devices  33.1 us (29%)
  Pallas kernels  23.1 us (20%)
  between operations  6.33 us (6%)
  local copies, waits for them, and re-layouts  3.7 us (3%)
  other arithmetic  2.88 us (3%)
    ppermute x21, starting transfers between devices, shift(): lax.ppermute(value, axis, [(i, (i + steps) % count) for i in range(count)])  29.5 us
    pallas_call x5, Pallas kernels, correlate(): pl.pallas_call(lambda *refs: correlate_kernel(count, list(places), seeded...  16.1 us
    ppermute x7, waiting for transfers between devices, round_z(): return lax.ppermute(value, ('zh', 'core', 'bank'), pairs)  16 us
    all_to_all x1, waiting for transfers between devices, local(): got = lax.all_to_all(block, PLANE, 0, 0, tiled=True)  13.7 us
    all_to_all x1, starting transfers between devices, local(): got = lax.all_to_all(block, PLANE, 0, 0, tiled=True)  10 us
    pallas_call x2, Pallas kernels, spread(): pl.pallas_call(spread_high_kernel if before else spread_low_kernel, in_sp...  5.46 us
    ppermute x7, starting transfers between devices, round_z(): return lax.ppermute(value, ('zh', 'core', 'bank'), pairs)  4.6 us
    ppermute x21, waiting for transfers between devices, shift(): lax.ppermute(value, axis, [(i, (i + steps) % count) for i in range(count)])  2.8 us
  transfers between devices with their start and end apart: 30, of which 13 were waited for; matrix products, arithmetic and copies ran while one was open for 2% of the time, Pallas kernels for 17%

profile of v4, /device:TPU:1, one launch (start us, length us, event | category | flops | bytes accessed | tf_op | source)
XLA Modules:
  0.0 115.1 jit_solution(5607127398313403289)
XLA Ops:
  0.0 1.9 %copy.7 = bf16[2,4,8,4,16,256]{5,4,3,2,1,0:T(8,128)(2,1)S(1)} copy(bf16[2,4,8,4,16,256]{5,4,2,1,0,3:T(8,128)(2,1)} %bitcast.43) | data formatting | bytes 4194304 | tf_op jit(solution)/shard_map/transpose | solution.py:281
  3.0 3.2 %collective-permute-start.1 = (bf16[32,64,256]{2,1,0:T(8,128)(2,1)}, bf16[32,64,256]{2,1,0:T(8,128)(2,1)}, u32[]{:S(2)}, u32[]{:S(2)}) collective-permute-start(bf16[32,64,256]{2,1,0:T(8,128)(2,1)} %dynamic-slice_bitcast_fusion.1), channel_id=1, source_target_pairs={{0,8},{8,0},{1,9},{9,1},{2,10},{10,2},{3,11},{11,3},{4,12},{12,4},... | collective-permute-start | bytes 3145736 | tf_op jit(solution)/shard_map/ppermute | solution.py:34
  6.3 1.9 %collective-permute-start = (bf16[128,512]{1,0:T(8,128)(2,1)S(1)}, bf16[128,512]{1,0:T(8,128)(2,1)S(1)}, u32[]{:S(2)}, u32[]{:S(2)}) collective-permute-start(bf16[128,512]{1,0:T(8,128)(2,1)S(1)} %slice.62), channel_id=1, source_target_pairs={{1,0},{8,1},{9,8},{16,9},{17,16},{24,17},{25,24},{32,25},{33,32},{... | collective-permute-start | bytes 393224 | tf_op jit(solution)/shard_map/ppermute | solution.py:288
  8.2 1.1 plan.1
  13.2 1.2 %fusion.3 = (bf16[64,2304]{1,0:T(8,128)(2,1)S(1)}, bf16[64,2304]{1,0:T(8,128)(2,1)S(1)}) fusion(bf16[64,2048]{1,0:T(8,128)(2,1)S(1)} %get-tuple-element.127, bf16[64,512]{1,0:T(8,128)(2,1)S(1)} %get-tuple-element.129, pred[64]{0:T(512)(128)(4,1)S(1)} %get-tuple-element.141, pred[64]{0:T(512)(128)(4,1)S(1)} %get-tuple-element.140, ...), kind=kLoop, calls=%fused_computation.20 | loop fusion | flops 5898240 | bytes 1245696 | tf_op jit(solution)/shard_map/jit(_where)/select_n | solution.py:295
  14.5 1.5 %broadcast_select_fusion.1 = (bf16[32,64,256]{2,1,0:T(8,128)(2,1)}, bf16[32,64,256]{2,1,0:T(8,128)(2,1)}) fusion(bf16[32,64,256]{2,1,0:T(8,128)(2,1)} %collective-permute-done.1, pred[]{:T(512)S(6)} %eq.56, bf16[2,32,64,256]{3,2,1,0:T(8,128)(2,1)S(1)} %bitcast.42, s32[]{:T(128)S(6)} %select_n.111), kind=kLoop, calls=%fused_computation.4 | loop fusion | flops 524288 | bytes 4194309 | tf_op jit(solution)/shard_map/jit(_where)/select_n | solution.py:301
  16.0 10.0 %all-to-all-start.1 = ((bf16[32,64,256]{2,1,0:T(8,128)(2,1)}), bf16[32,64,256]{2,1,0:T(8,128)(2,1)S(1)}, u32[]{:S(2)}, u32[]{:S(2)}) async-start(bf16[32,64,256]{2,1,0:T(8,128)(2,1)} %get-tuple-element.74), calls=%async_computation.1 | async-start | bytes 2097152 | tf_op jit(solution)/shard_map/all_to_all | solution.py:307
  26.0 1.4 %collective-permute-start.2 = (bf16[64,2304]{1,0:T(8,128)(2,1)S(1)}, bf16[64,2304]{1,0:T(8,128)(2,1)S(1)}, u32[]{:S(2)}, u32[]{:S(2)}) collective-permute-start(bf16[64,2304]{1,0:T(8,128)(2,1)S(1)} %get-tuple-element.78.refs_0_), channel_id=1, source_target_pairs={{0,2},{2,4},{4,6},{6,0},{1,3},{3,5},{5,7},{7,1},{8,10},{10,12},{12... | collective-permute-start | bytes 884744 | tf_op jit(solution)/shard_map/ppermute | solution.py:34
  27.4 1.5 %collective-permute-start.6 = (bf16[64,2304]{1,0:T(8,128)(2,1)S(1)}, bf16[64,2304]{1,0:T(8,128)(2,1)S(1)}, u32[]{:S(2)}, u32[]{:S(2)}) collective-permute-start(bf16[64,2304]{1,0:T(8,128)(2,1)S(1)} %get-tuple-element.88.refs_0_), channel_id=1, source_target_pairs={{0,6},{2,0},{4,2},{6,4},{1,7},{3,1},{5,3},{7,5},{8,14},{10,8},{12,... | collective-permute-start | bytes 884744 | tf_op jit(solution)/shard_map/ppermute | solution.py:34
  32.5 1.5 %collective-permute-start.4 = (bf16[64,2304]{1,0:T(8,128)(2,1)S(1)}, bf16[64,2304]{1,0:T(8,128)(2,1)S(1)}, u32[]{:S(2)}, u32[]{:S(2)}) collective-permute-start(bf16[64,2304]{1,0:T(8,128)(2,1)S(1)} %get-tuple-element.78.refs_0_), channel_id=1, source_target_pairs={{0,6},{2,0},{4,2},{6,4},{1,7},{3,1},{5,3},{7,5},{8,14},{10,8},{12,... | collective-permute-start | bytes 884744 | tf_op jit(solution)/shard_map/ppermute | solution.py:34
  34.3 2.7 %collective-permute-start.7 = (bf16[64,2304]{1,0:T(8,128)(2,1)S(1)}, bf16[64,2304]{1,0:T(8,128)(2,1)S(1)}, u32[]{:S(2)}, u32[]{:S(2)}) collective-permute-start(bf16[64,2304]{1,0:T(8,128)(2,1)S(1)} %collective-permute-done.6.refs_3_), channel_id=1, source_target_pairs={{0,6},{2,0},{4,2},{6,4},{1,7},{3,1},{5,3},{7,5},{8,14},{10,8},{12,... | collective-permute-start | bytes 884744 | tf_op jit(solution)/shard_map/ppermute | solution.py:34
  37.0 13.7 %all-to-all-done.1 = bf16[32,64,256]{2,1,0:T(8,128)(2,1)S(1)} async-done(((bf16[32,64,256]{2,1,0:T(8,128)(2,1)}), bf16[32,64,256]{2,1,0:T(8,128)(2,1)S(1)}, u32[]{:S(2)}, u32[]{:S(2)}) %all-to-all-start.1) | async-done | bytes 1048608 | tf_op jit(solution)/shard_map/all_to_all | solution.py:307
  50.7 2.8 %collective-permute-start.10 = (bf16[2,16,256]{2,1,0:T(8,128)(2,1)S(1)}, bf16[2,16,256]{2,1,0:T(8,128)(2,1)S(1)}, u32[]{:S(2)}, u32[]{:S(2)}) collective-permute-start(bf16[2,16,256]{2,1,0:T(8,128)(2,1)S(1)} %get-tuple-element.131), channel_id=1, source_target_pairs={{0,6},{2,0},{4,2},{6,4},{1,7},{3,1},{5,3},{7,5},{8,14},{10,8},{12,... | collective-permute-start | bytes 49160 | tf_op jit(solution)/shard_map/ppermute | solution.py:34
  53.6 1.6 %collective-permute-start.9 = (bf16[2,16,256]{2,1,0:T(8,128)(2,1)S(1)}, bf16[2,16,256]{2,1,0:T(8,128)(2,1)S(1)}, u32[]{:S(2)}, u32[]{:S(2)}) collective-permute-start(bf16[2,16,256]{2,1,0:T(8,128)(2,1)S(1)} %get-tuple-element.132), channel_id=1, source_target_pairs={{0,4},{2,6},{4,0},{6,2},{1,5},{3,7},{5,1},{7,3},{8,12},{10,14},{12... | collective-permute-start | bytes 49160 | tf_op jit(solution)/shard_map/ppermute | solution.py:34
  55.2 2.5 %spread.2 = (bf16[8,512,2304]{2,1,0:T(8,128)(2,1)S(1)}, f32[8,2304]{1,0:T(8,128)S(1)}) custom-call(bf16[64,2304]{1,0:T(8,128)(2,1)S(1)} %get-tuple-element.78.refs_0_, bf16[64,2304]{1,0:T(8,128)(2,1)S(1)} %collective-permute-done.2.refs_1_, bf16[64,2304]{1,0:T(8,128)(2,1)S(1)} %collective-permute-done.3.refs_2_, ...), custom_call_target="tpu_custom_call" | custom-call | flops 8388608 | bytes 12582912 | tf_op jit(solution)/shard_map/spread/pallas_call | solution.py:159
  58.0 1.8 %collective-permute-start.12 = (bf16[64,512]{1,0:T(8,128)(2,1)S(1)}, bf16[64,512]{1,0:T(8,128)(2,1)S(1)}, u32[]{:S(2)}, u32[]{:S(2)}) collective-permute-start(bf16[64,512]{1,0:T(8,128)(2,1)S(1)} %turn.1.refs_0_), channel_id=1, source_target_pairs={{0,32},{16,48},{32,0},{48,16},{1,33},{17,49},{33,1},{49,17},{2,34}... | collective-permute-start | bytes 196616 | tf_op jit(solution)/shard_map/ppermute | solution.py:34
  60.8 3.0 %spread.3 = (bf16[8,512,2304]{2,1,0:T(8,128)(2,1)S(1)}, f32[1,2048]{1,0:T(1,128)S(1)}) custom-call(bf16[64,2304]{1,0:T(8,128)(2,1)S(1)} %get-tuple-element.88.refs_0_, bf16[64,2304]{1,0:T(8,128)(2,1)S(1)} %collective-permute-done.5.refs_1_, bf16[64,2304]{1,0:T(8,128)(2,1)S(1)} %collective-permute-done.7.refs_2_, ...), custom_call_target="tpu_custom_call", output_to_operand_aliasing={{0}: (5, {})} | custom-call | flops 8388608 | bytes 12582912 | tf_op jit(solution)/shard_map/spread/pallas_call | solution.py:159
  64.0 7.8 %collective-permute-start.16 = (bf16[256,512]{1,0:T(8,128)(2,1)S(1)}, bf16[256,512]{1,0:T(8,128)(2,1)S(1)}, u32[]{:S(2)}, u32[]{:S(2)}) collective-permute-start(bf16[256,512]{1,0:T(8,128)(2,1)S(1)} %join.1.refs_1_), channel_id=1, source_target_pairs={{0,8},{8,0},{1,9},{9,1},{2,10},{10,2},{3,11},{11,3},{4,12},{12,4},... | collective-permute-start | bytes 786440 | tf_op jit(solution)/shard_map/ppermute | solution.py:34
  71.8 1.3 %collective-permute-start.14 = (bf16[256,512]{1,0:T(8,128)(2,1)S(1)}, bf16[256,512]{1,0:T(8,128)(2,1)S(1)}, u32[]{:S(2)}, u32[]{:S(2)}) collective-permute-start(bf16[256,512]{1,0:T(8,128)(2,1)S(1)} %join.1.refs_1_), channel_id=1, source_target_pairs={{0,1},{8,201},{1,64},{9,8},{64,65},{72,9},{65,128},{73,72},{128,12... | collective-permute-start | bytes 786440 | tf_op jit(solution)/shard_map/ppermute | solution.py:42
  73.4 2.3 %correlate.5 = (f32[16,2048]{1,0:T(8,128)S(1)}, f32[16,128]{1,0:T(8,128)S(1)}) custom-call(s32[9]{0:T(128)S(1)} %pad_add_fusion.refs_0_, bf16[256,512]{1,0:T(8,128)(2,1)S(1)} %join.1.refs_1_, bf16[256,512]{1,0:T(8,128)(2,1)S(1)} %collective-permute-done.16.refs_2_, bf16[8,512,2304]{2,1,0:T(8,128)(2,1)S(1)} %get-tuple-element.100.refs_3_.refs_5_), custom_call_target="tpu_custom_call" | custom-call | flops 1207959552 | bytes 3145728 | tf_op jit(solution)/shard_map/correlate/pallas_call | solution.py:256
  75.7 2.1 %collective-permute-done.14.refs_1_ = bf16[256,512]{1,0:T(8,128)(2,1)S(1)} collective-permute-done((bf16[256,512]{1,0:T(8,128)(2,1)S(1)}, bf16[256,512]{1,0:T(8,128)(2,1)S(1)}, u32[]{:S(2)}, u32[]{:S(2)}) %collective-permute-start.14) | collective-permute-done | bytes 262176 | tf_op jit(solution)/shard_map/ppermute | solution.py:42
  77.8 3.8 %collective-permute-done.15.refs_2_ = bf16[256,512]{1,0:T(8,128)(2,1)S(1)} collective-permute-done((bf16[256,512]{1,0:T(8,128)(2,1)S(1)}, bf16[256,512]{1,0:T(8,128)(2,1)S(1)}, u32[]{:S(2)}, u32[]{:S(2)}) %collective-permute-start.15) | collective-permute-done | bytes 262176 | tf_op jit(solution)/shard_map/ppermute | solution.py:42
  83.6 3.6 %correlate.6 = (f32[16,2048]{1,0:T(8,128)S(1)}, f32[16,128]{1,0:T(8,128)S(1)}) custom-call(s32[9]{0:T(128)S(1)} %pad_add_fusion.refs_0_, bf16[256,512]{1,0:T(8,128)(2,1)S(1)} %collective-permute-done.14.refs_1_, bf16[256,512]{1,0:T(8,128)(2,1)S(1)} %collective-permute-done.15.refs_2_, bf16[256,512]{1,0:T(8,128)(2,1)S(1)} %collective-permute-done.19.refs_3_, ...), custom_call_target="tpu_custom_call" | custom-call | flops 2415919104 | bytes 6291456 | tf_op jit(solution)/shard_map/correlate/pallas_call | solution.py:256
  87.2 2.1 %collective-permute-done.17.refs_1_ = bf16[256,512]{1,0:T(8,128)(2,1)S(1)} collective-permute-done((bf16[256,512]{1,0:T(8,128)(2,1)S(1)}, bf16[256,512]{1,0:T(8,128)(2,1)S(1)}, u32[]{:S(2)}, u32[]{:S(2)}) %collective-permute-start.17) | collective-permute-done | bytes 262176 | tf_op jit(solution)/shard_map/ppermute | solution.py:42
  89.3 2.6 %collective-permute-done.18.refs_2_ = bf16[256,512]{1,0:T(8,128)(2,1)S(1)} collective-permute-done((bf16[256,512]{1,0:T(8,128)(2,1)S(1)}, bf16[256,512]{1,0:T(8,128)(2,1)S(1)}, u32[]{:S(2)}, u32[]{:S(2)}) %collective-permute-start.18) | collective-permute-done | bytes 262176 | tf_op jit(solution)/shard_map/ppermute | solution.py:42
  93.8 3.6 %correlate.7 = (f32[16,2048]{1,0:T(8,128)S(1)}, f32[16,128]{1,0:T(8,128)S(1)}) custom-call(s32[9]{0:T(128)S(1)} %pad_add_fusion.refs_0_, bf16[256,512]{1,0:T(8,128)(2,1)S(1)} %collective-permute-done.17.refs_1_, bf16[256,512]{1,0:T(8,128)(2,1)S(1)} %collective-permute-done.18.refs_2_, bf16[256,512]{1,0:T(8,128)(2,1)S(1)} %collective-permute-done.23.refs_3_, ...), custom_call_target="tpu_custom_call" | custom-call | flops 2415919104 | bytes 6291456 | tf_op jit(solution)/shard_map/correlate/pallas_call | solution.py:256
  97.4 2.5 %collective-permute-done.21.refs_1_ = bf16[256,512]{1,0:T(8,128)(2,1)S(1)} collective-permute-done((bf16[256,512]{1,0:T(8,128)(2,1)S(1)}, bf16[256,512]{1,0:T(8,128)(2,1)S(1)}, u32[]{:S(2)}, u32[]{:S(2)}) %collective-permute-start.21) | collective-permute-done | bytes 262176 | tf_op jit(solution)/shard_map/ppermute | solution.py:42
  99.9 2.5 %collective-permute-done.22.refs_2_ = bf16[256,512]{1,0:T(8,128)(2,1)S(1)} collective-permute-done((bf16[256,512]{1,0:T(8,128)(2,1)S(1)}, bf16[256,512]{1,0:T(8,128)(2,1)S(1)}, u32[]{:S(2)}, u32[]{:S(2)}) %collective-permute-start.22) | collective-permute-done | bytes 262176 | tf_op jit(solution)/shard_map/ppermute | solution.py:42
  104.5 3.6 %correlate.8 = (f32[16,2048]{1,0:T(8,128)S(1)}, f32[16,128]{1,0:T(8,128)S(1)}) custom-call(s32[9]{0:T(128)S(1)} %pad_add_fusion.refs_0_, bf16[256,512]{1,0:T(8,128)(2,1)S(1)} %collective-permute-done.21.refs_1_, bf16[256,512]{1,0:T(8,128)(2,1)S(1)} %collective-permute-done.22.refs_2_, bf16[256,512]{1,0:T(8,128)(2,1)S(1)} %collective-permute-done.26.refs_3_, ...), custom_call_target="tpu_custom_call" | custom-call | flops 2415919104 | bytes 6291456 | tf_op jit(solution)/shard_map/correlate/pallas_call | solution.py:256
  108.5 2.5 %collective-permute-start.28 = (bf16[256,512]{1,0:T(8,128)(2,1)S(1)}, bf16[256,512]{1,0:T(8,128)(2,1)S(1)}, u32[]{:S(2)}, u32[]{:S(2)}) collective-permute-start(bf16[256,512]{1,0:T(8,128)(2,1)S(1)} %collective-permute-done.25.refs_1_), channel_id=1, source_target_pairs={{0,8},{8,0},{1,9},{9,1},{2,10},{10,2},{3,11},{11,3},{4,12},{12,4},... | collective-permute-start | bytes 786440 | tf_op jit(solution)/shard_map/ppermute | solution.py:34
  111.0 1.2 %collective-permute-done.28.refs_2_ = bf16[256,512]{1,0:T(8,128)(2,1)S(1)} collective-permute-done((bf16[256,512]{1,0:T(8,128)(2,1)S(1)}, bf16[256,512]{1,0:T(8,128)(2,1)S(1)}, u32[]{:S(2)}, u32[]{:S(2)}) %collective-permute-start.28) | collective-permute-done | bytes 262176 | tf_op jit(solution)/shard_map/ppermute | solution.py:34
  112.2 2.9 %correlate.9 = f32[2,8,2048]{2,1,0:T(8,128)} custom-call(s32[9]{0:T(128)S(1)} %pad_add_fusion.refs_0_, bf16[256,512]{1,0:T(8,128)(2,1)S(1)} %collective-permute-done.25.refs_1_, bf16[256,512]{1,0:T(8,128)(2,1)S(1)} %collective-permute-done.28.refs_2_, bf16[8,512,2304]{2,1,0:T(8,128)(2,1)S(1)} %get-tuple-element.100.refs_3_.refs_5_, ...), custom_call_target="tpu_custom_call" | custom-call | flops 1207959552 | bytes 3145728 | tf_op jit(solution)/shard_map/correlate/pallas_call | solution.py:256
  (63 shorter events, 11.0 us)
Async XLA Ops:
  1.9 10.6 %copy-start.2 = (s32[128]{0:T(128)S(1)}, s32[128]{0:T(128)}, u32[]{:S(2)}) copy-start(s32[128]{0:T(128)} %param.10) | copy-start | bytes 1540
  3.0 11.5 %collective-permute-start.1 = (bf16[32,64,256]{2,1,0:T(8,128)(2,1)}, bf16[32,64,256]{2,1,0:T(8,128)(2,1)}, u32[]{:S(2)}, u32[]{:S(2)}) collective-permute-start(bf16[32,64,256]{2,1,0:T(8,128)(2,1)} %dynamic-slice_bitcast_fusion.1), channel_id=1, source_target_pairs={{0,8},{8,0},{1,9},{9,1},{2,10},{10,2},{3,11},{11,3},{4,12},{12,4},... | collective-permute-start | bytes 3145736 | tf_op jit(solution)/shard_map/ppermute | solution.py:34
  6.3 7.0 %collective-permute-start = (bf16[128,512]{1,0:T(8,128)(2,1)S(1)}, bf16[128,512]{1,0:T(8,128)(2,1)S(1)}, u32[]{:S(2)}, u32[]{:S(2)}) collective-permute-start(bf16[128,512]{1,0:T(8,128)(2,1)S(1)} %slice.62), channel_id=1, source_target_pairs={{1,0},{8,1},{9,8},{16,9},{17,16},{24,17},{25,24},{32,25},{33,32},{... | collective-permute-start | bytes 393224 | tf_op jit(solution)/shard_map/ppermute | solution.py:288
  16.0 34.7 %all-to-all-start.1 = ((bf16[32,64,256]{2,1,0:T(8,128)(2,1)}), bf16[32,64,256]{2,1,0:T(8,128)(2,1)S(1)}, u32[]{:S(2)}, u32[]{:S(2)}) async-start(bf16[32,64,256]{2,1,0:T(8,128)(2,1)} %get-tuple-element.74), calls=%async_computation.1 | async-start | bytes 2097152 | tf_op jit(solution)/shard_map/all_to_all | solution.py:307
  26.0 8.3 %collective-permute-start.2 = (bf16[64,2304]{1,0:T(8,128)(2,1)S(1)}, bf16[64,2304]{1,0:T(8,128)(2,1)S(1)}, u32[]{:S(2)}, u32[]{:S(2)}) collective-permute-start(bf16[64,2304]{1,0:T(8,128)(2,1)S(1)} %get-tuple-element.78.refs_0_), channel_id=1, source_target_pairs={{0,2},{2,4},{4,6},{6,0},{1,3},{3,5},{5,7},{7,1},{8,10},{10,12},{12... | collective-permute-start | bytes 884744 | tf_op jit(solution)/shard_map/ppermute | solution.py:34
  27.4 6.9 %collective-permute-start.6 = (bf16[64,2304]{1,0:T(8,128)(2,1)S(1)}, bf16[64,2304]{1,0:T(8,128)(2,1)S(1)}, u32[]{:S(2)}, u32[]{:S(2)}) collective-permute-start(bf16[64,2304]{1,0:T(8,128)(2,1)S(1)} %get-tuple-element.88.refs_0_), channel_id=1, source_target_pairs={{0,6},{2,0},{4,2},{6,4},{1,7},{3,1},{5,3},{7,5},{8,14},{10,8},{12,... | collective-permute-start | bytes 884744 | tf_op jit(solution)/shard_map/ppermute | solution.py:34
  32.5 18.2 %collective-permute-start.4 = (bf16[64,2304]{1,0:T(8,128)(2,1)S(1)}, bf16[64,2304]{1,0:T(8,128)(2,1)S(1)}, u32[]{:S(2)}, u32[]{:S(2)}) collective-permute-start(bf16[64,2304]{1,0:T(8,128)(2,1)S(1)} %get-tuple-element.78.refs_0_), channel_id=1, source_target_pairs={{0,6},{2,0},{4,2},{6,4},{1,7},{3,1},{5,3},{7,5},{8,14},{10,8},{12,... | collective-permute-start | bytes 884744 | tf_op jit(solution)/shard_map/ppermute | solution.py:34
  33.9 16.8 %collective-permute-start.5 = (bf16[64,2304]{1,0:T(8,128)(2,1)S(1)}, bf16[64,2304]{1,0:T(8,128)(2,1)S(1)}, u32[]{:S(2)}, u32[]{:S(2)}) collective-permute-start(bf16[64,2304]{1,0:T(8,128)(2,1)S(1)} %get-tuple-element.88.refs_0_), channel_id=1, source_target_pairs={{0,2},{2,4},{4,6},{6,0},{1,3},{3,5},{5,7},{7,1},{8,10},{10,12},{12... | collective-permute-start | bytes 884744 | tf_op jit(solution)/shard_map/ppermute | solution.py:34
  34.3 16.4 %collective-permute-start.3 = (bf16[64,2304]{1,0:T(8,128)(2,1)S(1)}, bf16[64,2304]{1,0:T(8,128)(2,1)S(1)}, u32[]{:S(2)}, u32[]{:S(2)}) collective-permute-start(bf16[64,2304]{1,0:T(8,128)(2,1)S(1)} %collective-permute-done.2.refs_1_), channel_id=1, source_target_pairs={{0,2},{2,4},{4,6},{6,0},{1,3},{3,5},{5,7},{7,1},{8,10},{10,12},{12... | collective-permute-start | bytes 884744 | tf_op jit(solution)/shard_map/ppermute | solution.py:34
  34.3 16.4 %collective-permute-start.7 = (bf16[64,2304]{1,0:T(8,128)(2,1)S(1)}, bf16[64,2304]{1,0:T(8,128)(2,1)S(1)}, u32[]{:S(2)}, u32[]{:S(2)}) collective-permute-start(bf16[64,2304]{1,0:T(8,128)(2,1)S(1)} %collective-permute-done.6.refs_3_), channel_id=1, source_target_pairs={{0,6},{2,0},{4,2},{6,4},{1,7},{3,1},{5,3},{7,5},{8,14},{10,8},{12,... | collective-permute-start | bytes 884744 | tf_op jit(solution)/shard_map/ppermute | solution.py:34
  50.7 7.0 %collective-permute-start.10 = (bf16[2,16,256]{2,1,0:T(8,128)(2,1)S(1)}, bf16[2,16,256]{2,1,0:T(8,128)(2,1)S(1)}, u32[]{:S(2)}, u32[]{:S(2)}) collective-permute-start(bf16[2,16,256]{2,1,0:T(8,128)(2,1)S(1)} %get-tuple-element.131), channel_id=1, source_target_pairs={{0,6},{2,0},{4,2},{6,4},{1,7},{3,1},{5,3},{7,5},{8,14},{10,8},{12,... | collective-permute-start | bytes 49160 | tf_op jit(solution)/shard_map/ppermute | solution.py:34
  53.6 4.2 %collective-permute-start.8 = (bf16[2,16,256]{2,1,0:T(8,128)(2,1)S(1)}, bf16[2,16,256]{2,1,0:T(8,128)(2,1)S(1)}, u32[]{:S(2)}, u32[]{:S(2)}) collective-permute-start(bf16[2,16,256]{2,1,0:T(8,128)(2,1)S(1)} %get-tuple-element.133), channel_id=1, source_target_pairs={{0,2},{2,4},{4,6},{6,0},{1,3},{3,5},{5,7},{7,1},{8,10},{10,12},{12... | collective-permute-start | bytes 49160 | tf_op jit(solution)/shard_map/ppermute | solution.py:34
  53.6 4.2 %collective-permute-start.9 = (bf16[2,16,256]{2,1,0:T(8,128)(2,1)S(1)}, bf16[2,16,256]{2,1,0:T(8,128)(2,1)S(1)}, u32[]{:S(2)}, u32[]{:S(2)}) collective-permute-start(bf16[2,16,256]{2,1,0:T(8,128)(2,1)S(1)} %get-tuple-element.132), channel_id=1, source_target_pairs={{0,4},{2,6},{4,0},{6,2},{1,5},{3,7},{5,1},{7,3},{8,12},{10,14},{12... | collective-permute-start | bytes 49160 | tf_op jit(solution)/shard_map/ppermute | solution.py:34
  57.9 15.3 %copy-start.3 = (s32[8]{0:T(128)S(1)}, s32[8]{0:T(128)}, u32[]{:S(2)}) copy-start(s32[8]{0:T(128)} %constant.97) | copy-start | bytes 100
  58.0 5.8 %collective-permute-start.11 = (bf16[64,512]{1,0:T(8,128)(2,1)S(1)}, bf16[64,512]{1,0:T(8,128)(2,1)S(1)}, u32[]{:S(2)}, u32[]{:S(2)}) collective-permute-start(bf16[64,512]{1,0:T(8,128)(2,1)S(1)} %turn.1.refs_0_), channel_id=1, source_target_pairs={{0,16},{16,32},{32,48},{48,0},{1,17},{17,33},{33,49},{49,1},{2,18}... | collective-permute-start | bytes 196616 | tf_op jit(solution)/shard_map/ppermute | solution.py:34
  58.0 5.7 %collective-permute-start.12 = (bf16[64,512]{1,0:T(8,128)(2,1)S(1)}, bf16[64,512]{1,0:T(8,128)(2,1)S(1)}, u32[]{:S(2)}, u32[]{:S(2)}) collective-permute-start(bf16[64,512]{1,0:T(8,128)(2,1)S(1)} %turn.1.refs_0_), channel_id=1, source_target_pairs={{0,32},{16,48},{32,0},{48,16},{1,33},{17,49},{33,1},{49,17},{2,34}... | collective-permute-start | bytes 196616 | tf_op jit(solution)/shard_map/ppermute | solution.py:34
  59.9 3.9 %collective-permute-start.13 = (bf16[64,512]{1,0:T(8,128)(2,1)S(1)}, bf16[64,512]{1,0:T(8,128)(2,1)S(1)}, u32[]{:S(2)}, u32[]{:S(2)}) collective-permute-start(bf16[64,512]{1,0:T(8,128)(2,1)S(1)} %turn.1.refs_0_), channel_id=1, source_target_pairs={{0,48},{16,0},{32,16},{48,32},{1,49},{17,1},{33,17},{49,33},{2,50}... | collective-permute-start | bytes 196616 | tf_op jit(solution)/shard_map/ppermute | solution.py:34
  64.0 9.4 %collective-permute-start.16 = (bf16[256,512]{1,0:T(8,128)(2,1)S(1)}, bf16[256,512]{1,0:T(8,128)(2,1)S(1)}, u32[]{:S(2)}, u32[]{:S(2)}) collective-permute-start(bf16[256,512]{1,0:T(8,128)(2,1)S(1)} %join.1.refs_1_), channel_id=1, source_target_pairs={{0,8},{8,0},{1,9},{9,1},{2,10},{10,2},{3,11},{11,3},{4,12},{12,4},... | collective-permute-start | bytes 786440 | tf_op jit(solution)/shard_map/ppermute | solution.py:34
  71.8 6.0 %collective-permute-start.14 = (bf16[256,512]{1,0:T(8,128)(2,1)S(1)}, bf16[256,512]{1,0:T(8,128)(2,1)S(1)}, u32[]{:S(2)}, u32[]{:S(2)}) collective-permute-start(bf16[256,512]{1,0:T(8,128)(2,1)S(1)} %join.1.refs_1_), channel_id=1, source_target_pairs={{0,1},{8,201},{1,64},{9,8},{64,65},{72,9},{65,128},{73,72},{128,12... | collective-permute-start | bytes 786440 | tf_op jit(solution)/shard_map/ppermute | solution.py:42
  73.1 8.5 %collective-permute-start.15 = (bf16[256,512]{1,0:T(8,128)(2,1)S(1)}, bf16[256,512]{1,0:T(8,128)(2,1)S(1)}, u32[]{:S(2)}, u32[]{:S(2)}) collective-permute-start(bf16[256,512]{1,0:T(8,128)(2,1)S(1)} %join.1.refs_1_), channel_id=1, source_target_pairs={{0,193},{8,9},{1,0},{9,72},{64,1},{72,73},{65,64},{73,136},{128,65... | collective-permute-start | bytes 786440 | tf_op jit(solution)/shard_map/ppermute | solution.py:42
  81.6 2.0 %collective-permute-start.19 = (bf16[256,512]{1,0:T(8,128)(2,1)S(1)}, bf16[256,512]{1,0:T(8,128)(2,1)S(1)}, u32[]{:S(2)}, u32[]{:S(2)}) collective-permute-start(bf16[256,512]{1,0:T(8,128)(2,1)S(1)} %collective-permute-done.15.refs_2_), channel_id=1, source_target_pairs={{0,8},{8,0},{1,9},{9,1},{2,10},{10,2},{3,11},{11,3},{4,12},{12,4},... | collective-permute-start | bytes 786440 | tf_op jit(solution)/shard_map/ppermute | solution.py:34
  81.6 2.0 %collective-permute-start.20 = (bf16[256,512]{1,0:T(8,128)(2,1)S(1)}, bf16[256,512]{1,0:T(8,128)(2,1)S(1)}, u32[]{:S(2)}, u32[]{:S(2)}) collective-permute-start(bf16[256,512]{1,0:T(8,128)(2,1)S(1)} %collective-permute-done.14.refs_1_), channel_id=1, source_target_pairs={{0,8},{8,0},{1,9},{9,1},{2,10},{10,2},{3,11},{11,3},{4,12},{12,4},... | collective-permute-start | bytes 786440 | tf_op jit(solution)/shard_map/ppermute | solution.py:34
  82.1 7.2 %collective-permute-start.17 = (bf16[256,512]{1,0:T(8,128)(2,1)S(1)}, bf16[256,512]{1,0:T(8,128)(2,1)S(1)}, u32[]{:S(2)}, u32[]{:S(2)}) collective-permute-start(bf16[256,512]{1,0:T(8,128)(2,1)S(1)} %collective-permute-done.14.refs_1_), channel_id=1, source_target_pairs={{0,1},{8,201},{1,64},{9,8},{64,65},{72,9},{65,128},{73,72},{128,12... | collective-permute-start | bytes 786440 | tf_op jit(solution)/shard_map/ppermute | solution.py:42
  83.1 8.8 %collective-permute-start.18 = (bf16[256,512]{1,0:T(8,128)(2,1)S(1)}, bf16[256,512]{1,0:T(8,128)(2,1)S(1)}, u32[]{:S(2)}, u32[]{:S(2)}) collective-permute-start(bf16[256,512]{1,0:T(8,128)(2,1)S(1)} %collective-permute-done.15.refs_2_), channel_id=1, source_target_pairs={{0,193},{8,9},{1,0},{9,72},{64,1},{72,73},{65,64},{73,136},{128,65... | collective-permute-start | bytes 786440 | tf_op jit(solution)/shard_map/ppermute | solution.py:42
  91.8 2.0 %collective-permute-start.23 = (bf16[256,512]{1,0:T(8,128)(2,1)S(1)}, bf16[256,512]{1,0:T(8,128)(2,1)S(1)}, u32[]{:S(2)}, u32[]{:S(2)}) collective-permute-start(bf16[256,512]{1,0:T(8,128)(2,1)S(1)} %collective-permute-done.18.refs_2_), channel_id=1, source_target_pairs={{0,8},{8,0},{1,9},{9,1},{2,10},{10,2},{3,11},{11,3},{4,12},{12,4},... | collective-permute-start | bytes 786440 | tf_op jit(solution)/shard_map/ppermute | solution.py:34
  92.1 1.7 %collective-permute-start.24 = (bf16[256,512]{1,0:T(8,128)(2,1)S(1)}, bf16[256,512]{1,0:T(8,128)(2,1)S(1)}, u32[]{:S(2)}, u32[]{:S(2)}) collective-permute-start(bf16[256,512]{1,0:T(8,128)(2,1)S(1)} %collective-permute-done.17.refs_1_), channel_id=1, source_target_pairs={{0,8},{8,0},{1,9},{9,1},{2,10},{10,2},{3,11},{11,3},{4,12},{12,4},... | collective-permute-start | bytes 786440 | tf_op jit(solution)/shard_map/ppermute | solution.py:34
  92.3 7.6 %collective-permute-start.21 = (bf16[256,512]{1,0:T(8,128)(2,1)S(1)}, bf16[256,512]{1,0:T(8,128)(2,1)S(1)}, u32[]{:S(2)}, u32[]{:S(2)}) collective-permute-start(bf16[256,512]{1,0:T(8,128)(2,1)S(1)} %collective-permute-done.17.refs_1_), channel_id=1, source_target_pairs={{0,1},{8,201},{1,64},{9,8},{64,65},{72,9},{65,128},{73,72},{128,12... | collective-permute-start | bytes 786440 | tf_op jit(solution)/shard_map/ppermute | solution.py:42
  93.0 9.5 %collective-permute-start.22 = (bf16[256,512]{1,0:T(8,128)(2,1)S(1)}, bf16[256,512]{1,0:T(8,128)(2,1)S(1)}, u32[]{:S(2)}, u32[]{:S(2)}) collective-permute-start(bf16[256,512]{1,0:T(8,128)(2,1)S(1)} %collective-permute-done.18.refs_2_), channel_id=1, source_target_pairs={{0,193},{8,9},{1,0},{9,72},{64,1},{72,73},{65,64},{73,136},{128,65... | collective-permute-start | bytes 786440 | tf_op jit(solution)/shard_map/ppermute | solution.py:42
  102.5 1.6 %collective-permute-start.26 = (bf16[256,512]{1,0:T(8,128)(2,1)S(1)}, bf16[256,512]{1,0:T(8,128)(2,1)S(1)}, u32[]{:S(2)}, u32[]{:S(2)}) collective-permute-start(bf16[256,512]{1,0:T(8,128)(2,1)S(1)} %collective-permute-done.22.refs_2_), channel_id=1, source_target_pairs={{0,8},{8,0},{1,9},{9,1},{2,10},{10,2},{3,11},{11,3},{4,12},{12,4},... | collective-permute-start | bytes 786440 | tf_op jit(solution)/shard_map/ppermute | solution.py:34
  102.9 1.5 %collective-permute-start.27 = (bf16[256,512]{1,0:T(8,128)(2,1)S(1)}, bf16[256,512]{1,0:T(8,128)(2,1)S(1)}, u32[]{:S(2)}, u32[]{:S(2)}) collective-permute-start(bf16[256,512]{1,0:T(8,128)(2,1)S(1)} %collective-permute-done.21.refs_1_), channel_id=1, source_target_pairs={{0,8},{8,0},{1,9},{9,1},{2,10},{10,2},{3,11},{11,3},{4,12},{12,4},... | collective-permute-start | bytes 786440 | tf_op jit(solution)/shard_map/ppermute | solution.py:34
  103.0 5.5 %collective-permute-start.25 = (bf16[256,512]{1,0:T(8,128)(2,1)S(1)}, bf16[256,512]{1,0:T(8,128)(2,1)S(1)}, u32[]{:S(2)}, u32[]{:S(2)}) collective-permute-start(bf16[256,512]{1,0:T(8,128)(2,1)S(1)} %collective-permute-done.21.refs_1_), channel_id=1, source_target_pairs={{0,1},{8,201},{1,64},{9,8},{64,65},{72,9},{65,128},{73,72},{128,12... | collective-permute-start | bytes 786440 | tf_op jit(solution)/shard_map/ppermute | solution.py:42
  108.5 3.7 %collective-permute-start.28 = (bf16[256,512]{1,0:T(8,128)(2,1)S(1)}, bf16[256,512]{1,0:T(8,128)(2,1)S(1)}, u32[]{:S(2)}, u32[]{:S(2)}) collective-permute-start(bf16[256,512]{1,0:T(8,128)(2,1)S(1)} %collective-permute-done.25.refs_1_), channel_id=1, source_target_pairs={{0,8},{8,0},{1,9},{9,1},{2,10},{10,2},{3,11},{11,3},{4,12},{12,4},... | collective-permute-start | bytes 786440 | tf_op jit(solution)/shard_map/ppermute | solution.py:34
  (2 other events, 10.7 us)
